TPU v7x, 256 devices: a whole 4x4x8 slice. The times are simulated.
256 devices in a mesh: frame: 64 (over x, y_hi, z), tensor: 4 (over y_lo, core).
Axes of the slice: x: 4, y: 4 (y_hi: 2, y_lo: 2; y = y_hi * 2 + y_lo), z: 8, core: 2. Of those that a mesh axis runs over, the one named last changes fastest.
Arguments:
- queries: bfloat16 [24576, 2560], P('frame', 'tensor'), may hold values from -320 to 320, as said below
- keys: bfloat16 [24576, 2560], P('frame', 'tensor'), may hold values from -12 to 12
- values: bfloat16 [24576, 2560], P('frame', 'tensor'), may hold values from -6 to 6
- stream_in: bfloat16 [24576, 5120], P('frame', 'tensor'), may hold values from -120 to 120
- out_weight: bfloat16 [2560, 5120], P('tensor'), may hold values from -0.5 to 0.5
- time_weight: bfloat16 [3, 256, 5120], P(None, None, 'tensor'), may hold values from -0.375 to 0.375
- head_weight: bfloat16 [5120, 64], P('tensor'), may hold values from -0.078125 to 0.078125
- latent: float32 [24576, 64], P('frame'), may hold values from -6 to 6
- new_noise: float32 [384, 64], replicated, may hold values from -6 to 6
- levels: int32 [64], P('frame'), may hold values from 1 to 128, as said below
- timesteps: int32 [129], replicated, may hold values from 0 to 1000, as said below
Outputs:
- stream: bfloat16 [24576, 5120], P('frame', 'tensor')
- velocity: float32 [24576, 64], P('frame')
- queue_next: float32 [24576, 64], P('frame')
Inputs may be any that keep to these rules, and one draw needn't show every extreme that they name: `queries`: queries of the hidden draw may reach large magnitudes. `levels`: Non-decreasing along the queue; the first slot holds level 1 and the last slot level 128. `timesteps`: strictly rising; the first entry is 0 and the last is 1000.
All inputs are finite; a program needn't handle non-finite values.
Results may differ from a plain program's by a relative error of at most 0.013.
Values may be sent and summed in bfloat16 or wider, within the bound.
No kernel may reach another device: no remote copies, remote signals or barrier semaphores. Data moves between devices by JAX's collectives and lax.ppermute only.
A program may use at most 128 MiB of HBM per device.

v0:
```python
import math

import jax
import jax.numpy as jnp
from jax import lax
from jax.sharding import PartitionSpec as P

D = 5120
HD = 128
TFREQ = 256
PART_BITS = 3


def swapped(x, axis, stride):
    return lax.ppermute(x, axis, [(i, i ^ 1 << stride) for i in range(lax.axis_size(axis))])


def shifted(x, axis, by):
    length = lax.axis_size(axis)
    pairs = [(i, i + by) for i in range(length) if 0 <= i + by < length]
    return lax.ppermute(x, axis, pairs)


def sinusoid(time_values, freq_width):
    half_width = freq_width // 2
    frequencies = jnp.exp(
        -math.log(10000.0) * jnp.arange(half_width, dtype=jnp.float32) / half_width
    )
    angles = time_values[:, None] * frequencies[None, :]
    return jnp.concatenate([jnp.cos(angles), jnp.sin(angles)], axis=-1)


def lookup(table_values, positions):
    matches = jnp.arange(table_values.shape[0], dtype=jnp.int32)[None, :] == positions[:, None]
    return jnp.sum(jnp.where(matches, table_values[None, :], 0), axis=1).astype(jnp.float32)


def attend_block(running, queries, key_block, value_block, head_count):
    old_peak, denominator, accumulated = running
    row_count = queries.shape[0]
    query_heads = queries.reshape(row_count, head_count, HD)
    key_heads = key_block.reshape(key_block.shape[0], head_count, HD)
    value_heads = value_block.reshape(value_block.shape[0], head_count, HD)
    scores = jnp.einsum(
        "qhd,khd->hqk", query_heads, key_heads, preferred_element_type=jnp.float32
    ) * HD ** (-0.5)
    new_peak = jnp.maximum(old_peak, jnp.max(scores, axis=-1))
    shrink_factor = jnp.exp(old_peak - new_peak)
    exponentials = jnp.exp(scores - new_peak[..., None])
    denominator = denominator * shrink_factor + jnp.sum(exponentials, axis=-1)
    accumulated = accumulated * shrink_factor[..., None] + jnp.einsum(
        "hqk,khd->hqd",
        exponentials.astype(jnp.bfloat16),
        value_heads,
        preferred_element_type=jnp.float32,
    )
    return (new_peak, denominator, accumulated)


def local(
    queries,
    keys,
    values,
    stream_in,
    out_weight,
    time_weight,
    head_weight,
    latent,
    new_noise,
    levels,
    timesteps,
):
    row_count = queries.shape[0]
    head_count = queries.shape[1] // HD
    frame_index = lax.axis_index("frame")
    frame_count = lax.axis_size("frame")
    t_now = lookup(timesteps, levels)
    t_next = lookup(timesteps, levels - 1)
    embedding = sinusoid(t_now, TFREQ).astype(jnp.bfloat16)
    modulation = jnp.einsum(
        "fj,cjd->cfd", embedding, time_weight, preferred_element_type=jnp.float32
    )
    gate_mod = modulation[0]
    shift_mod = modulation[1]
    scale_mod = modulation[2]
    running = (
        jnp.full((head_count, row_count), -1e30, jnp.float32),
        jnp.zeros((head_count, row_count), jnp.float32),
        jnp.zeros((head_count, row_count, HD), jnp.float32),
    )
    kv_pair = jnp.stack([keys, values])
    kv_set = kv_pair[None]
    for bit_index in range(PART_BITS):
        partner_set = swapped(kv_set, "frame", bit_index)
        kv_set = jnp.concatenate([kv_set, partner_set], axis=0)

    def scan_step(loop_state, kv_block):
        return (attend_block(loop_state, queries, kv_block[0], kv_block[1], head_count), None)

    running, _ = lax.scan(scan_step, running, kv_set)
    accumulated = running[2] / running[1][..., None]
    attended = (
        accumulated.transpose(1, 0, 2).reshape(row_count, head_count * HD).astype(jnp.bfloat16)
    )
    partial_terms = jnp.dot(attended, out_weight, preferred_element_type=jnp.float32)
    mixed_sum = lax.psum_scatter(
        partial_terms.astype(jnp.bfloat16), "tensor", scatter_dimension=1, tiled=True
    ).astype(jnp.float32)
    hidden = stream_in.astype(jnp.float32) + gate_mod * mixed_sum
    stream = hidden.astype(jnp.bfloat16)
    head_float = head_weight.astype(jnp.float32)
    lift_factor = 1.0 + scale_mod
    local_sums = jnp.sum(hidden, axis=1)
    local_squares = jnp.sum(hidden * hidden, axis=1)
    row_sums, row_squares = lax.psum((local_sums, local_squares), "tensor")
    row_mean = row_sums / D
    row_var = row_squares / D - row_mean * row_mean
    inv_std = lax.rsqrt(row_var + 1e-06)
    normed = (hidden - row_mean[:, None]) * inv_std[:, None] * lift_factor + shift_mod
    velocity = lax.psum(
        jnp.dot(normed, head_float, precision=lax.Precision.HIGHEST).astype(jnp.bfloat16), "tensor"
    ).astype(jnp.float32)
    updated = latent + (t_next - t_now) / 1000.0 * velocity
    arrived = shifted(updated.astype(jnp.bfloat16), "frame", -1).astype(updated.dtype)
    queue_next = jnp.where(frame_index == frame_count - 1, new_noise, arrived)
    return (stream, velocity, queue_next)


def solution(mesh):
    return jax.shard_map(
        local,
        mesh=mesh,
        in_specs=(
            P("frame", "tensor"),
            P("frame", "tensor"),
            P("frame", "tensor"),
            P("frame", "tensor"),
            P("tensor", None),
            P(None, None, "tensor"),
            P("tensor", None),
            P("frame", None),
            P(),
            P("frame"),
            P(),
        ),
        out_specs=(P("frame", "tensor"), P("frame", None), P("frame", None)),
        check_vma=False,
    )
```

profile of v0, /device:TPU:6, one launch (start us, length us, event | category | flops | bytes accessed | tf_op | source)
XLA Modules:
  0.0 470.8 jit_solution(15301100377234890271)
XLA Ops:
  10.1 2.0 collective-permute-start
  12.1 21.8 %collective-permute-done = bf16[1,2,384,640]{2,3,1,0:T(8,128)(2,1)S(1)} collective-permute-done((bf16[1,2,384,640]{2,3,1,0:T(8,128)(2,1)S(1)}, bf16[1,2,384,640]{2,3,1,0:T(8,128)(2,1)S(1)}, u32[]{:S(2)}, u32[]{:S(2)}) %collective-permute-start) | collective-permute-done | bytes 983072 | tf_op jit(solution)/shard_map/ppermute | solution.py:15
  34.1 3.4 collective-permute-start.1
  37.4 84.3 %collective-permute-done.1 = bf16[2,2,384,640]{2,3,1,0:T(8,128)(2,1)S(1)} collective-permute-done((bf16[2,2,384,640]{2,3,1,0:T(8,128)(2,1)S(1)}, bf16[2,2,384,640]{2,3,1,0:T(8,128)(2,1)S(1)}, u32[]{:S(2)}, u32[]{:S(2)}) %collective-permute-start.1) | collective-permute-done | bytes 1966112 | tf_op jit(solution)/shard_map/ppermute | solution.py:15
  121.7 2.3 pad_maximum_fusion.1
  124.3 6.2 %collective-permute-start.2 = (bf16[4,2,384,640]{2,3,1,0:T(8,128)(2,1)}, bf16[4,2,384,640]{2,3,1,0:T(8,128)(2,1)}, u32[]{:S(2)}, u32[]{:S(2)}) collective-permute-start(bf16[4,2,384,640]{2,3,1,0:T(8,128)(2,1)} %pad_maximum_fusion.1), channel_id=1, source_target_pairs={{0,16},{4,20},{8,24},{12,28},{16,0},{20,4},{24,8},{28,12},{32,48},... | collective-permute-start | bytes 11796488 | tf_op jit(solution)/shard_map/ppermute | solution.py:15
  131.5 169.0 %collective-permute-done.2 = bf16[4,2,384,640]{2,3,1,0:T(8,128)(2,1)} collective-permute-done((bf16[4,2,384,640]{2,3,1,0:T(8,128)(2,1)}, bf16[4,2,384,640]{2,3,1,0:T(8,128)(2,1)}, u32[]{:S(2)}, u32[]{:S(2)}) %collective-permute-start.2) | collective-permute-done | bytes 3932192 | tf_op jit(solution)/shard_map/ppermute | solution.py:15
  300.6 6.8 %pad_maximum_fusion = bf16[8,2,384,640]{2,3,1,0:T(8,128)(2,1)} fusion(bf16[4,2,384,640]{2,3,1,0:T(8,128)(2,1)} %collective-permute-done.2, bf16[2,2,384,640]{2,3,1,0:T(8,128)(2,1)} %copy-done.4, bf16[1,2,384,640]{2,3,1,0:T(8,128)(2,1)} %copy-done.3, bf16[1,2,384,640]{2,3,1,0:T(8,128)(2,1)} %copy-done.2), kind=kLoop, calls=%fused_computation.17 | loop fusion | flops 11796480 | bytes 15728640 | tf_op jit(solution)/shard_map/concatenate | solution.py:95
  307.4 68.1 %while.15 = (s32[]{:T(128)}, f32[5,384]{1,0:T(8,128)S(1)}, f32[5,384]{1,0:T(8,128)S(1)}, f32[5,384,128]{2,1,0:T(8,128)S(1)}, bf16[8,2,384,640]{2,3,1,0:T(8,128)(...) while((s32[]{:T(128)}, f32[5,384]{1,0:T(8,128)S(1)}, f32[5,384]{1,0:T(8,128)S(1)}, ...), condition=%wide.region_4.5_spmd.clone, body=%wide.region_1.4_spmd.clone.sunk | while | flops 384132480 | bytes 26173592 | solution.py:100
  308.7 3.3 bitcast_reduce_fusion.2
  312.0 2.5 fusion.50
  317.2 3.3 bitcast_reduce_fusion.2
  320.5 2.5 fusion.50
  325.7 3.3 bitcast_reduce_fusion.2
  329.0 2.5 fusion.50
  334.2 3.3 bitcast_reduce_fusion.2
  337.5 2.5 fusion.50
  342.7 3.3 bitcast_reduce_fusion.2
  346.0 2.5 fusion.50
  351.2 3.3 bitcast_reduce_fusion.2
  354.6 2.5 fusion.50
  359.7 3.3 bitcast_reduce_fusion.2
  363.1 2.5 fusion.50
  368.3 3.3 bitcast_reduce_fusion.2
  371.6 2.5 fusion.50
  378.0 8.0 %convolution_convert_fusion = bf16[384,5120]{1,0:T(8,128)(2,1)} fusion(bf16[384,640]{0,1:T(8,128)(2,1)S(1)} %bitcast.57, bf16[640,5120]{1,0:T(8,128)(2,1)} %param.17), kind=kOutput, calls=%fused_computation.18 | convolution fusion | flops 2518548480 | bytes 10977280 | tf_op jit(solution)/shard_map/dot_general | solution.py:105
  389.2 41.7 %reduce-scatter.2.cloned.1.call-done = bf16[384,1280]{1,0:T(8,128)(2,1)} async-done(((bf16[384,5120]{1,0:T(8,128)(2,1)}), bf16[384,1280]{1,0:T(8,128)(2,1)}) %reduce-scatter.2.cloned.1.call-update) | async-done | bytes 983056 | tf_op jit(solution)/shard_map/reduce_scatter | solution.py:106
  431.0 2.6 fusion.17
  433.6 6.0 %all-reduce = (f32[384]{0:T(512)S(1)}, f32[384]{0:T(512)S(1)}) all-reduce(f32[384]{0:T(512)S(1)} %get-tuple-element.66, f32[384]{0:T(512)S(1)} %get-tuple-element.65), channel_id=1, replica_groups=mesh['frame'=64,'tensor'=4] {'tensor'}, use_global_device_ids=true, to_apply=%region_9.10 | all-reduce | flops 768 | bytes 6144 | tf_op jit(solution)/shard_map/psum | solution.py:115
  439.6 2.8 fusion.19
  442.4 10.5 %psum.23 = bf16[384,64]{0,1:T(8,128)(2,1)S(1)} all-reduce(bf16[384,64]{0,1:T(8,128)(2,1)S(1)} %fusion.19), channel_id=1, replica_groups=mesh['frame'=64,'tensor'=4] {'tensor'}, use_global_device_ids=true, to_apply=%region_10.11 | all-reduce | flops 24576 | bytes 98304 | tf_op jit(solution)/shard_map/psum | solution.py:120
  453.6 8.0 %collective-permute-start.3 = (bf16[384,64]{0,1:T(8,128)(2,1)S(1)}, bf16[384,64]{0,1:T(8,128)(2,1)S(1)}, u32[]{:S(2)}, u32[]{:S(2)}) collective-permute-start(bf16[384,64]{0,1:T(8,128)(2,1)S(1)} %get-tuple-element.88), channel_id=1, source_target_pairs={{4,0},{8,4},{12,8},{16,12},{20,16},{24,20},{28,24},{32,28},{36,32}... | collective-permute-start | bytes 147464 | tf_op jit(solution)/shard_map/ppermute | solution.py:21
  (99 shorter events, 32.6 us)
Async XLA Ops:
  7.2 381.0 %copy-start = (bf16[3,256,1280]{2,1,0:T(8,128)(2,1)S(1)}, bf16[3,256,1280]{2,1,0:T(8,128)(2,1)}, u32[]{:S(2)}) copy-start(bf16[3,256,1280]{2,1,0:T(8,128)(2,1)} %param.18) | copy-start | bytes 5898244
  7.2 423.8 %reduce-scatter.2.cloned.1.call-start = ((), (), s32[]{:S(2)}) async-start(), calls=%async_computation.1 | async-start | bytes 4915200 | tf_op jit(solution)/shard_map/reduce_scatter | solution.py:106
  10.1 114.0 %copy-start.2 = (bf16[1,2,384,640]{2,3,1,0:T(8,128)(2,1)}, bf16[1,2,384,640]{2,3,1,0:T(8,128)(2,1)S(1)}, u32[]{:S(2)}) copy-start(bf16[1,2,384,640]{2,3,1,0:T(8,128)(2,1)S(1)} %maximum_bitcast_fusion) | copy-start | bytes 2949124
  10.1 23.8 %collective-permute-start = (bf16[1,2,384,640]{2,3,1,0:T(8,128)(2,1)S(1)}, bf16[1,2,384,640]{2,3,1,0:T(8,128)(2,1)S(1)}, u32[]{:S(2)}, u32[]{:S(2)}) collective-permute-start(bf16[1,2,384,640]{2,3,1,0:T(8,128)(2,1)S(1)} %maximum_bitcast_fusion), channel_id=1, source_target_pairs={{0,4},{4,0},{8,12},{12,8},{16,20},{20,16},{24,28},{28,24},{32,36},... | collective-permute-start | bytes 2949128 | tf_op jit(solution)/shard_map/ppermute | solution.py:15
  33.8 90.2 %copy-start.3 = (bf16[1,2,384,640]{2,3,1,0:T(8,128)(2,1)}, bf16[1,2,384,640]{2,3,1,0:T(8,128)(2,1)S(1)}, u32[]{:S(2)}) copy-start(bf16[1,2,384,640]{2,3,1,0:T(8,128)(2,1)S(1)} %collective-permute-done) | copy-start | bytes 2949124
  34.1 96.4 %copy-start.6 = (bf16[384,640]{1,0:T(8,128)(2,1)S(1)}, bf16[384,640]{1,0:T(8,128)(2,1)}, u32[]{:S(2)}) copy-start(bf16[384,640]{1,0:T(8,128)(2,1)} %param.13) | copy-start | bytes 1474564
  34.1 87.6 %collective-permute-start.1 = (bf16[2,2,384,640]{2,3,1,0:T(8,128)(2,1)S(1)}, bf16[2,2,384,640]{2,3,1,0:T(8,128)(2,1)S(1)}, u32[]{:S(2)}, u32[]{:S(2)}) collective-permute-start(bf16[2,2,384,640]{2,3,1,0:T(8,128)(2,1)S(1)} %pad_maximum_fusion.2), channel_id=1, source_target_pairs={{0,8},{4,12},{8,0},{12,4},{16,24},{20,28},{24,16},{28,20},{32,40},... | collective-permute-start | bytes 5898248 | tf_op jit(solution)/shard_map/ppermute | solution.py:15
  121.7 2.6 copy-start.4
  124.3 176.2 %collective-permute-start.2 = (bf16[4,2,384,640]{2,3,1,0:T(8,128)(2,1)}, bf16[4,2,384,640]{2,3,1,0:T(8,128)(2,1)}, u32[]{:S(2)}, u32[]{:S(2)}) collective-permute-start(bf16[4,2,384,640]{2,3,1,0:T(8,128)(2,1)} %pad_maximum_fusion.1), channel_id=1, source_target_pairs={{0,16},{4,20},{8,24},{12,28},{16,0},{20,4},{24,8},{28,12},{32,48},... | collective-permute-start | bytes 11796488 | tf_op jit(solution)/shard_map/ppermute | solution.py:15
  312.0 2.7 copy-start.1
  320.5 2.7 copy-start.1
  329.0 2.7 copy-start.1
  337.5 2.7 copy-start.1
  346.0 2.7 copy-start.1
  354.5 2.7 copy-start.1
  363.1 2.7 copy-start.1
  371.6 2.7 copy-start.1
  386.1 0.8 copy-start.9
  386.1 44.9 %copy-start.5 = (bf16[384,1280]{1,0:T(8,128)(2,1)S(1)}, bf16[384,1280]{1,0:T(8,128)(2,1)}, u32[]{:S(2)}) copy-start(bf16[384,1280]{1,0:T(8,128)(2,1)} %param.16) | copy-start | bytes 2949124
  386.1 53.5 %copy-start.10 = (bf16[1280,64]{0,1:T(8,128)(2,1)S(1)}, bf16[1280,64]{0,1:T(8,128)(2,1)}, u32[]{:S(2)}) copy-start(bf16[1280,64]{0,1:T(8,128)(2,1)} %param.19) | copy-start | bytes 491524
  431.0 22.0 %copy-start.7 = (f32[384,64]{0,1:T(8,128)S(1)}, f32[384,64]{0,1:T(8,128)}, u32[]{:S(2)}) copy-start(f32[384,64]{0,1:T(8,128)} %param.20) | copy-start | bytes 294916
  433.6 29.8 %copy-start.8 = (f32[384,64]{0,1:T(8,128)S(1)}, f32[384,64]{0,1:T(8,128)}, u32[]{:S(2)}) copy-start(f32[384,64]{0,1:T(8,128)} %param.21) | copy-start | bytes 294916
  453.6 9.7 %collective-permute-start.3 = (bf16[384,64]{0,1:T(8,128)(2,1)S(1)}, bf16[384,64]{0,1:T(8,128)(2,1)S(1)}, u32[]{:S(2)}, u32[]{:S(2)}) collective-permute-start(bf16[384,64]{0,1:T(8,128)(2,1)S(1)} %get-tuple-element.88), channel_id=1, source_target_pairs={{4,0},{8,4},{12,8},{16,12},{20,16},{24,20},{28,24},{32,28},{36,32}... | collective-permute-start | bytes 147464 | tf_op jit(solution)/shard_map/ppermute | solution.py:21
Sparse Core Ops, SparseCore 0:
  386.2 44.7 reduce-scatter.1
where the time goes:
time: 472 us; the launch traced here: 471 us
  waiting for transfers between devices  319 us (68%)
  matrix products  47 us (10%)
  other arithmetic  35.4 us (8%)
  starting transfers between devices  19.5 us (4%)
  local copies, waits for them, and re-layouts  17.3 us (4%)
  blocking collectives  16.5 us (3%)
  between operations  16.1 us (3%)
    ppermute x3, waiting for transfers between devices, swapped(): lax.ppermute(x, axis, [(i, i ^ 1 << stride) for i in range(lax.axis_size(...  275 us
    reduce_scatter x1, waiting for transfers between devices, local(): lax.psum_scatter(partial_terms.astype(jnp.bfloat16), 'tensor', scatter_di...  41.7 us
    dot_general x8, matrix products, attend_block(): jnp.einsum('qhd,khd->hqk', query_heads, key_heads, preferred_element_type...  26.5 us
    reduce_sum x8, other arithmetic, attend_block(): denominator = denominator * shrink_factor + jnp.sum(exponentials, axis=-1)  19.9 us
    ppermute x3, starting transfers between devices, swapped(): lax.ppermute(x, axis, [(i, i ^ 1 << stride) for i in range(lax.axis_size(...  11.5 us
    psum x1, blocking collectives, local(): lax.psum(jnp.dot(normed, head_float, precision=lax.Precision.HIGHEST).ast...  10.5 us
    slice x8, local copies, waits for them, and re-layouts, scan_step(): kv_block[1]  10.3 us
  transfers between devices with their start and end apart: 5, of which 5 were waited for; matrix products, arithmetic and copies ran while one was open for 0% of the time, Pallas kernels for 0%

commit v1 on v0

v1 whole, which is shorter than its diff:
```python
import math

import jax
import jax.numpy as jnp
from jax import lax
from jax.experimental import pallas as pl
from jax.experimental.pallas import tpu as pltpu
from jax.sharding import PartitionSpec as P

D = 5120
HD = 128
TFREQ = 256
PART = 8
N_TENSOR = 4
F32 = jnp.float32
BF16 = jnp.bfloat16
COLUMN_BLOCK = 256
SPREAD_HEADS = 4
HALF_STRIDE = 16
SMALL = pl.CostEstimate(flops=1000, bytes_accessed=1000, transcendentals=0)
EXP_SCALE = HD ** (-0.5) / math.log(2.0)
VMEM_LIMIT = 16 * 1024 * 1024


def params():
    return pltpu.CompilerParams(vmem_limit_bytes=VMEM_LIMIT)


def spread(x, distance, backward=False):
    pairs = []
    for frame in range(lax.axis_size("frame")):
        for core in range(N_TENSOR):
            at = (frame - core) % PART
            step = distance if (at + distance) % 2 == 0 else -distance
            target = frame // PART * PART + (frame + step) % PART
            pairs.append((frame * N_TENSOR + core, target * N_TENSOR + core))
    if backward:
        pairs = [(b, a) for a, b in pairs]
    return lax.ppermute(x, ("frame", "tensor"), pairs)


def swap_pair(x):
    pairs = []
    for frame in range(lax.axis_size("frame")):
        for core in range(N_TENSOR):
            at = (frame - core) % PART
            target = frame // PART * PART + ((at ^ 1) + core) % PART
            pairs.append((frame * N_TENSOR + core, target * N_TENSOR + core))
    return lax.ppermute(x, ("frame", "tensor"), pairs)


def swap_half(x):
    return lax.ppermute(x, "frame", [(i, i ^ HALF_STRIDE) for i in range(lax.axis_size("frame"))])


def peer(x, mask):
    return lax.ppermute(x, "tensor", [(i, i ^ mask) for i in range(N_TENSOR)])


def shifted(x, axis, by):
    length = lax.axis_size(axis)
    pairs = [(i, i + by) for i in range(length) if 0 <= i + by < length]
    return lax.ppermute(x, axis, pairs)


def sinusoid(time_values, freq_width):
    half_width = freq_width // 2
    frequencies = jnp.exp(
        -math.log(10000.0) * jnp.arange(half_width, dtype=jnp.float32) / half_width
    )
    angles = time_values[:, None] * frequencies[None, :]
    return jnp.concatenate([jnp.cos(angles), jnp.sin(angles)], axis=-1)


def lookup(table_values, positions):
    matches = jnp.arange(table_values.shape[0], dtype=jnp.int32)[None, :] == positions[:, None]
    return jnp.sum(jnp.where(matches, table_values[None, :], 0), axis=1).astype(jnp.float32)


def dot(a, b):
    return jnp.dot(a, b, preferred_element_type=F32)


def dot_t(a, b):
    return lax.dot_general(a, b, (((1,), (1,)), ((), ())), preferred_element_type=F32)


def split3(x):
    hi = x.astype(BF16)
    rest = x - hi.astype(F32)
    mid = rest.astype(BF16)
    return hi, mid, (rest - mid.astype(F32)).astype(BF16)


def pack_kernel(head_ref, q_ref, k_ref, v_ref, x1_ref, x2_ref, x3_ref, kv_ref, q_out_ref, sem):
    common = pl.ds(SPREAD_HEADS * HD, HD)

    def lanes(at):
        return pl.ds(pl.multiple_of(head_ref[at] * HD, HD), HD)

    copies = []

    def move(source, source_lanes, target, slot):
        copy = pltpu.make_async_copy(
            source.at[:, source_lanes], target.at[:, pl.ds(slot * HD, HD)], sem.at[len(copies)]
        )
        copy.start()
        copies.append(copy)

    for at, ref in ((3, x3_ref), (2, x2_ref), (1, x1_ref), (0, kv_ref)):
        move(k_ref, lanes(at), ref, 0)
        move(v_ref, lanes(at), ref, 1)
        move(k_ref, common, ref, 2)
        move(v_ref, common, ref, 3)
        if at:
            move(q_ref, lanes(at), ref, 4)
    move(q_ref, lanes(0), q_out_ref, 0)
    move(q_ref, common, q_out_ref, 1)
    for copy in copies:
        copy.wait()


def attend_kernel(query_lanes, own_query, block_count, state_low, first, last, *refs):
    refs = list(refs)
    q_refs = [refs.pop(0) for _ in query_lanes]
    blocks = [refs.pop(0) for _ in range(block_count)]
    if not first:
        acc_in, peak_in, total_in = refs.pop(0), refs.pop(0), refs.pop(0)
    row_count = q_refs[0].shape[0]
    for at, (q_ref, (q_low, shared)) in enumerate(zip(q_refs, query_lanes)):
        key_low = 2 * HD if shared else 0
        query = q_ref[:, q_low : q_low + HD]
        scores = [dot_t(query, ref[:, key_low : key_low + HD]) for ref in blocks]
        peak = max_of([jnp.max(s, axis=1, keepdims=True) for s in scores])
        rows = slice((state_low + at) * row_count, (state_low + at + 1) * row_count)
        if not first:
            old_peak = peak_in[rows, 0:1]
            peak = jnp.maximum(peak, old_peak)
        acc = None
        total = None
        for s, ref in zip(scores, blocks):
            weights = jnp.exp2((s - peak) * EXP_SCALE)
            part = sum_lanes(weights)
            total = part if total is None else total + part
            mixed = dot(weights.astype(BF16), ref[:, key_low + HD : key_low + 2 * HD])
            acc = mixed if acc is None else acc + mixed
        if not first:
            shrink = jnp.exp2((old_peak - peak) * EXP_SCALE)
            acc = acc + acc_in[rows, :] * shrink
            total = total + total_in[rows, :] * shrink
        if last:
            out = (acc / jnp.sum(total, axis=1, keepdims=True)).astype(BF16)
            if own_query:
                refs[0][:, at * HD : (at + 1) * HD] = out
            else:
                refs[at][...] = out
        else:
            refs[0][rows, :] = acc
            refs[1][rows, :] = jnp.broadcast_to(peak, acc.shape)
            refs[2][rows, :] = total


def max_of(values):
    result = values[0]
    for value in values[1:]:
        result = jnp.maximum(result, value)
    return result


def sum_lanes(x):
    result = x[:, :HD]
    for low in range(HD, x.shape[1], HD):
        result = result + x[:, low : low + HD]
    return result


def attend(queries, query_lanes, blocks, state, state_low, last, own_query):
    row_count = queries[0].shape[0]
    operands = list(queries) + list(blocks)
    first = state is None
    if not first:
        operands += list(state)
    if not last:
        out_shape = [jax.ShapeDtypeStruct((row_count * len(queries), HD), F32)] * 3
    elif own_query:
        out_shape = jax.ShapeDtypeStruct((row_count, HD * len(queries)), BF16)
    else:
        out_shape = [jax.ShapeDtypeStruct((row_count, HD), BF16)] * len(queries)

    def body(*refs):
        attend_kernel(query_lanes, own_query, len(blocks), state_low, first, last, *refs)

    return pl.pallas_call(body, out_shape=out_shape, compiler_params=params(), cost_estimate=SMALL)(*operands)


def modulate_kernel(embedding_ref, time_ref, head_ref, gate_ref, lifted_ref, extra_ref):
    width = gate_ref.shape[1]
    channels = head_ref.shape[0]
    embedding = jnp.broadcast_to(embedding_ref[...], (16, TFREQ))
    gate_ref[...] = dot(embedding, time_ref[0])[:8]
    shift = dot(embedding, time_ref[1])[:1]
    lift = 1.0 + dot(embedding, time_ref[2])[:1]
    head = head_ref[...].astype(F32)
    lifted = head * lift
    high = lifted.astype(BF16)
    low = (lifted - high.astype(F32)).astype(BF16)
    lifted_ref[0:channels] = high
    lifted_ref[channels:] = low
    lift_head = jnp.sum(high.astype(F32) + low.astype(F32), axis=1, keepdims=True)
    shift_head = jnp.sum(head * shift, axis=1, keepdims=True)
    extra_ref[...] = place(split3(lift_head) + split3(shift_head), extra_ref.shape).astype(BF16)


def place(pieces, shape):
    lane = lax.broadcasted_iota(jnp.int32, shape, 1)
    result = jnp.zeros(shape, F32)
    for at, piece in enumerate(pieces):
        result = jnp.where(lane == at, piece.astype(F32), result)
    return result


def head_rows(head_ref, w_ref, rows, lanes):
    parts = []
    for row in rows:
        if row is None:
            parts.append(w_ref[SPREAD_HEADS * HD : (SPREAD_HEADS + 1) * HD, lanes])
        else:
            parts.append(w_ref[pl.ds(pl.multiple_of(head_ref[row] * HD, HD), HD), lanes])
    return jnp.concatenate(parts, axis=0)


def column_blocks(width):
    return [(low, min(COLUMN_BLOCK, width - low)) for low in range(0, width, COLUMN_BLOCK)]


def project_kernel(halves, row_sets, with_base, head_ref, *refs):
    count = len(row_sets)
    out_ref = refs[-1]
    width = out_ref.shape[1]
    inputs, weights = refs[:count], refs[count : (1 + halves) * count]
    base_ref = refs[(1 + halves) * count] if with_base else None
    for half in range(halves):
        offset = 0
        if halves > 1:
            offset = pl.multiple_of((head_ref[8] ^ half) * (width // halves), HD)
        for low, size in column_blocks(width // halves):
            out_lanes = pl.ds(offset + low, size)
            acc = base_ref[:, out_lanes] if with_base else None
            for at, (a_ref, rows) in enumerate(zip(inputs, row_sets)):
                w_ref = weights[at * halves + half]
                part = dot(a_ref[...], head_rows(head_ref, w_ref, rows, pl.ds(low, size)))
                acc = part if acc is None else acc + part
            out_ref[:, out_lanes] = acc


def project(heads, inputs, weights, row_sets, base=None):
    row_count = inputs[0].shape[0]
    halves = len(weights) // len(inputs)
    width = weights[0].shape[1] * halves
    operands = [heads, *inputs, *weights] + ([] if base is None else [base])

    def body(*refs):
        project_kernel(halves, row_sets, base is not None, *refs)

    return pl.pallas_call(
        body,
        in_specs=[pl.BlockSpec(memory_space=pltpu.SMEM)]
        + [pl.BlockSpec(memory_space=pltpu.VMEM)] * (len(operands) - 1),
        out_shape=jax.ShapeDtypeStruct((row_count, width), F32),
        compiler_params=params(),
        cost_estimate=SMALL,
    )(*operands)


def hidden_kernel(
    row_sets,
    head_ref,
    a0,
    a1,
    w0_mine,
    w0_other,
    w1_mine,
    w1_other,
    acc_ref,
    in_ref,
    gate_ref,
    lifted_ref,
    extra_ref,
    stream_ref,
    message_ref,
):
    row_count, width = stream_ref.shape
    channels = extra_ref.shape[0]
    total = None
    squares = None
    share = None
    rest = None
    for half, low, size in [(h, *block) for h in range(2) for block in column_blocks(width // 2)]:
        lanes = pl.ds(pl.multiple_of((head_ref[8] ^ half) * (width // 2), HD) + low, size)
        mixed = acc_ref[:, lanes]
        for a_ref, w_ref, rows in zip((a0, a1), ((w0_mine, w0_other)[half], (w1_mine, w1_other)[half]), row_sets):
            mixed = mixed + dot(a_ref[...], head_rows(head_ref, w_ref, rows, pl.ds(low, size)))
        hidden = in_ref[:, lanes].astype(F32) + gate_ref[0:1, lanes] * mixed
        high = hidden.astype(BF16)
        stream_ref[:, lanes] = high
        small = (hidden - high.astype(F32)).astype(BF16)
        parts = (
            sum_lanes(hidden),
            sum_lanes(hidden * hidden),
            dot_t(lifted_ref[:, lanes], high),
            dot_t(lifted_ref[0:channels, lanes], small),
        )
        if total is None:
            total, squares, share, rest = parts
        else:
            total, squares = total + parts[0], squares + parts[1]
            share, rest = share + parts[2], rest + parts[3]
    mean = jnp.sum(total, axis=1, keepdims=True) * (1.0 / width)
    spread = jnp.sum(squares, axis=1, keepdims=True) - mean * mean * width
    stats = jnp.transpose(place((mean, spread), (row_count, HD)))
    mean_row, spread_row = stats[0:1], stats[1:2]
    extra = extra_ref[...].astype(F32)
    lift_head = extra[:, 0:1] + extra[:, 1:2] + extra[:, 2:3]
    share = share[0:channels] + share[channels:] + rest - lift_head * mean_row
    rows = [x.astype(F32) for x in split3(mean_row) + split3(spread_row)]
    rows = jnp.concatenate(rows + [jnp.zeros((10, row_count), F32)], axis=0)
    message_ref[0:channels, 0:row_count] = share.astype(BF16)
    message_ref[channels:, 0:row_count] = rows.astype(BF16)
    message_ref[0:channels, row_count:] = extra_ref[...]
    message_ref[channels:, row_count:] = jnp.zeros((16, HD), BF16)


def finish_kernel(m0, m1, m2, m3, latent_ref, step_ref, velocity_ref, updated_ref):
    channels, row_count = velocity_ref.shape
    refs = (m0, m1, m2, m3)

    def tree(values):
        return (values[0] + values[1]) + (values[2] + values[3])

    shares = [ref[0:channels, 0:row_count].astype(F32) for ref in refs]
    stats = [ref[channels:, 0:row_count].astype(F32) for ref in refs]
    extras = [ref[0:channels, row_count:].astype(F32) for ref in refs]
    means = [x[0:1] + x[1:2] + x[2:3] for x in stats]
    spreads = [x[3:4] + x[4:5] + x[5:6] for x in stats]
    lifts = [x[:, 0:1] + x[:, 1:2] + x[:, 2:3] for x in extras]
    shifts = [x[:, 3:4] + x[:, 4:5] + x[:, 5:6] for x in extras]
    mean = tree(means) * (1.0 / N_TENSOR)
    offsets = [x - mean for x in means]
    variance = tree(spreads) * (1.0 / D) + tree([x * x for x in offsets]) * (1.0 / N_TENSOR)
    inv_std = lax.rsqrt(variance + 1e-06)
    total = tree([s + o * b for s, o, b in zip(shares, offsets, lifts)])
    velocity = total * inv_std + tree(shifts)
    velocity_ref[...] = velocity
    updated_ref[...] = (latent_ref[...] + step_ref[0, 0] * velocity).astype(BF16)


def local(
    queries,
    keys,
    values,
    stream_in,
    out_weight,
    time_weight,
    head_weight,
    latent,
    new_noise,
    levels,
    timesteps,
):
    row_count, width = stream_in.shape
    channels = latent.shape[1]
    frame_index = lax.axis_index("frame")
    frame_count = lax.axis_size("frame")
    tensor_index = lax.axis_index("tensor")
    barrier = lax.optimization_barrier

    def columns(mask, low=0, size=width):
        start = (tensor_index ^ mask) * width + low
        return lax.dynamic_slice(out_weight, (0, start), (out_weight.shape[0], size))

    core_index = tensor_index % 2

    def heads_of(core):
        place_in_ring = (frame_index - core) % PART
        pair, member = place_in_ring // 2, place_in_ring % 2
        ahead, behind = (pair + 1) % SPREAD_HEADS, (pair + SPREAD_HEADS - 1) % SPREAD_HEADS
        return [
            pair,
            jnp.where(member == 1, ahead, behind),
            jnp.where(member == 1, behind, ahead),
            (pair + 2) % SPREAD_HEADS,
        ]

    half_index = frame_index // HALF_STRIDE % 2
    heads = jnp.stack(heads_of(core_index) + heads_of(1 - core_index) + [half_index]).astype(jnp.int32)
    kv_width, packed_width = 4 * HD, 5 * HD
    x1, x2, x3, own_kv, own_q = pl.pallas_call(
        pack_kernel,
        in_specs=[pl.BlockSpec(memory_space=pltpu.SMEM)] + [pl.BlockSpec(memory_space=pl.ANY)] * 3,
        out_specs=[pl.BlockSpec(memory_space=pl.ANY)] * 5,
        scratch_shapes=[pltpu.SemaphoreType.DMA((21,))],
        out_shape=[jax.ShapeDtypeStruct((row_count, packed_width), BF16)] * 3
        + [jax.ShapeDtypeStruct((row_count, kv_width), BF16), jax.ShapeDtypeStruct((row_count, 2 * HD), BF16)],
        compiler_params=params(),
        cost_estimate=SMALL,
    )(heads, queries, keys, values)
    x3 = spread(x3, 3)
    x2 = spread(x2, 2)
    x1 = spread(x1, 1)
    half_width = width // 2
    across = [peer(columns(mask, half_index * half_width, half_width), mask) for mask in (2, 3)]
    x3, across = barrier((x3, across))
    across_other = [swap_half(w) for w in across]
    partner = [swap_pair(own_kv)] + [swap_pair(x[:, :kv_width]) for x in (x1, x2, x3)]
    queries_in = (x1, x2, x3, own_q, own_q)
    query_lanes = ((kv_width, False),) * 3 + ((0, False), (HD, True))
    state = attend(
        queries_in, query_lanes, (own_kv, x1, x2, x3, *partner[:2]), None, 0, False, False
    )
    results = attend(queries_in[:3], query_lanes[:3], partner[2:], state, 0, True, False)
    mine = attend(queries_in[3:], query_lanes[3:], partner[2:], state, 3, True, True)
    results, across_other[0] = barrier((results, across_other[0]))
    back = [spread(x, i + 1, True) for i, x in enumerate(results)]
    back = jnp.concatenate(back, axis=1)

    weights = [columns(0), peer(columns(1), 1)]
    far_weights = [across[0], across_other[0], across[1], across_other[1]]

    t_now = lookup(timesteps, levels)
    t_next = lookup(timesteps, levels - 1)
    embedding = sinusoid(t_now, TFREQ).astype(BF16)
    step = ((t_next - t_now) / 1000.0).reshape(1, 1)
    head = head_weight.T
    gate, lifted, extra = pl.pallas_call(
        modulate_kernel,
        out_shape=[
            jax.ShapeDtypeStruct((8, width), F32),
            jax.ShapeDtypeStruct((2 * channels, width), BF16),
            jax.ShapeDtypeStruct((channels, HD), BF16),
        ],
        compiler_params=params(),
        cost_estimate=SMALL,
    )(embedding, time_weight, head)

    mine_all = [mine] + [peer(mine, mask) for mask in (1, 2, 3)]
    back_beside, back_across = peer(back, 1), peer(back, 2)
    back_last = peer(back_across, 1)
    mine_rows, back_rows = ((0, None), (4, None)), ((1, 2, 3), (5, 6, 7))
    acc = project(heads, mine_all[:2], weights, mine_rows)
    acc = project(heads, mine_all[2:], far_weights, mine_rows, acc)
    acc = project(heads, [back, back_beside], weights, back_rows, acc)

    def finish_hidden(*refs):
        hidden_kernel(back_rows, *refs)

    stream, message = pl.pallas_call(
        finish_hidden,
        in_specs=[pl.BlockSpec(memory_space=pltpu.SMEM)] + [pl.BlockSpec(memory_space=pltpu.VMEM)] * 11,
        out_shape=[
            jax.ShapeDtypeStruct((row_count, width), BF16),
            jax.ShapeDtypeStruct((channels + 16, row_count + HD), BF16),
        ],
        compiler_params=params(),
        cost_estimate=SMALL,
    )(heads, back_across, back_last, *far_weights, acc, stream_in, gate, lifted, extra)
    messages = [message] + [peer(message, mask) for mask in (1, 2, 3)]
    velocity, updated = pl.pallas_call(
        finish_kernel,
        in_specs=[pl.BlockSpec(memory_space=pltpu.VMEM)] * 5 + [pl.BlockSpec(memory_space=pltpu.SMEM)],
        out_shape=[
            jax.ShapeDtypeStruct((channels, row_count), F32),
            jax.ShapeDtypeStruct((channels, row_count), BF16),
        ],
        compiler_params=params(),
        cost_estimate=SMALL,
    )(*messages, latent.T, step)
    arrived = shifted(updated, "frame", -1).astype(F32)
    queue_next = jnp.where(frame_index == frame_count - 1, new_noise.T, arrived)
    return (stream, velocity.T, queue_next.T)


def solution(mesh):
    return jax.shard_map(
        local,
        mesh=mesh,
        in_specs=(
            P("frame", "tensor"),
            P("frame", "tensor"),
            P("frame", "tensor"),
            P("frame", "tensor"),
            P("tensor", None),
            P(None, None, "tensor"),
            P("tensor", None),
            P("frame", None),
            P(),
            P("frame"),
            P(),
        ),
        out_specs=(P("frame", "tensor"), P("frame", None), P("frame", None)),
        check_vma=False,
    )
```

time: 472 us -> 134 us (0.28)
  waiting for transfers between devices: 319 us -> 53 us
  matrix products: 47 us -> 0 us
  other arithmetic: 35.4 us -> 1.42 us
  Pallas kernels: 0 us -> 25.8 us
  starting transfers between devices: 19.5 us -> 40.5 us
  blocking collectives: 16.5 us -> 0 us
  between operations: 16.1 us -> 2.97 us
  local copies, waits for them, and re-layouts: 17.3 us -> 9.63 us
    ppermute x3 -> x24, waiting for transfers between devices: 275 us -> 51.3 us  [the longest x6 32.6 us: spread(): return lax.ppermute(x, ('frame', 'tensor'), pairs)]
    dot_general x19 -> x0, matrix products: 47 us -> none  [the longest x8 26.5 us: attend_block(): jnp.einsum('qhd,khd->hqk', query_heads, key_heads, preferred_element_type...]
    reduce_scatter x1 -> x0, waiting for transfers between devices: 41.7 us -> none  [local(): lax.psum_scatter(partial_terms.astype(jnp.bfloat16), 'tensor', scatter_di...]
    pallas_call x0 -> x10, Pallas kernels: none -> 25.8 us  [the longest x3 9.9 us: attend(): pl.pallas_call(body, out_shape=out_shape, compiler_params=params(), cost_...]
    reduce_sum x9 -> x0, other arithmetic: 22.4 us -> none  [the longest x8 19.9 us: attend_block(): denominator = denominator * shrink_factor + jnp.sum(exponentials, axis=-1)]
    ppermute x3 -> x24, starting transfers between devices: 11.5 us -> 33.4 us  [the longest x6 17.4 us: spread(): return lax.ppermute(x, ('frame', 'tensor'), pairs)]
    psum x2 -> x0, blocking collectives: 16.5 us -> none  [the longest x1 10.5 us: local(): lax.psum(jnp.dot(normed, head_float, precision=lax.Precision.HIGHEST).ast...]
    slice x8 -> x3, local copies, waits for them, and re-layouts: 10.3 us -> 0.08 us  [local(): x[:, :kv_width]]
  transfers between devices with their start and end apart: 5 -> 25, of which waited for: 5 -> 11; matrix products, arithmetic and copies ran while one was open for 0% -> 3% of each run, Pallas kernels for 0% -> 15%
where the time goes in v1:
time: 134 us; the launch traced here: 133 us
  waiting for transfers between devices  53 us (40%)
  starting transfers between devices  40.5 us (30%)
  Pallas kernels  25.8 us (19%)
  local copies, waits for them, and re-layouts  9.63 us (7%)
  between operations  2.97 us (2%)
  other arithmetic  1.42 us (1%)
    ppermute x6, waiting for transfers between devices, spread(): return lax.ppermute(x, ('frame', 'tensor'), pairs)  32.6 us
    ppermute x6, starting transfers between devices, spread(): return lax.ppermute(x, ('frame', 'tensor'), pairs)  17.4 us
    ppermute x12, waiting for transfers between devices, peer(): return lax.ppermute(x, 'tensor', [(i, i ^ mask) for i in range(N_TENSOR)])  10.3 us
    pallas_call x3, Pallas kernels, attend(): pl.pallas_call(body, out_shape=out_shape, compiler_params=params(), cost_...  9.9 us
    ppermute x4, waiting for transfers between devices, swap_pair(): return lax.ppermute(x, ('frame', 'tensor'), pairs)  8.29 us
    ppermute x12, starting transfers between devices, peer(): return lax.ppermute(x, 'tensor', [(i, i ^ mask) for i in range(N_TENSOR)])  8.26 us
    pallas_call x3, Pallas kernels, project(): pl.pallas_call(body, in_specs=[pl.BlockSpec(memory_space=pltpu.SMEM)] + [...  7.32 us
    ppermute x1, starting transfers between devices, shifted(): return lax.ppermute(x, axis, pairs)  7.05 us
  transfers between devices with their start and end apart: 25, of which 11 were waited for; matrix products, arithmetic and copies ran while one was open for 3% of the time, Pallas kernels for 15%

profile of v1, /device:TPU:6, one launch (start us, length us, event | category | flops | bytes accessed | tf_op | source)
XLA Modules:
  0.0 133.2 jit_solution(1480280349908406972)
XLA Ops:
  0.7 2.8 %constant_dynamic-slice_fusion.2 = (bf16[640,640]{1,0:T(8,128)(2,1)}, bf16[640,640]{1,0:T(8,128)(2,1)}) fusion(bf16[640,5120]{1,0:T(8,128)(2,1)} %param.15, s32[]{:T(128)S(6)} %select_n.122, s32[]{:T(128)S(6)} %select_n.121), kind=kLoop, calls=%fused_computation.12 | loop fusion | bytes 3276808 | tf_op jit(solution)/shard_map/dynamic_slice | solution.py:379
  5.2 1.9 %shard_map.130 = (bf16[384,640]{1,0:T(8,128)(2,1)}, bf16[384,640]{1,0:T(8,128)(2,1)}, bf16[384,640]{1,0:T(8,128)(2,1)}, bf16[384,512]{1,0:T(8,128)(2,1)S(1)}, bf16[384,256]{1,0:T(8,128)(2,1)S(1)}) custom-call(s32[9]{0:T(128)S(1)} %stack.39.head_ref.refs_0_, bf16[384,640]{1,0:T(8,128)(2,1)S(1)} %copy-done.4, bf16[384,640]{1,0:T(8,128)(2,1)S(1)} %copy-done.5, ...), custom_call_target="tpu_custom_call" | custom-call | flops 1000 | bytes 1000 | tf_op jit(solution)/shard_map/pallas_call | solution.py:397
  7.9 6.7 %collective-permute-start.2 = (bf16[384,640]{1,0:T(8,128)(2,1)}, bf16[384,640]{1,0:T(8,128)(2,1)S(1)}, u32[]{:S(2)}, u32[]{:S(2)}) collective-permute-start(bf16[384,640]{1,0:T(8,128)(2,1)} %get-tuple-element.30), channel_id=1, source_target_pairs={{0,20},{1,13},{2,22},{3,15},{4,16},{5,25},{6,18},{7,27},{8,28},{9,... | collective-permute-start | bytes 1474568 | tf_op jit(solution)/shard_map/ppermute | solution.py:39
  14.7 2.5 %collective-permute-start.1 = (bf16[384,640]{1,0:T(8,128)(2,1)}, bf16[384,640]{1,0:T(8,128)(2,1)S(1)}, u32[]{:S(2)}, u32[]{:S(2)}) collective-permute-start(bf16[384,640]{1,0:T(8,128)(2,1)} %get-tuple-element.29), channel_id=1, source_target_pairs={{0,8},{1,25},{2,10},{3,27},{4,28},{5,13},{6,30},{7,15},{8,16},{9,1... | collective-permute-start | bytes 1474568 | tf_op jit(solution)/shard_map/ppermute | solution.py:39
  17.1 25.0 %collective-permute-done.2.refs_2_.refs_8_ = bf16[384,640]{1,0:T(8,128)(2,1)S(1)} collective-permute-done((bf16[384,640]{1,0:T(8,128)(2,1)}, bf16[384,640]{1,0:T(8,128)(2,1)S(1)}, u32[]{:S(2)}, u32[]{:S(2)}) %collective-permute-start.2) | collective-permute-done | bytes 491552 | tf_op jit(solution)/shard_map/ppermute | solution.py:39
  43.0 3.3 %constant_dynamic-slice_fusion = (bf16[640,1280]{1,0:T(8,128)(2,1)}, bf16[640,1280]{1,0:T(8,128)(2,1)S(1)}) fusion(bf16[640,5120]{1,0:T(8,128)(2,1)} %param.15, s32[]{:T(128)S(6)} %select_n.124, s32[]{:T(128)S(6)} %select_n.123), kind=kLoop, calls=%fused_computation.10 | loop fusion | bytes 6553608 | tf_op jit(solution)/shard_map/dynamic_slice | solution.py:379
  46.3 1.7 %collective-permute-start.7 = (bf16[384,512]{1,0:T(8,128)(2,1)S(1)}, bf16[384,512]{1,0:T(8,128)(2,1)S(1)}, u32[]{:S(2)}, u32[]{:S(2)}) collective-permute-start(bf16[384,512]{1,0:T(8,128)(2,1)S(1)} %copy-done.8), channel_id=1, source_target_pairs={{0,4},{1,29},{2,6},{3,31},{4,0},{5,9},{6,2},{7,11},{8,12},{9,5},{1... | collective-permute-start | bytes 1179656 | tf_op jit(solution)/shard_map/ppermute | solution.py:49
  48.4 1.8 %collective-permute-start.5 = (bf16[384,512]{1,0:T(8,128)(2,1)S(1)}, bf16[384,512]{1,0:T(8,128)(2,1)S(1)}, u32[]{:S(2)}, u32[]{:S(2)}) collective-permute-start(bf16[384,512]{1,0:T(8,128)(2,1)S(1)} %slice.12), channel_id=1, source_target_pairs={{0,4},{1,29},{2,6},{3,31},{4,0},{5,9},{6,2},{7,11},{8,12},{9,5},{1... | collective-permute-start | bytes 1179656 | tf_op jit(solution)/shard_map/ppermute | solution.py:49
  50.3 3.7 %collective-permute-done.7.refs_9_ = bf16[384,512]{1,0:T(8,128)(2,1)S(1)} collective-permute-done((bf16[384,512]{1,0:T(8,128)(2,1)S(1)}, bf16[384,512]{1,0:T(8,128)(2,1)S(1)}, u32[]{:S(2)}, u32[]{:S(2)}) %collective-permute-start.7) | collective-permute-done | bytes 393248 | tf_op jit(solution)/shard_map/ppermute | solution.py:49
  54.0 1.7 %collective-permute-start.6 = (bf16[384,512]{1,0:T(8,128)(2,1)S(1)}, bf16[384,512]{1,0:T(8,128)(2,1)S(1)}, u32[]{:S(2)}, u32[]{:S(2)}) collective-permute-start(bf16[384,512]{1,0:T(8,128)(2,1)S(1)} %slice.10), channel_id=1, source_target_pairs={{0,4},{1,29},{2,6},{3,31},{4,0},{5,9},{6,2},{7,11},{8,12},{9,5},{1... | collective-permute-start | bytes 1179656 | tf_op jit(solution)/shard_map/ppermute | solution.py:49
  55.8 2.5 %collective-permute-done.8.refs_10_ = bf16[384,512]{1,0:T(8,128)(2,1)S(1)} collective-permute-done((bf16[384,512]{1,0:T(8,128)(2,1)S(1)}, bf16[384,512]{1,0:T(8,128)(2,1)S(1)}, u32[]{:S(2)}, u32[]{:S(2)}) %collective-permute-start.8) | collective-permute-done | bytes 393248 | tf_op jit(solution)/shard_map/ppermute | solution.py:49
  58.3 6.3 %shard_map.131 = (f32[1920,128]{1,0:T(8,128)S(1)}, f32[1920,128]{1,0:T(8,128)S(1)}, f32[1920,128]{1,0:T(8,128)S(1)}) custom-call(bf16[384,640]{1,0:T(8,128)(2,1)S(1)} %collective-permute-done.refs_0_.refs_6_, bf16[384,640]{1,0:T(8,128)(2,1)S(1)} %collective-permute-done.1.refs_1_.refs_7_, bf16[384,640]{1,0:T(8,128)(2,1)S(1)} %collective-permute-done.2.refs_2_.refs_8_, ...), custom_call_target="tpu_custom_call" | custom-call | flops 1000 | bytes 1000 | tf_op jit(solution)/shard_map/pallas_call | solution.py:193
  64.6 2.1 %collective-permute-done.6.refs_4_.refs_3_ = bf16[384,512]{1,0:T(8,128)(2,1)S(1)} collective-permute-done((bf16[384,512]{1,0:T(8,128)(2,1)S(1)}, bf16[384,512]{1,0:T(8,128)(2,1)S(1)}, u32[]{:S(2)}, u32[]{:S(2)}) %collective-permute-start.6) | collective-permute-done | bytes 393248 | tf_op jit(solution)/shard_map/ppermute | solution.py:49
  66.7 2.1 %shard_map.132 = (bf16[384,128]{1,0:T(8,128)(2,1)S(1)}, bf16[384,128]{1,0:T(8,128)(2,1)S(1)}, bf16[384,128]{1,0:T(8,128)(2,1)S(1)}) custom-call(bf16[384,640]{1,0:T(8,128)(2,1)S(1)} %collective-permute-done.refs_0_.refs_6_, bf16[384,640]{1,0:T(8,128)(2,1)S(1)} %collective-permute-done.1.refs_1_.refs_7_, ...), custom_call_target="tpu_custom_call" | custom-call | flops 1000 | bytes 1000 | tf_op jit(solution)/shard_map/pallas_call | solution.py:193
  68.8 5.8 %collective-permute-start.10 = (bf16[384,128]{1,0:T(8,128)(2,1)S(1)}, bf16[384,128]{1,0:T(8,128)(2,1)S(1)}, u32[]{:S(2)}, u32[]{:S(2)}) collective-permute-start(bf16[384,128]{1,0:T(8,128)(2,1)S(1)} %get-tuple-element.41), channel_id=1, source_target_pairs={{28,0},{5,1},{30,2},{7,3},{8,4},{1,5},{10,6},{3,7},{4,8},{13,9},{6... | collective-permute-start | bytes 294920 | tf_op jit(solution)/shard_map/ppermute | solution.py:39
  75.8 1.5 %collective-permute-start.11 = (bf16[384,128]{1,0:T(8,128)(2,1)S(1)}, bf16[384,128]{1,0:T(8,128)(2,1)S(1)}, u32[]{:S(2)}, u32[]{:S(2)}) collective-permute-start(bf16[384,128]{1,0:T(8,128)(2,1)S(1)} %get-tuple-element.42), channel_id=1, source_target_pairs={{8,0},{25,1},{10,2},{27,3},{28,4},{13,5},{30,6},{15,7},{16,8},{1,9... | collective-permute-start | bytes 294920 | tf_op jit(solution)/shard_map/ppermute | solution.py:39
  78.2 3.7 %collective-permute-done.11 = bf16[384,128]{1,0:T(8,128)(2,1)S(1)} collective-permute-done((bf16[384,128]{1,0:T(8,128)(2,1)S(1)}, bf16[384,128]{1,0:T(8,128)(2,1)S(1)}, u32[]{:S(2)}, u32[]{:S(2)}) %collective-permute-start.11) | collective-permute-done | bytes 98336 | tf_op jit(solution)/shard_map/ppermute | solution.py:39
  82.0 3.9 %collective-permute-done.12 = bf16[384,128]{1,0:T(8,128)(2,1)S(1)} collective-permute-done((bf16[384,128]{1,0:T(8,128)(2,1)S(1)}, bf16[384,128]{1,0:T(8,128)(2,1)S(1)}, u32[]{:S(2)}, u32[]{:S(2)}) %collective-permute-start.12) | collective-permute-done | bytes 98336 | tf_op jit(solution)/shard_map/ppermute | solution.py:39
  86.0 1.9 %collective-permute-start.13 = (bf16[384,384]{1,0:T(8,128)(2,1)S(1)}, bf16[384,384]{1,0:T(8,128)(2,1)}, u32[]{:S(2)}, u32[]{:S(2)}) collective-permute-start(bf16[384,384]{1,0:T(8,128)(2,1)S(1)} %constant_dynamic-update-slice_fusion.refs_1_), channel_id=1, source_target_pairs={{0,2},{1,3},{2,0},{3,1},{4,6},{5,7},{6,4},{7,5},{8,10},{9,11},{10,... | collective-permute-start | bytes 884744 | tf_op jit(solution)/shard_map/ppermute | solution.py:57
  87.8 1.5 %shard_map.133.refs_1_ = bf16[384,256]{1,0:T(8,128)(2,1)S(1)} custom-call(bf16[384,256]{1,0:T(8,128)(2,1)S(1)} %get-tuple-element.32.refs_3_.refs_4_.refs_0_.refs_1_, bf16[384,256]{1,0:T(8,128)(2,1)S(1)} %get-tuple-element.32.refs_3_.refs_4_.refs_0_.refs_1_, bf16[384,512]{1,0:T(8,128)(2,1)S(1)} %collective-permute-done.5.refs_3_.refs_2_, ...), custom_call_target="tpu_custom_call" | custom-call | flops 1000 | bytes 1000 | tf_op jit(solution)/shard_map/pallas_call | solution.py:193
  90.7 2.4 %collective-permute-done.13.refs_1_ = bf16[384,384]{1,0:T(8,128)(2,1)} collective-permute-done((bf16[384,384]{1,0:T(8,128)(2,1)S(1)}, bf16[384,384]{1,0:T(8,128)(2,1)}, u32[]{:S(2)}, u32[]{:S(2)}) %collective-permute-start.13) | collective-permute-done | bytes 294944 | tf_op jit(solution)/shard_map/ppermute | solution.py:57
  94.5 1.8 %collective-permute-start.19 = (bf16[384,256]{1,0:T(8,128)(2,1)S(1)}, bf16[384,256]{1,0:T(8,128)(2,1)S(1)}, u32[]{:S(2)}, u32[]{:S(2)}) collective-permute-start(bf16[384,256]{1,0:T(8,128)(2,1)S(1)} %shard_map.133.refs_1_), channel_id=1, source_target_pairs={{0,3},{1,2},{2,1},{3,0},{4,7},{5,6},{6,5},{7,4},{8,11},{9,10},{10,... | collective-permute-start | bytes 589832 | tf_op jit(solution)/shard_map/ppermute | solution.py:57
  96.8 1.5 %copy-done.2 = bf16[3,256,1280]{2,1,0:T(8,128)(2,1)S(1)} copy-done((bf16[3,256,1280]{2,1,0:T(8,128)(2,1)S(1)}, bf16[3,256,1280]{2,1,0:T(8,128)(2,1)}, u32[]{:S(2)}) %copy-start.2) | copy-done | bytes 1966104
  99.8 2.3 %shard_map.134.refs_7_ = f32[384,1280]{1,0:T(8,128)S(1)} custom-call(s32[9]{0:T(128)S(1)} %stack.39.head_ref.refs_0_, bf16[384,256]{1,0:T(8,128)(2,1)S(1)} %shard_map.133.refs_1_, bf16[384,256]{1,0:T(8,128)(2,1)} %collective-permute-done.20.refs_2_, bf16[640,1280]{1,0:T(8,128)(2,1)S(1)} %get-tuple-element.56.refs_3_, ...), custom_call_target="tpu_custom_call" | custom-call | flops 1000 | bytes 1000 | tf_op jit(solution)/shard_map/pallas_call | solution.py:265
  102.1 3.9 %collective-permute-done.18.refs_1_ = bf16[384,256]{1,0:T(8,128)(2,1)S(1)} collective-permute-done((bf16[384,256]{1,0:T(8,128)(2,1)S(1)}, bf16[384,256]{1,0:T(8,128)(2,1)S(1)}, u32[]{:S(2)}, u32[]{:S(2)}) %collective-permute-start.18) | collective-permute-done | bytes 196640 | tf_op jit(solution)/shard_map/ppermute | solution.py:57
  106.0 2.3 %shard_map.135.refs_5_ = f32[384,1280]{1,0:T(8,128)S(1)} custom-call(s32[9]{0:T(128)S(1)} %stack.39.head_ref.refs_0_, bf16[384,256]{1,0:T(8,128)(2,1)S(1)} %collective-permute-done.18.refs_1_, bf16[384,256]{1,0:T(8,128)(2,1)S(1)} %collective-permute-done.19.refs_2_, bf16[640,640]{1,0:T(8,128)(2,1)} %collective-permute-done.3.refs_3_, ...), custom_call_target="tpu_custom_call" | custom-call | flops 1000 | bytes 1000 | tf_op jit(solution)/shard_map/pallas_call | solution.py:265
  108.4 2.7 %shard_map.136.refs_7_ = f32[384,1280]{1,0:T(8,128)S(1)} custom-call(s32[9]{0:T(128)S(1)} %stack.39.head_ref.refs_0_, bf16[384,384]{1,0:T(8,128)(2,1)S(1)} %constant_dynamic-update-slice_fusion.refs_1_, bf16[384,384]{1,0:T(8,128)(2,1)S(1)} %collective-permute-done.16.refs_2_, bf16[640,1280]{1,0:T(8,128)(2,1)S(1)} %get-tuple-element.56.refs_3_, ...), custom_call_target="tpu_custom_call" | custom-call | flops 1000 | bytes 1000 | tf_op jit(solution)/shard_map/pallas_call | solution.py:265
  111.1 5.3 %shard_map.138 = (bf16[384,1280]{1,0:T(8,128)(2,1)}, bf16[80,512]{1,0:T(8,128)(2,1)S(1)}) custom-call(s32[9]{0:T(128)S(1)} %stack.39.head_ref.refs_0_, bf16[384,384]{1,0:T(8,128)(2,1)} %collective-permute-done.13.refs_1_, bf16[384,384]{1,0:T(8,128)(2,1)S(1)} %collective-permute-done.14.refs_2_, bf16[640,640]{1,0:T(8,128)(2,1)} %collective-permute-done.3.refs_3_, ...), custom_call_target="tpu_custom_call" | custom-call | flops 1000 | bytes 1000 | tf_op jit(solution)/shard_map/pallas_call | solution.py:456
  118.9 2.1 %collective-permute-done.23.m3 = bf16[80,512]{1,0:T(8,128)(2,1)S(1)} collective-permute-done((bf16[80,512]{1,0:T(8,128)(2,1)S(1)}, bf16[80,512]{1,0:T(8,128)(2,1)S(1)}, u32[]{:S(2)}, u32[]{:S(2)}) %collective-permute-start.23) | collective-permute-done | bytes 81952 | tf_op jit(solution)/shard_map/ppermute | solution.py:57
  121.0 1.9 %collective-permute-done.22.m2 = bf16[80,512]{1,0:T(8,128)(2,1)S(1)} collective-permute-done((bf16[80,512]{1,0:T(8,128)(2,1)S(1)}, bf16[80,512]{1,0:T(8,128)(2,1)S(1)}, u32[]{:S(2)}, u32[]{:S(2)}) %collective-permute-start.22) | collective-permute-done | bytes 81952 | tf_op jit(solution)/shard_map/ppermute | solution.py:57
  123.8 7.1 %collective-permute-start.24 = (bf16[64,384]{1,0:T(8,128)(2,1)S(1)}, bf16[64,384]{1,0:T(8,128)(2,1)S(1)}, u32[]{:S(2)}, u32[]{:S(2)}) collective-permute-start(bf16[64,384]{1,0:T(8,128)(2,1)S(1)} %get-tuple-element.52), channel_id=1, source_target_pairs={{4,0},{8,4},{12,8},{16,12},{20,16},{24,20},{28,24},{32,28},{36,32}... | collective-permute-start | bytes 147464 | tf_op jit(solution)/shard_map/ppermute | solution.py:63
  130.8 1.7 %collective-permute-done.24 = bf16[64,384]{1,0:T(8,128)(2,1)S(1)} collective-permute-done((bf16[64,384]{1,0:T(8,128)(2,1)S(1)}, bf16[64,384]{1,0:T(8,128)(2,1)S(1)}, u32[]{:S(2)}, u32[]{:S(2)}) %collective-permute-start.24) | collective-permute-done | bytes 49184 | tf_op jit(solution)/shard_map/ppermute | solution.py:63
  (67 shorter events, 12.8 us)
Async XLA Ops:
  0.6 4.6 %copy-start.6 = (bf16[384,640]{1,0:T(8,128)(2,1)S(1)}, bf16[384,640]{1,0:T(8,128)(2,1)}, u32[]{:S(2)}) copy-start(bf16[384,640]{1,0:T(8,128)(2,1)} %v_ref.1) | copy-start | bytes 1474564
  3.5 38.6 %collective-permute-start.4 = (bf16[640,640]{1,0:T(8,128)(2,1)}, bf16[640,640]{1,0:T(8,128)(2,1)}, u32[]{:S(2)}, u32[]{:S(2)}) collective-permute-start(bf16[640,640]{1,0:T(8,128)(2,1)} %get-tuple-element.57), channel_id=1, source_target_pairs={{0,3},{1,2},{2,1},{3,0},{4,7},{5,6},{6,5},{7,4},{8,11},{9,10},{10,... | collective-permute-start | bytes 2457608 | tf_op jit(solution)/shard_map/ppermute | solution.py:57
  4.5 37.6 %collective-permute-start.3 = (bf16[640,640]{1,0:T(8,128)(2,1)}, bf16[640,640]{1,0:T(8,128)(2,1)}, u32[]{:S(2)}, u32[]{:S(2)}) collective-permute-start(bf16[640,640]{1,0:T(8,128)(2,1)} %get-tuple-element.58), channel_id=1, source_target_pairs={{0,2},{1,3},{2,0},{3,1},{4,6},{5,7},{6,4},{7,5},{8,10},{9,11},{10,... | collective-permute-start | bytes 2457608 | tf_op jit(solution)/shard_map/ppermute | solution.py:57
  7.9 34.2 %collective-permute-start.2 = (bf16[384,640]{1,0:T(8,128)(2,1)}, bf16[384,640]{1,0:T(8,128)(2,1)S(1)}, u32[]{:S(2)}, u32[]{:S(2)}) collective-permute-start(bf16[384,640]{1,0:T(8,128)(2,1)} %get-tuple-element.30), channel_id=1, source_target_pairs={{0,20},{1,13},{2,22},{3,15},{4,16},{5,25},{6,18},{7,27},{8,28},{9,... | collective-permute-start | bytes 1474568 | tf_op jit(solution)/shard_map/ppermute | solution.py:39
  14.7 33.4 %collective-permute-start = (bf16[384,640]{1,0:T(8,128)(2,1)}, bf16[384,640]{1,0:T(8,128)(2,1)S(1)}, u32[]{:S(2)}, u32[]{:S(2)}) collective-permute-start(bf16[384,640]{1,0:T(8,128)(2,1)} %get-tuple-element.28), channel_id=1, source_target_pairs={{0,28},{1,5},{2,30},{3,7},{4,8},{5,1},{6,10},{7,3},{8,4},{9,13},{1... | collective-permute-start | bytes 1474568 | tf_op jit(solution)/shard_map/ppermute | solution.py:39
  14.7 33.8 %collective-permute-start.1 = (bf16[384,640]{1,0:T(8,128)(2,1)}, bf16[384,640]{1,0:T(8,128)(2,1)S(1)}, u32[]{:S(2)}, u32[]{:S(2)}) collective-permute-start(bf16[384,640]{1,0:T(8,128)(2,1)} %get-tuple-element.29), channel_id=1, source_target_pairs={{0,8},{1,25},{2,10},{3,27},{4,28},{5,13},{6,30},{7,15},{8,16},{9,1... | collective-permute-start | bytes 1474568 | tf_op jit(solution)/shard_map/ppermute | solution.py:39
  17.1 29.1 %copy-start.8 = (bf16[384,512]{1,0:T(8,128)(2,1)S(1)}, bf16[384,512]{1,0:T(8,128)(2,1)}, u32[]{:S(2)}) copy-start(bf16[384,512]{1,0:T(8,128)(2,1)} %copy-done.7) | copy-start | bytes 1179652
  42.1 26.7 %collective-permute-start.9 = (bf16[640,640]{1,0:T(8,128)(2,1)}, bf16[640,640]{1,0:T(8,128)(2,1)S(1)}, u32[]{:S(2)}, u32[]{:S(2)}) collective-permute-start(bf16[640,640]{1,0:T(8,128)(2,1)} %collective-permute-done.3.refs_3_), channel_id=1, source_target_pairs={{0,64},{4,68},{8,72},{12,76},{16,80},{20,84},{24,88},{28,92},{32,9... | collective-permute-start | bytes 2457608 | tf_op jit(solution)/shard_map/ppermute | solution.py:53
  46.3 50.0 %collective-permute-start.17 = (bf16[640,1280]{1,0:T(8,128)(2,1)}, bf16[640,1280]{1,0:T(8,128)(2,1)}, u32[]{:S(2)}, u32[]{:S(2)}) collective-permute-start(bf16[640,1280]{1,0:T(8,128)(2,1)} %get-tuple-element.55), channel_id=1, source_target_pairs={{0,1},{1,0},{2,3},{3,2},{4,5},{5,4},{6,7},{7,6},{8,9},{9,8},{10,11... | collective-permute-start | bytes 4915208 | tf_op jit(solution)/shard_map/ppermute | solution.py:57
  46.3 7.8 %collective-permute-start.7 = (bf16[384,512]{1,0:T(8,128)(2,1)S(1)}, bf16[384,512]{1,0:T(8,128)(2,1)S(1)}, u32[]{:S(2)}, u32[]{:S(2)}) collective-permute-start(bf16[384,512]{1,0:T(8,128)(2,1)S(1)} %copy-done.8), channel_id=1, source_target_pairs={{0,4},{1,29},{2,6},{3,31},{4,0},{5,9},{6,2},{7,11},{8,12},{9,5},{1... | collective-permute-start | bytes 1179656 | tf_op jit(solution)/shard_map/ppermute | solution.py:49
  48.0 10.2 %collective-permute-start.8 = (bf16[384,512]{1,0:T(8,128)(2,1)S(1)}, bf16[384,512]{1,0:T(8,128)(2,1)S(1)}, u32[]{:S(2)}, u32[]{:S(2)}) collective-permute-start(bf16[384,512]{1,0:T(8,128)(2,1)S(1)} %slice.13), channel_id=1, source_target_pairs={{0,4},{1,29},{2,6},{3,31},{4,0},{5,9},{6,2},{7,11},{8,12},{9,5},{1... | collective-permute-start | bytes 1179656 | tf_op jit(solution)/shard_map/ppermute | solution.py:49
  48.4 16.2 %collective-permute-start.5 = (bf16[384,512]{1,0:T(8,128)(2,1)S(1)}, bf16[384,512]{1,0:T(8,128)(2,1)S(1)}, u32[]{:S(2)}, u32[]{:S(2)}) collective-permute-start(bf16[384,512]{1,0:T(8,128)(2,1)S(1)} %slice.12), channel_id=1, source_target_pairs={{0,4},{1,29},{2,6},{3,31},{4,0},{5,9},{6,2},{7,11},{8,12},{9,5},{1... | collective-permute-start | bytes 1179656 | tf_op jit(solution)/shard_map/ppermute | solution.py:49
  54.0 12.6 %collective-permute-start.6 = (bf16[384,512]{1,0:T(8,128)(2,1)S(1)}, bf16[384,512]{1,0:T(8,128)(2,1)S(1)}, u32[]{:S(2)}, u32[]{:S(2)}) collective-permute-start(bf16[384,512]{1,0:T(8,128)(2,1)S(1)} %slice.10), channel_id=1, source_target_pairs={{0,4},{1,29},{2,6},{3,31},{4,0},{5,9},{6,2},{7,11},{8,12},{9,5},{1... | collective-permute-start | bytes 1179656 | tf_op jit(solution)/shard_map/ppermute | solution.py:49
  68.8 20.5 %copy-start = (bf16[640,640]{1,0:T(8,128)(2,1)}, bf16[640,640]{1,0:T(8,128)(2,1)S(1)}, u32[]{:S(2)}) copy-start(bf16[640,640]{1,0:T(8,128)(2,1)S(1)} %collective-permute-done.9.refs_4_) | copy-start | bytes 2457604
  68.8 9.4 %collective-permute-start.10 = (bf16[384,128]{1,0:T(8,128)(2,1)S(1)}, bf16[384,128]{1,0:T(8,128)(2,1)S(1)}, u32[]{:S(2)}, u32[]{:S(2)}) collective-permute-start(bf16[384,128]{1,0:T(8,128)(2,1)S(1)} %get-tuple-element.41), channel_id=1, source_target_pairs={{28,0},{5,1},{30,2},{7,3},{8,4},{1,5},{10,6},{3,7},{4,8},{13,9},{6... | collective-permute-start | bytes 294920 | tf_op jit(solution)/shard_map/ppermute | solution.py:39
  74.6 31.5 %collective-permute-start.15 = (bf16[640,640]{1,0:T(8,128)(2,1)}, bf16[640,640]{1,0:T(8,128)(2,1)S(1)}, u32[]{:S(2)}, u32[]{:S(2)}) collective-permute-start(bf16[640,640]{1,0:T(8,128)(2,1)} %collective-permute-done.4.refs_5_), channel_id=1, source_target_pairs={{0,64},{4,68},{8,72},{12,76},{16,80},{20,84},{24,88},{28,92},{32,9... | collective-permute-start | bytes 2457608 | tf_op jit(solution)/shard_map/ppermute | solution.py:53
  75.8 6.2 %collective-permute-start.11 = (bf16[384,128]{1,0:T(8,128)(2,1)S(1)}, bf16[384,128]{1,0:T(8,128)(2,1)S(1)}, u32[]{:S(2)}, u32[]{:S(2)}) collective-permute-start(bf16[384,128]{1,0:T(8,128)(2,1)S(1)} %get-tuple-element.42), channel_id=1, source_target_pairs={{8,0},{25,1},{10,2},{27,3},{28,4},{13,5},{30,6},{15,7},{16,8},{1,9... | collective-permute-start | bytes 294920 | tf_op jit(solution)/shard_map/ppermute | solution.py:39
  77.2 8.7 %collective-permute-start.12 = (bf16[384,128]{1,0:T(8,128)(2,1)S(1)}, bf16[384,128]{1,0:T(8,128)(2,1)S(1)}, u32[]{:S(2)}, u32[]{:S(2)}) collective-permute-start(bf16[384,128]{1,0:T(8,128)(2,1)S(1)} %get-tuple-element.43), channel_id=1, source_target_pairs={{20,0},{13,1},{22,2},{15,3},{16,4},{25,5},{18,6},{27,7},{28,8},{21... | collective-permute-start | bytes 294920 | tf_op jit(solution)/shard_map/ppermute | solution.py:39
  85.9 7.2 %copy-start.12 = (s32[129]{0:T(256)S(1)}, s32[129]{0:T(256)}, u32[]{:S(2)}) copy-start(s32[129]{0:T(256)} %param.21) | copy-start | bytes 1552
  86.0 7.1 %collective-permute-start.13 = (bf16[384,384]{1,0:T(8,128)(2,1)S(1)}, bf16[384,384]{1,0:T(8,128)(2,1)}, u32[]{:S(2)}, u32[]{:S(2)}) collective-permute-start(bf16[384,384]{1,0:T(8,128)(2,1)S(1)} %constant_dynamic-update-slice_fusion.refs_1_), channel_id=1, source_target_pairs={{0,2},{1,3},{2,0},{3,1},{4,6},{5,7},{6,4},{7,5},{8,10},{9,11},{10,... | collective-permute-start | bytes 884744 | tf_op jit(solution)/shard_map/ppermute | solution.py:57
  89.3 5.2 %collective-permute-start.20 = (bf16[384,256]{1,0:T(8,128)(2,1)S(1)}, bf16[384,256]{1,0:T(8,128)(2,1)}, u32[]{:S(2)}, u32[]{:S(2)}) collective-permute-start(bf16[384,256]{1,0:T(8,128)(2,1)S(1)} %shard_map.133.refs_1_), channel_id=1, source_target_pairs={{0,1},{1,0},{2,3},{3,2},{4,5},{5,4},{6,7},{7,6},{8,9},{9,8},{10,11... | collective-permute-start | bytes 589832 | tf_op jit(solution)/shard_map/ppermute | solution.py:57
  90.1 18.3 %collective-permute-start.16 = (bf16[384,384]{1,0:T(8,128)(2,1)S(1)}, bf16[384,384]{1,0:T(8,128)(2,1)S(1)}, u32[]{:S(2)}, u32[]{:S(2)}) collective-permute-start(bf16[384,384]{1,0:T(8,128)(2,1)S(1)} %constant_dynamic-update-slice_fusion.refs_1_), channel_id=1, source_target_pairs={{0,1},{1,0},{2,3},{3,2},{4,5},{5,4},{6,7},{7,6},{8,9},{9,8},{10,11... | collective-permute-start | bytes 884744 | tf_op jit(solution)/shard_map/ppermute | solution.py:57
  93.1 18.0 %collective-permute-start.14 = (bf16[384,384]{1,0:T(8,128)(2,1)}, bf16[384,384]{1,0:T(8,128)(2,1)S(1)}, u32[]{:S(2)}, u32[]{:S(2)}) collective-permute-start(bf16[384,384]{1,0:T(8,128)(2,1)} %collective-permute-done.13.refs_1_), channel_id=1, source_target_pairs={{0,1},{1,0},{2,3},{3,2},{4,5},{5,4},{6,7},{7,6},{8,9},{9,8},{10,11... | collective-permute-start | bytes 884744 | tf_op jit(solution)/shard_map/ppermute | solution.py:57
  94.5 7.6 %collective-permute-start.19 = (bf16[384,256]{1,0:T(8,128)(2,1)S(1)}, bf16[384,256]{1,0:T(8,128)(2,1)S(1)}, u32[]{:S(2)}, u32[]{:S(2)}) collective-permute-start(bf16[384,256]{1,0:T(8,128)(2,1)S(1)} %shard_map.133.refs_1_), channel_id=1, source_target_pairs={{0,3},{1,2},{2,1},{3,0},{4,7},{5,6},{6,5},{7,4},{8,11},{9,10},{10,... | collective-permute-start | bytes 589832 | tf_op jit(solution)/shard_map/ppermute | solution.py:57
  96.3 9.7 %collective-permute-start.18 = (bf16[384,256]{1,0:T(8,128)(2,1)S(1)}, bf16[384,256]{1,0:T(8,128)(2,1)S(1)}, u32[]{:S(2)}, u32[]{:S(2)}) collective-permute-start(bf16[384,256]{1,0:T(8,128)(2,1)S(1)} %shard_map.133.refs_1_), channel_id=1, source_target_pairs={{0,2},{1,3},{2,0},{3,1},{4,6},{5,7},{6,4},{7,5},{8,10},{9,11},{10,... | collective-permute-start | bytes 589832 | tf_op jit(solution)/shard_map/ppermute | solution.py:57
  99.8 6.2 %copy-start.1 = (bf16[640,640]{1,0:T(8,128)(2,1)S(1)}, bf16[640,640]{1,0:T(8,128)(2,1)}, u32[]{:S(2)}) copy-start(bf16[640,640]{1,0:T(8,128)(2,1)} %copy-done) | copy-start | bytes 2457604
  111.1 11.8 %copy-start.10 = (f32[384,64]{0,1:T(8,128)S(1)}, f32[384,64]{0,1:T(8,128)}, u32[]{:S(2)}) copy-start(f32[384,64]{0,1:T(8,128)} %param.18) | copy-start | bytes 294916
  111.1 21.4 %copy-start.11 = (f32[384,64]{0,1:T(8,128)S(1)}, f32[384,64]{0,1:T(8,128)}, u32[]{:S(2)}) copy-start(f32[384,64]{0,1:T(8,128)} %param.19) | copy-start | bytes 294916
  116.4 4.6 %collective-permute-start.23 = (bf16[80,512]{1,0:T(8,128)(2,1)S(1)}, bf16[80,512]{1,0:T(8,128)(2,1)S(1)}, u32[]{:S(2)}, u32[]{:S(2)}) collective-permute-start(bf16[80,512]{1,0:T(8,128)(2,1)S(1)} %get-tuple-element.50.m0), channel_id=1, source_target_pairs={{0,3},{1,2},{2,1},{3,0},{4,7},{5,6},{6,5},{7,4},{8,11},{9,10},{10,... | collective-permute-start | bytes 245768 | tf_op jit(solution)/shard_map/ppermute | solution.py:57
  117.1 5.9 %collective-permute-start.22 = (bf16[80,512]{1,0:T(8,128)(2,1)S(1)}, bf16[80,512]{1,0:T(8,128)(2,1)S(1)}, u32[]{:S(2)}, u32[]{:S(2)}) collective-permute-start(bf16[80,512]{1,0:T(8,128)(2,1)S(1)} %get-tuple-element.50.m0), channel_id=1, source_target_pairs={{0,2},{1,3},{2,0},{3,1},{4,6},{5,7},{6,4},{7,5},{8,10},{9,11},{10,... | collective-permute-start | bytes 245768 | tf_op jit(solution)/shard_map/ppermute | solution.py:57
  118.0 4.9 %collective-permute-start.21 = (bf16[80,512]{1,0:T(8,128)(2,1)S(1)}, bf16[80,512]{1,0:T(8,128)(2,1)S(1)}, u32[]{:S(2)}, u32[]{:S(2)}) collective-permute-start(bf16[80,512]{1,0:T(8,128)(2,1)S(1)} %get-tuple-element.50.m0), channel_id=1, source_target_pairs={{0,1},{1,0},{2,3},{3,2},{4,5},{5,4},{6,7},{7,6},{8,9},{9,8},{10,11... | collective-permute-start | bytes 245768 | tf_op jit(solution)/shard_map/ppermute | solution.py:57
  123.8 8.8 %collective-permute-start.24 = (bf16[64,384]{1,0:T(8,128)(2,1)S(1)}, bf16[64,384]{1,0:T(8,128)(2,1)S(1)}, u32[]{:S(2)}, u32[]{:S(2)}) collective-permute-start(bf16[64,384]{1,0:T(8,128)(2,1)S(1)} %get-tuple-element.52), channel_id=1, source_target_pairs={{4,0},{8,4},{12,8},{16,12},{20,16},{24,20},{28,24},{32,28},{36,32}... | collective-permute-start | bytes 147464 | tf_op jit(solution)/shard_map/ppermute | solution.py:63
  (6 other events, 15.2 us)

commit v2 on v1

--- a/solution.py
+++ b/solution.py
@@ -16,14 +16,15 @@
 BF16 = jnp.bfloat16
 COLUMN_BLOCK = 256
 SPREAD_HEADS = 4
-HALF_STRIDE = 16
 SMALL = pl.CostEstimate(flops=1000, bytes_accessed=1000, transcendentals=0)
+ATTEND_COST = pl.CostEstimate(flops=9_000_000_000, bytes_accessed=1000, transcendentals=0)
 EXP_SCALE = HD ** (-0.5) / math.log(2.0)
 VMEM_LIMIT = 16 * 1024 * 1024
-
-
-def params():
-    return pltpu.CompilerParams(vmem_limit_bytes=VMEM_LIMIT)
+COPY_LIMIT = 56 * 1024 * 1024
+
+
+def params(limit=VMEM_LIMIT):
+    return pltpu.CompilerParams(vmem_limit_bytes=limit)
 
 
 def spread(x, distance, backward=False):
@@ -49,8 +50,12 @@
     return lax.ppermute(x, ("frame", "tensor"), pairs)
 
 
-def swap_half(x):
-    return lax.ppermute(x, "frame", [(i, i ^ HALF_STRIDE) for i in range(lax.axis_size("frame"))])
+def across_both(x):
+    pairs = []
+    for frame in range(lax.axis_size("frame")):
+        for at in range(N_TENSOR):
+            pairs.append((frame * N_TENSOR + at, (frame ^ PART) * N_TENSOR + (at ^ 2)))
+    return lax.ppermute(x, ("frame", "tensor"), pairs)
 
 
 def peer(x, mask):
@@ -92,35 +97,34 @@
     return hi, mid, (rest - mid.astype(F32)).astype(BF16)
 
 
-def pack_kernel(head_ref, q_ref, k_ref, v_ref, x1_ref, x2_ref, x3_ref, kv_ref, q_out_ref, sem):
+def pack_kernel(
+    head_ref, q_hbm, k_hbm, v_hbm, x1_ref, x2_ref, x3_ref, kv_ref, q_out_ref, q_ref, k_ref, v_ref, sem
+):
     common = pl.ds(SPREAD_HEADS * HD, HD)
+    copies = [
+        pltpu.make_async_copy(source, target, sem.at[at])
+        for at, (source, target) in enumerate(((k_hbm, k_ref), (v_hbm, v_ref), (q_hbm, q_ref)))
+    ]
+    for copy in copies:
+        copy.start()
 
     def lanes(at):
         return pl.ds(pl.multiple_of(head_ref[at] * HD, HD), HD)
 
-    copies = []
-
-    def move(source, source_lanes, target, slot):
-        copy = pltpu.make_async_copy(
-            source.at[:, source_lanes], target.at[:, pl.ds(slot * HD, HD)], sem.at[len(copies)]
-        )
-        copy.start()
-        copies.append(copy)
-
-    for at, ref in ((3, x3_ref), (2, x2_ref), (1, x1_ref), (0, kv_ref)):
-        move(k_ref, lanes(at), ref, 0)
-        move(v_ref, lanes(at), ref, 1)
-        move(k_ref, common, ref, 2)
-        move(v_ref, common, ref, 3)
-        if at:
-            move(q_ref, lanes(at), ref, 4)
-    move(q_ref, lanes(0), q_out_ref, 0)
-    move(q_ref, common, q_out_ref, 1)
-    for copy in copies:
+    targets = ((3, x3_ref), (2, x2_ref), (1, x1_ref), (0, kv_ref))
+    for slot, (copy, source) in enumerate(zip(copies[:2], (k_ref, v_ref))):
         copy.wait()
-
-
-def attend_kernel(query_lanes, own_query, block_count, state_low, first, last, *refs):
+        for at, ref in targets:
+            ref[:, slot * HD : (slot + 1) * HD] = source[:, lanes(at)]
+            ref[:, (slot + 2) * HD : (slot + 3) * HD] = source[:, common]
+    copies[2].wait()
+    for at, ref in targets[:3]:
+        ref[:, 4 * HD :] = q_ref[:, lanes(at)]
+    q_out_ref[:, 0:HD] = q_ref[:, lanes(0)]
+    q_out_ref[:, HD:] = q_ref[:, common]
+
+
+def attend_kernel(query_lanes, block_count, first, last, *refs):
     refs = list(refs)
     q_refs = [refs.pop(0) for _ in query_lanes]
     blocks = [refs.pop(0) for _ in range(block_count)]
@@ -132,7 +136,7 @@
         query = q_ref[:, q_low : q_low + HD]
         scores = [dot_t(query, ref[:, key_low : key_low + HD]) for ref in blocks]
         peak = max_of([jnp.max(s, axis=1, keepdims=True) for s in scores])
-        rows = slice((state_low + at) * row_count, (state_low + at + 1) * row_count)
+        rows = slice(at * row_count, (at + 1) * row_count)
         if not first:
             old_peak = peak_in[rows, 0:1]
             peak = jnp.maximum(peak, old_peak)
@@ -150,10 +154,11 @@
             total = total + total_in[rows, :] * shrink
         if last:
             out = (acc / jnp.sum(total, axis=1, keepdims=True)).astype(BF16)
-            if own_query:
-                refs[0][:, at * HD : (at + 1) * HD] = out
+            if at < PART // 2 - 1:
+                refs[at][...] = out
             else:
-                refs[at][...] = out
+                low = (at - PART // 2 + 1) * HD
+                refs[-1][:, low : low + HD] = out
         else:
             refs[0][rows, :] = acc
             refs[1][rows, :] = jnp.broadcast_to(peak, acc.shape)
@@ -174,23 +179,21 @@
     return result
 
 
-def attend(queries, query_lanes, blocks, state, state_low, last, own_query):
+def attend(queries, query_lanes, blocks, state, cost):
     row_count = queries[0].shape[0]
     operands = list(queries) + list(blocks)
     first = state is None
-    if not first:
+    if first:
+        out_shape = [jax.ShapeDtypeStruct((row_count * len(queries), HD), F32)] * 3
+    else:
         operands += list(state)
-    if not last:
-        out_shape = [jax.ShapeDtypeStruct((row_count * len(queries), HD), F32)] * 3
-    elif own_query:
-        out_shape = jax.ShapeDtypeStruct((row_count, HD * len(queries)), BF16)
-    else:
-        out_shape = [jax.ShapeDtypeStruct((row_count, HD), BF16)] * len(queries)
+        out_shape = [jax.ShapeDtypeStruct((row_count, HD), BF16)] * 3
+        out_shape += [jax.ShapeDtypeStruct((row_count, 2 * HD), BF16)]
 
     def body(*refs):
-        attend_kernel(query_lanes, own_query, len(blocks), state_low, first, last, *refs)
-
-    return pl.pallas_call(body, out_shape=out_shape, compiler_params=params(), cost_estimate=SMALL)(*operands)
+        attend_kernel(query_lanes, len(blocks), first, not first, *refs)
+
+    return pl.pallas_call(body, out_shape=out_shape, compiler_params=params(), cost_estimate=cost)(*operands)
 
 
 def modulate_kernel(embedding_ref, time_ref, head_ref, gate_ref, lifted_ref, extra_ref):
@@ -229,65 +232,53 @@
     return jnp.concatenate(parts, axis=0)
 
 
-def column_blocks(width):
-    return [(low, min(COLUMN_BLOCK, width - low)) for low in range(0, width, COLUMN_BLOCK)]
-
-
-def project_kernel(halves, row_sets, with_base, head_ref, *refs):
-    count = len(row_sets)
-    out_ref = refs[-1]
+def mix_kernel(out_dtype, terms, with_base, head_ref, *refs):
+    refs = list(refs)
+    sources = []
+    for input_count, weight_count, rows, column in terms:
+        inputs = [refs.pop(0) for _ in range(input_count)]
+        sources.append((inputs, [refs.pop(0) for _ in range(weight_count)], rows, column))
+    base_ref = refs.pop(0) if with_base else None
+    out_ref = refs[0]
     width = out_ref.shape[1]
-    inputs, weights = refs[:count], refs[count : (1 + halves) * count]
-    base_ref = refs[(1 + halves) * count] if with_base else None
-    for half in range(halves):
-        offset = 0
-        if halves > 1:
-            offset = pl.multiple_of((head_ref[8] ^ half) * (width // halves), HD)
-        for low, size in column_blocks(width // halves):
-            out_lanes = pl.ds(offset + low, size)
-            acc = base_ref[:, out_lanes] if with_base else None
-            for at, (a_ref, rows) in enumerate(zip(inputs, row_sets)):
-                w_ref = weights[at * halves + half]
-                part = dot(a_ref[...], head_rows(head_ref, w_ref, rows, pl.ds(low, size)))
-                acc = part if acc is None else acc + part
-            out_ref[:, out_lanes] = acc
-
-
-def project(heads, inputs, weights, row_sets, base=None):
-    row_count = inputs[0].shape[0]
-    halves = len(weights) // len(inputs)
-    width = weights[0].shape[1] * halves
-    operands = [heads, *inputs, *weights] + ([] if base is None else [base])
+    for low in range(0, width, COLUMN_BLOCK):
+        lanes = pl.ds(low, COLUMN_BLOCK)
+        acc = base_ref[:, lanes] if with_base else None
+        for inputs, weights, rows, column in sources:
+            offset = 0 if column is None else pl.multiple_of(head_ref[column] * width, HD)
+            weight = head_rows(head_ref, weights[0], rows, pl.ds(offset + low, COLUMN_BLOCK))
+            value = inputs[0][...]
+            if len(inputs) > 1:
+                value = jnp.concatenate([ref[...] for ref in inputs], axis=1)
+            part = dot(value, weight)
+            acc = part if acc is None else acc + part
+        out_ref[:, lanes] = acc.astype(out_dtype)
+
+
+def mix(heads, width, terms, out_dtype, base=None):
+    shapes, operands = [], [heads]
+    for inputs, weights, rows, column in terms:
+        shapes.append((len(inputs), len(weights), rows, column))
+        operands += [*inputs, *weights]
+    if base is not None:
+        operands.append(base)
+    row_count = operands[1].shape[0]
 
     def body(*refs):
-        project_kernel(halves, row_sets, base is not None, *refs)
+        mix_kernel(out_dtype, shapes, base is not None, *refs)
 
     return pl.pallas_call(
         body,
         in_specs=[pl.BlockSpec(memory_space=pltpu.SMEM)]
         + [pl.BlockSpec(memory_space=pltpu.VMEM)] * (len(operands) - 1),
-        out_shape=jax.ShapeDtypeStruct((row_count, width), F32),
+        out_shape=jax.ShapeDtypeStruct((row_count, width), out_dtype),
         compiler_params=params(),
         cost_estimate=SMALL,
     )(*operands)
 
 
 def hidden_kernel(
-    row_sets,
-    head_ref,
-    a0,
-    a1,
-    w0_mine,
-    w0_other,
-    w1_mine,
-    w1_other,
-    acc_ref,
-    in_ref,
-    gate_ref,
-    lifted_ref,
-    extra_ref,
-    stream_ref,
-    message_ref,
+    acc_ref, other_ref, in_ref, gate_ref, lifted_ref, extra_ref, stream_ref, message_ref
 ):
     row_count, width = stream_ref.shape
     channels = extra_ref.shape[0]
@@ -295,11 +286,9 @@
     squares = None
     share = None
     rest = None
-    for half, low, size in [(h, *block) for h in range(2) for block in column_blocks(width // 2)]:
-        lanes = pl.ds(pl.multiple_of((head_ref[8] ^ half) * (width // 2), HD) + low, size)
-        mixed = acc_ref[:, lanes]
-        for a_ref, w_ref, rows in zip((a0, a1), ((w0_mine, w0_other)[half], (w1_mine, w1_other)[half]), row_sets):
-            mixed = mixed + dot(a_ref[...], head_rows(head_ref, w_ref, rows, pl.ds(low, size)))
+    for low in range(0, width, COLUMN_BLOCK):
+        lanes = slice(low, low + COLUMN_BLOCK)
+        mixed = acc_ref[:, lanes] + other_ref[:, lanes].astype(F32)
         hidden = in_ref[:, lanes].astype(F32) + gate_ref[0:1, lanes] * mixed
         high = hidden.astype(BF16)
         stream_ref[:, lanes] = high
@@ -374,58 +363,6 @@
     tensor_index = lax.axis_index("tensor")
     barrier = lax.optimization_barrier
 
-    def columns(mask, low=0, size=width):
-        start = (tensor_index ^ mask) * width + low
-        return lax.dynamic_slice(out_weight, (0, start), (out_weight.shape[0], size))
-
-    core_index = tensor_index % 2
-
-    def heads_of(core):
-        place_in_ring = (frame_index - core) % PART
-        pair, member = place_in_ring // 2, place_in_ring % 2
-        ahead, behind = (pair + 1) % SPREAD_HEADS, (pair + SPREAD_HEADS - 1) % SPREAD_HEADS
-        return [
-            pair,
-            jnp.where(member == 1, ahead, behind),
-            jnp.where(member == 1, behind, ahead),
-            (pair + 2) % SPREAD_HEADS,
-        ]
-
-    half_index = frame_index // HALF_STRIDE % 2
-    heads = jnp.stack(heads_of(core_index) + heads_of(1 - core_index) + [half_index]).astype(jnp.int32)
-    kv_width, packed_width = 4 * HD, 5 * HD
-    x1, x2, x3, own_kv, own_q = pl.pallas_call(
-        pack_kernel,
-        in_specs=[pl.BlockSpec(memory_space=pltpu.SMEM)] + [pl.BlockSpec(memory_space=pl.ANY)] * 3,
-        out_specs=[pl.BlockSpec(memory_space=pl.ANY)] * 5,
-        scratch_shapes=[pltpu.SemaphoreType.DMA((21,))],
-        out_shape=[jax.ShapeDtypeStruct((row_count, packed_width), BF16)] * 3
-        + [jax.ShapeDtypeStruct((row_count, kv_width), BF16), jax.ShapeDtypeStruct((row_count, 2 * HD), BF16)],
-        compiler_params=params(),
-        cost_estimate=SMALL,
-    )(heads, queries, keys, values)
-    x3 = spread(x3, 3)
-    x2 = spread(x2, 2)
-    x1 = spread(x1, 1)
-    half_width = width // 2
-    across = [peer(columns(mask, half_index * half_width, half_width), mask) for mask in (2, 3)]
-    x3, across = barrier((x3, across))
-    across_other = [swap_half(w) for w in across]
-    partner = [swap_pair(own_kv)] + [swap_pair(x[:, :kv_width]) for x in (x1, x2, x3)]
-    queries_in = (x1, x2, x3, own_q, own_q)
-    query_lanes = ((kv_width, False),) * 3 + ((0, False), (HD, True))
-    state = attend(
-        queries_in, query_lanes, (own_kv, x1, x2, x3, *partner[:2]), None, 0, False, False
-    )
-    results = attend(queries_in[:3], query_lanes[:3], partner[2:], state, 0, True, False)
-    mine = attend(queries_in[3:], query_lanes[3:], partner[2:], state, 3, True, True)
-    results, across_other[0] = barrier((results, across_other[0]))
-    back = [spread(x, i + 1, True) for i, x in enumerate(results)]
-    back = jnp.concatenate(back, axis=1)
-
-    weights = [columns(0), peer(columns(1), 1)]
-    far_weights = [across[0], across_other[0], across[1], across_other[1]]
-
     t_now = lookup(timesteps, levels)
     t_next = lookup(timesteps, levels - 1)
     embedding = sinusoid(t_now, TFREQ).astype(BF16)
@@ -441,28 +378,86 @@
         compiler_params=params(),
         cost_estimate=SMALL,
     )(embedding, time_weight, head)
-
-    mine_all = [mine] + [peer(mine, mask) for mask in (1, 2, 3)]
-    back_beside, back_across = peer(back, 1), peer(back, 2)
-    back_last = peer(back_across, 1)
-    mine_rows, back_rows = ((0, None), (4, None)), ((1, 2, 3), (5, 6, 7))
-    acc = project(heads, mine_all[:2], weights, mine_rows)
-    acc = project(heads, mine_all[2:], far_weights, mine_rows, acc)
-    acc = project(heads, [back, back_beside], weights, back_rows, acc)
-
-    def finish_hidden(*refs):
-        hidden_kernel(back_rows, *refs)
+    tables = (gate, lifted, extra, step)
+
+    core_index, side = tensor_index % 2, tensor_index // 2
+    at = (frame_index - core_index) % PART
+    pair, member = at // 2, at % 2
+    ahead, behind = (pair + 1) % SPREAD_HEADS, (pair + SPREAD_HEADS - 1) % SPREAD_HEADS
+    heads = jnp.stack(
+        [
+            pair,
+            jnp.where(member == 1, ahead, behind),
+            jnp.where(member == 1, behind, ahead),
+            (pair + 2) % SPREAD_HEADS,
+            side,
+            core_index,
+            1 - core_index,
+        ]
+    ).astype(jnp.int32)
+    depth = out_weight.shape[0]
+    kv_width, packed_width = 4 * HD, 5 * HD
+    in_smem = pl.BlockSpec(memory_space=pltpu.SMEM)
+    in_hbm = pl.BlockSpec(memory_space=pltpu.HBM)
+    x1, x2, x3, own_kv, own_q = pl.pallas_call(
+        pack_kernel,
+        in_specs=[in_smem] + [in_hbm] * 3,
+        out_specs=[pl.BlockSpec(memory_space=pltpu.VMEM)] * 5,
+        scratch_shapes=[pltpu.VMEM(queries.shape, BF16)] * 3 + [pltpu.SemaphoreType.DMA((3,))],
+        out_shape=[jax.ShapeDtypeStruct((row_count, packed_width), BF16)] * 3
+        + [jax.ShapeDtypeStruct((row_count, kv_width), BF16), jax.ShapeDtypeStruct((row_count, 2 * HD), BF16)],
+        compiler_params=params(COPY_LIMIT),
+        cost_estimate=SMALL,
+    )(heads, queries, keys, values)
+
+    x3 = spread(x3, 3)
+    x2 = spread(x2, 2)
+    x1 = spread(x1, 1)
+    partner = [swap_pair(own_kv)]
+    far = [
+        lax.dynamic_slice(out_weight, (0, ((1 - side) * 2 + core) * width), (depth, width))
+        for core in (core_index, 1 - core_index)
+    ]
+    far = [peer(far[0], 2), across_both(far[1])]
+    own_weight = lax.dynamic_slice(out_weight, (0, side * 2 * width), (depth, 2 * width))
+    x1, x2, x3, partner, own_weight, tables = barrier((x1, x2, x3, partner, own_weight, tables))
+    gate, lifted, extra, step = tables
+    partner += [swap_pair(x[:, :kv_width]) for x in (x1, x2, x3)]
+    queries_in = (x1, x2, x3, own_q, own_q)
+    query_lanes = ((kv_width, False),) * 3 + ((0, False), (HD, True))
+    state = attend(queries_in, query_lanes, (own_kv, x1, x2, x3, partner[0]), None, ATTEND_COST)
+    state, far = barrier((state, far))
+    *results, mine = attend(queries_in, query_lanes, partner[1:], state, SMALL)
+    back = [spread(x, i + 1, True) for i, x in enumerate(results)]
+    back_across = [peer(x, 2) for x in back]
+    mine_across = peer(mine, 2)
+    mine_rows, back_rows = (0, None), (1, 2, 3)
+    sums = [
+        mix(
+            heads,
+            width,
+            [
+                ([mine], [own_weight], mine_rows, column),
+                (back, [own_weight], back_rows, column),
+                ([mine_across], [weight], mine_rows, None),
+            ],
+            F32,
+        )
+        for column, weight in ((6, far[1]), (5, far[0]))
+    ]
+    sent = mix(heads, width, [(back_across, [far[1]], back_rows, None)], BF16, sums[0])
+    kept = mix(heads, width, [(back_across, [far[0]], back_rows, None)], F32, sums[1])
+    received = peer(sent, 1)
 
     stream, message = pl.pallas_call(
-        finish_hidden,
-        in_specs=[pl.BlockSpec(memory_space=pltpu.SMEM)] + [pl.BlockSpec(memory_space=pltpu.VMEM)] * 11,
+        hidden_kernel,
         out_shape=[
             jax.ShapeDtypeStruct((row_count, width), BF16),
             jax.ShapeDtypeStruct((channels + 16, row_count + HD), BF16),
         ],
         compiler_params=params(),
         cost_estimate=SMALL,
-    )(heads, back_across, back_last, *far_weights, acc, stream_in, gate, lifted, extra)
+    )(kept, received, stream_in, gate, lifted, extra)
     messages = [message] + [peer(message, mask) for mask in (1, 2, 3)]
     velocity, updated = pl.pallas_call(
         finish_kernel,

time: 134 us -> 114 us (0.85)
  waiting for transfers between devices: 53 us -> 33.9 us
  starting transfers between devices: 40.5 us -> 37.3 us
  local copies, waits for them, and re-layouts: 9.63 us -> 12 us
    ppermute x6, waiting for transfers between devices: 32.6 us -> 23.6 us  [spread(): return lax.ppermute(x, ('frame', 'tensor'), pairs)]
    ppermute x4, waiting for transfers between devices: 8.29 us -> 2.25 us  [swap_pair(): return lax.ppermute(x, ('frame', 'tensor'), pairs)]
    ppermute x12 -> x9, waiting for transfers between devices: 10.3 us -> 6.2 us  [peer(): return lax.ppermute(x, 'tensor', [(i, i ^ mask) for i in range(N_TENSOR)])]
    pallas_call x3 -> x2, Pallas kernels: 9.9 us -> 13.8 us  [attend(): pl.pallas_call(body, out_shape=out_shape, compiler_params=params(), cost_...]
    pallas_call x5 -> x6, Pallas kernels: 14.5 us -> 11.2 us  [the longest x4 5.89 us: mix(): pl.pallas_call(body, in_specs=[pl.BlockSpec(memory_space=pltpu.SMEM)] + [...]
    slice x3, local copies, waits for them, and re-layouts: 0.08 us -> 3.06 us  [local(): partner += [swap_pair(x[:, :kv_width]) for x in (x1, x2, x3)]]
    ppermute x6, starting transfers between devices: 17.4 us -> 15.2 us  [spread(): return lax.ppermute(x, ('frame', 'tensor'), pairs)]
    ppermute x1, starting transfers between devices: 7.05 us -> 5.12 us  [shifted(): return lax.ppermute(x, axis, pairs)]
  transfers between devices with their start and end apart: 25 -> 21, of which waited for: 11 -> 11; matrix products, arithmetic and copies ran while one was open for 3% -> 9% of each run, Pallas kernels for 15% -> 11%
where the time goes in v2:
time: 114 us
  starting transfers between devices  37.3 us (33%)
  waiting for transfers between devices  33.9 us (30%)
  Pallas kernels  26.4 us (23%)
  local copies, waits for them, and re-layouts  12 us (11%)
  between operations  2.88 us (3%)
  other arithmetic  1.39 us (1%)
    ppermute x6, waiting for transfers between devices, spread(): return lax.ppermute(x, ('frame', 'tensor'), pairs)  23.6 us
    ppermute x6, starting transfers between devices, spread(): return lax.ppermute(x, ('frame', 'tensor'), pairs)  15.2 us
    pallas_call x2, Pallas kernels, attend(): pl.pallas_call(body, out_shape=out_shape, compiler_params=params(), cost_...  13.8 us
    ppermute x9, starting transfers between devices, peer(): return lax.ppermute(x, 'tensor', [(i, i ^ mask) for i in range(N_TENSOR)])  8.35 us
    ppermute x4, starting transfers between devices, swap_pair(): return lax.ppermute(x, ('frame', 'tensor'), pairs)  6.43 us
    ppermute x9, waiting for transfers between devices, peer(): return lax.ppermute(x, 'tensor', [(i, i ^ mask) for i in range(N_TENSOR)])  6.2 us
    pallas_call x4, Pallas kernels, mix(): pl.pallas_call(body, in_specs=[pl.BlockSpec(memory_space=pltpu.SMEM)] + [...  5.89 us
    ppermute x1, starting transfers between devices, shifted(): return lax.ppermute(x, axis, pairs)  5.12 us
  transfers between devices with their start and end apart: 21, of which 11 were waited for; matrix products, arithmetic and copies ran while one was open for 9% of the time, Pallas kernels for 11%

profile of v2, /device:TPU:6, one launch (start us, length us, event | category | flops | bytes accessed | tf_op | source)
XLA Modules:
  0.0 113.9 jit_solution(11665010423082530988)
XLA Ops:
  1.4 3.4 %shard_map.130 = (bf16[384,640]{1,0:T(8,128)(2,1)}, bf16[384,640]{1,0:T(8,128)(2,1)}, bf16[384,640]{1,0:T(8,128)(2,1)}, bf16[384,512]{1,0:T(8,128)(2,1)}, bf16[384,256]{1,0:T(8,128)(2,1)}) custom-call(s32[7]{0:T(128)} %stack.31.head_ref.refs_0_, bf16[384,640]{1,0:T(8,128)(2,1)} %q_hbm.1, bf16[384,640]{1,0:T(8,128)(2,1)} %k_hbm.1, bf16[384,640]{1,0:T(8,128)(2,1)} %v_hbm.1), custom_call_target="tpu_custom_call" | custom-call | flops 1000 | bytes 1000 | tf_op jit(solution)/shard_map/pallas_call | solution.py:402
  4.8 2.0 %collective-permute-start.3 = (bf16[384,512]{1,0:T(8,128)(2,1)}, bf16[384,512]{1,0:T(8,128)(2,1)}, u32[]{:S(2)}, u32[]{:S(2)}) collective-permute-start(bf16[384,512]{1,0:T(8,128)(2,1)} %get-tuple-element.39.refs_5_), channel_id=1, source_target_pairs={{0,4},{1,29},{2,6},{3,31},{4,0},{5,9},{6,2},{7,11},{8,12},{9,5},{1... | collective-permute-start | bytes 1179656 | tf_op jit(solution)/shard_map/ppermute | solution.py:50
  6.8 3.9 %constant_dynamic-slice_fusion = (bf16[640,1280]{1,0:T(8,128)(2,1)}, bf16[640,1280]{1,0:T(8,128)(2,1)}) fusion(bf16[640,5120]{1,0:T(8,128)(2,1)} %param.15, s32[]{:T(128)S(6)} %select_n.80, s32[]{:T(128)S(6)} %select_n.79), kind=kLoop, calls=%fused_computation.7 | loop fusion | bytes 6553608 | tf_op jit(solution)/shard_map/dynamic_slice | solution.py:418
  10.6 1.6 %collective-permute-start.7 = (bf16[640,1280]{1,0:T(8,128)(2,1)}, bf16[640,1280]{1,0:T(8,128)(2,1)S(1)}, u32[]{:S(2)}, u32[]{:S(2)}) collective-permute-start(bf16[640,1280]{1,0:T(8,128)(2,1)} %get-tuple-element.72), channel_id=1, source_target_pairs={{0,2},{1,3},{2,0},{3,1},{4,6},{5,7},{6,4},{7,5},{8,10},{9,11},{10,... | collective-permute-start | bytes 4915208 | tf_op jit(solution)/shard_map/ppermute | solution.py:62
  12.2 2.2 %collective-permute-start.8 = (bf16[640,1280]{1,0:T(8,128)(2,1)}, bf16[640,1280]{1,0:T(8,128)(2,1)S(1)}, u32[]{:S(2)}, u32[]{:S(2)}) collective-permute-start(bf16[640,1280]{1,0:T(8,128)(2,1)} %get-tuple-element.71), channel_id=1, source_target_pairs={{0,34},{1,35},{2,32},{3,33},{4,38},{5,39},{6,36},{7,37},{8,42},{9,... | collective-permute-start | bytes 4915208 | tf_op jit(solution)/shard_map/ppermute | solution.py:58
  14.4 4.9 %collective-permute-start = (bf16[384,640]{1,0:T(8,128)(2,1)}, bf16[384,640]{1,0:T(8,128)(2,1)}, u32[]{:S(2)}, u32[]{:S(2)}) collective-permute-start(bf16[384,640]{1,0:T(8,128)(2,1)} %get-tuple-element.36), channel_id=1, source_target_pairs={{0,28},{1,5},{2,30},{3,7},{4,8},{5,1},{6,10},{7,3},{8,4},{9,13},{1... | collective-permute-start | bytes 1474568 | tf_op jit(solution)/shard_map/ppermute | solution.py:40
  21.3 4.7 %collective-permute-start.2 = (bf16[384,640]{1,0:T(8,128)(2,1)}, bf16[384,640]{1,0:T(8,128)(2,1)}, u32[]{:S(2)}, u32[]{:S(2)}) collective-permute-start(bf16[384,640]{1,0:T(8,128)(2,1)} %get-tuple-element.38), channel_id=1, source_target_pairs={{0,20},{1,13},{2,22},{3,15},{4,16},{5,25},{6,18},{7,27},{8,28},{9,... | collective-permute-start | bytes 1474568 | tf_op jit(solution)/shard_map/ppermute | solution.py:40
  26.0 1.5 %copy-done = bf16[3,256,1280]{2,1,0:T(8,128)(2,1)S(1)} copy-done((bf16[3,256,1280]{2,1,0:T(8,128)(2,1)S(1)}, bf16[3,256,1280]{2,1,0:T(8,128)(2,1)}, u32[]{:S(2)}) %copy-start) | copy-done | bytes 1966104
  29.4 2.1 %constant_dynamic-slice_fusion.2.refs_2_.refs_6_ = bf16[640,2560]{1,0:T(8,128)(2,1)S(1)} fusion(bf16[640,5120]{1,0:T(8,128)(2,1)} %param.15, s32[]{:T(128)S(6)} %select_n.76), kind=kLoop, calls=%fused_computation.9 | loop fusion | bytes 6553604 | tf_op jit(solution)/shard_map/dynamic_slice | solution.py:422
  31.6 2.6 %collective-permute-done.refs_0_.refs_6_ = bf16[384,640]{1,0:T(8,128)(2,1)} collective-permute-done((bf16[384,640]{1,0:T(8,128)(2,1)}, bf16[384,640]{1,0:T(8,128)(2,1)}, u32[]{:S(2)}, u32[]{:S(2)}) %collective-permute-start) | collective-permute-done | bytes 491552 | tf_op jit(solution)/shard_map/ppermute | solution.py:40
  34.2 8.2 %collective-permute-done.1.refs_1_.refs_7_ = bf16[384,640]{1,0:T(8,128)(2,1)} collective-permute-done((bf16[384,640]{1,0:T(8,128)(2,1)}, bf16[384,640]{1,0:T(8,128)(2,1)}, u32[]{:S(2)}, u32[]{:S(2)}) %collective-permute-start.1) | collective-permute-done | bytes 491552 | tf_op jit(solution)/shard_map/ppermute | solution.py:40
  42.4 10.3 %collective-permute-done.2.refs_2_.refs_8_ = bf16[384,640]{1,0:T(8,128)(2,1)} collective-permute-done((bf16[384,640]{1,0:T(8,128)(2,1)}, bf16[384,640]{1,0:T(8,128)(2,1)}, u32[]{:S(2)}, u32[]{:S(2)}) %collective-permute-start.2) | collective-permute-done | bytes 491552 | tf_op jit(solution)/shard_map/ppermute | solution.py:40
  53.7 2.0 %collective-permute-start.4 = (bf16[384,512]{1,0:T(8,128)(2,1)S(1)}, bf16[384,512]{1,0:T(8,128)(2,1)S(1)}, u32[]{:S(2)}, u32[]{:S(2)}) collective-permute-start(bf16[384,512]{1,0:T(8,128)(2,1)S(1)} %slice.9), channel_id=1, source_target_pairs={{0,4},{1,29},{2,6},{3,31},{4,0},{5,9},{6,2},{7,11},{8,12},{9,5},{1... | collective-permute-start | bytes 1179656 | tf_op jit(solution)/shard_map/ppermute | solution.py:50
  57.9 2.2 %collective-permute-start.6 = (bf16[384,512]{1,0:T(8,128)(2,1)S(1)}, bf16[384,512]{1,0:T(8,128)(2,1)S(1)}, u32[]{:S(2)}, u32[]{:S(2)}) collective-permute-start(bf16[384,512]{1,0:T(8,128)(2,1)S(1)} %slice.11), channel_id=1, source_target_pairs={{0,4},{1,29},{2,6},{3,31},{4,0},{5,9},{6,2},{7,11},{8,12},{9,5},{1... | collective-permute-start | bytes 1179656 | tf_op jit(solution)/shard_map/ppermute | solution.py:50
  60.2 7.5 %shard_map.132 = (f32[1920,128]{1,0:T(8,128)S(1)}, f32[1920,128]{1,0:T(8,128)S(1)}, f32[1920,128]{1,0:T(8,128)S(1)}) custom-call(bf16[384,640]{1,0:T(8,128)(2,1)} %collective-permute-done.refs_0_.refs_6_, bf16[384,640]{1,0:T(8,128)(2,1)} %collective-permute-done.1.refs_1_.refs_7_, bf16[384,640]{1,0:T(8,128)(2,1)} %collective-permute-done.2.refs_2_.refs_8_, ...), custom_call_target="tpu_custom_call" | custom-call | flops 8999999488 | bytes 1000 | tf_op jit(solution)/shard_map/pallas_call | solution.py:196
  67.7 2.2 %collective-permute-done.6.refs_7_ = bf16[384,512]{1,0:T(8,128)(2,1)S(1)} collective-permute-done((bf16[384,512]{1,0:T(8,128)(2,1)S(1)}, bf16[384,512]{1,0:T(8,128)(2,1)S(1)}, u32[]{:S(2)}, u32[]{:S(2)}) %collective-permute-start.6) | collective-permute-done | bytes 393248 | tf_op jit(solution)/shard_map/ppermute | solution.py:50
  70.0 6.3 %shard_map.133 = (bf16[384,128]{1,0:T(8,128)(2,1)S(1)}, bf16[384,128]{1,0:T(8,128)(2,1)S(1)}, bf16[384,128]{1,0:T(8,128)(2,1)S(1)}, bf16[384,256]{1,0:T(8,128)(2,1)S(1)}) custom-call(bf16[384,640]{1,0:T(8,128)(2,1)} %collective-permute-done.refs_0_.refs_6_, bf16[384,640]{1,0:T(8,128)(2,1)} %collective-permute-done.1.refs_1_.refs_7_, ...), custom_call_target="tpu_custom_call" | custom-call | flops 1000 | bytes 1000 | tf_op jit(solution)/shard_map/pallas_call | solution.py:196
  77.1 1.8 %collective-permute-start.9 = (bf16[384,128]{1,0:T(8,128)(2,1)S(1)}, bf16[384,128]{1,0:T(8,128)(2,1)S(1)}, u32[]{:S(2)}, u32[]{:S(2)}) collective-permute-start(bf16[384,128]{1,0:T(8,128)(2,1)S(1)} %get-tuple-element.54), channel_id=1, source_target_pairs={{28,0},{5,1},{30,2},{7,3},{8,4},{1,5},{10,6},{3,7},{4,8},{13,9},{6... | collective-permute-start | bytes 294920 | tf_op jit(solution)/shard_map/ppermute | solution.py:40
  78.8 1.5 %collective-permute-start.11 = (bf16[384,128]{1,0:T(8,128)(2,1)S(1)}, bf16[384,128]{1,0:T(8,128)(2,1)S(1)}, u32[]{:S(2)}, u32[]{:S(2)}) collective-permute-start(bf16[384,128]{1,0:T(8,128)(2,1)S(1)} %get-tuple-element.55), channel_id=1, source_target_pairs={{8,0},{25,1},{10,2},{27,3},{28,4},{13,5},{30,6},{15,7},{16,8},{1,9... | collective-permute-start | bytes 294920 | tf_op jit(solution)/shard_map/ppermute | solution.py:40
  80.3 2.4 %collective-permute-start.13 = (bf16[384,128]{1,0:T(8,128)(2,1)S(1)}, bf16[384,128]{1,0:T(8,128)(2,1)S(1)}, u32[]{:S(2)}, u32[]{:S(2)}) collective-permute-start(bf16[384,128]{1,0:T(8,128)(2,1)S(1)} %get-tuple-element.56), channel_id=1, source_target_pairs={{20,0},{13,1},{22,2},{15,3},{16,4},{25,5},{18,6},{27,7},{28,8},{21... | collective-permute-start | bytes 294920 | tf_op jit(solution)/shard_map/ppermute | solution.py:40
  82.9 1.3 %collective-permute-start.10 = (bf16[384,128]{1,0:T(8,128)(2,1)S(1)}, bf16[384,128]{1,0:T(8,128)(2,1)S(1)}, u32[]{:S(2)}, u32[]{:S(2)}) collective-permute-start(bf16[384,128]{1,0:T(8,128)(2,1)S(1)} %collective-permute-done.9.refs_3_), channel_id=1, source_target_pairs={{0,2},{1,3},{2,0},{3,1},{4,6},{5,7},{6,4},{7,5},{8,10},{9,11},{10,... | collective-permute-start | bytes 294920 | tf_op jit(solution)/shard_map/ppermute | solution.py:62
  84.5 1.3 %collective-permute-start.12 = (bf16[384,128]{1,0:T(8,128)(2,1)S(1)}, bf16[384,128]{1,0:T(8,128)(2,1)S(1)}, u32[]{:S(2)}, u32[]{:S(2)}) collective-permute-start(bf16[384,128]{1,0:T(8,128)(2,1)S(1)} %collective-permute-done.11.refs_4_), channel_id=1, source_target_pairs={{0,2},{1,3},{2,0},{3,1},{4,6},{5,7},{6,4},{7,5},{8,10},{9,11},{10,... | collective-permute-start | bytes 294920 | tf_op jit(solution)/shard_map/ppermute | solution.py:62
  85.8 2.1 %collective-permute-done.13.refs_5_ = bf16[384,128]{1,0:T(8,128)(2,1)S(1)} collective-permute-done((bf16[384,128]{1,0:T(8,128)(2,1)S(1)}, bf16[384,128]{1,0:T(8,128)(2,1)S(1)}, u32[]{:S(2)}, u32[]{:S(2)}) %collective-permute-start.13) | collective-permute-done | bytes 98336 | tf_op jit(solution)/shard_map/ppermute | solution.py:40
  87.9 1.3 %collective-permute-start.14 = (bf16[384,128]{1,0:T(8,128)(2,1)S(1)}, bf16[384,128]{1,0:T(8,128)(2,1)S(1)}, u32[]{:S(2)}, u32[]{:S(2)}) collective-permute-start(bf16[384,128]{1,0:T(8,128)(2,1)S(1)} %collective-permute-done.13.refs_5_), channel_id=1, source_target_pairs={{0,2},{1,3},{2,0},{3,1},{4,6},{5,7},{6,4},{7,5},{8,10},{9,11},{10,... | collective-permute-start | bytes 294920 | tf_op jit(solution)/shard_map/ppermute | solution.py:62
  89.3 1.7 %shard_map.136.refs_5_ = f32[384,1280]{1,0:T(8,128)S(1)} custom-call(s32[7]{0:T(128)S(1)} %copy-done.7, bf16[384,256]{1,0:T(8,128)(2,1)S(1)} %get-tuple-element.58.refs_1_, bf16[640,2560]{1,0:T(8,128)(2,1)S(1)} %constant_dynamic-slice_fusion.2.refs_2_.refs_6_, bf16[384,128]{1,0:T(8,128)(2,1)S(1)} %collective-permute-done.9.refs_3_, ...), custom_call_target="tpu_custom_call" | custom-call | flops 1000 | bytes 1000 | tf_op jit(solution)/shard_map/pallas_call | solution.py:270
  91.0 1.5 %collective-permute-done.14.refs_3_ = bf16[384,128]{1,0:T(8,128)(2,1)S(1)} collective-permute-done((bf16[384,128]{1,0:T(8,128)(2,1)S(1)}, bf16[384,128]{1,0:T(8,128)(2,1)S(1)}, u32[]{:S(2)}, u32[]{:S(2)}) %collective-permute-start.14) | collective-permute-done | bytes 98336 | tf_op jit(solution)/shard_map/ppermute | solution.py:62
  93.9 1.7 %shard_map.134.refs_5_ = f32[384,1280]{1,0:T(8,128)S(1)} custom-call(s32[7]{0:T(128)S(1)} %copy-done.7, bf16[384,256]{1,0:T(8,128)(2,1)S(1)} %get-tuple-element.58.refs_1_, bf16[640,2560]{1,0:T(8,128)(2,1)S(1)} %constant_dynamic-slice_fusion.2.refs_2_.refs_6_, bf16[384,128]{1,0:T(8,128)(2,1)S(1)} %collective-permute-done.9.refs_3_, ...), custom_call_target="tpu_custom_call" | custom-call | flops 1000 | bytes 1000 | tf_op jit(solution)/shard_map/pallas_call | solution.py:270
  96.9 1.9 %shard_map.138 = (bf16[384,1280]{1,0:T(8,128)(2,1)}, bf16[80,512]{1,0:T(8,128)(2,1)S(1)}) custom-call(f32[384,1280]{1,0:T(8,128)S(1)} %shard_map.135.acc_ref, bf16[384,1280]{1,0:T(8,128)(2,1)S(1)} %collective-permute-done.16.other_ref, bf16[384,1280]{1,0:T(8,128)(2,1)S(1)} %copy-done.1, f32[8,1280]{1,0:T(8,128)S(1)} %get-tuple-element.61.gate_ref, ...), custom_call_target="tpu_custom_call" | custom-call | flops 1000 | bytes 1000 | tf_op jit(solution)/shard_map/pallas_call | solution.py:452
  100.7 3.2 %collective-permute-done.18.m2 = bf16[80,512]{1,0:T(8,128)(2,1)S(1)} collective-permute-done((bf16[80,512]{1,0:T(8,128)(2,1)S(1)}, bf16[80,512]{1,0:T(8,128)(2,1)S(1)}, u32[]{:S(2)}, u32[]{:S(2)}) %collective-permute-start.18) | collective-permute-done | bytes 81952 | tf_op jit(solution)/shard_map/ppermute | solution.py:62
  103.9 1.5 %collective-permute-done.19.m3 = bf16[80,512]{1,0:T(8,128)(2,1)S(1)} collective-permute-done((bf16[80,512]{1,0:T(8,128)(2,1)S(1)}, bf16[80,512]{1,0:T(8,128)(2,1)S(1)}, u32[]{:S(2)}, u32[]{:S(2)}) %collective-permute-start.19) | collective-permute-done | bytes 81952 | tf_op jit(solution)/shard_map/ppermute | solution.py:62
  106.2 5.1 %collective-permute-start.20 = (bf16[64,384]{1,0:T(8,128)(2,1)S(1)}, bf16[64,384]{1,0:T(8,128)(2,1)S(1)}, u32[]{:S(2)}, u32[]{:S(2)}) collective-permute-start(bf16[64,384]{1,0:T(8,128)(2,1)S(1)} %get-tuple-element.68), channel_id=1, source_target_pairs={{4,0},{8,4},{12,8},{16,12},{20,16},{24,20},{28,24},{32,28},{36,32}... | collective-permute-start | bytes 147464 | tf_op jit(solution)/shard_map/ppermute | solution.py:68
  111.4 1.8 %collective-permute-done.20 = bf16[64,384]{1,0:T(8,128)(2,1)S(1)} collective-permute-done((bf16[64,384]{1,0:T(8,128)(2,1)S(1)}, bf16[64,384]{1,0:T(8,128)(2,1)S(1)}, u32[]{:S(2)}, u32[]{:S(2)}) %collective-permute-start.20) | collective-permute-done | bytes 49184 | tf_op jit(solution)/shard_map/ppermute | solution.py:68
  (52 shorter events, 13.0 us)
Async XLA Ops:
  4.8 16.6 %collective-permute-start.3 = (bf16[384,512]{1,0:T(8,128)(2,1)}, bf16[384,512]{1,0:T(8,128)(2,1)}, u32[]{:S(2)}, u32[]{:S(2)}) collective-permute-start(bf16[384,512]{1,0:T(8,128)(2,1)} %get-tuple-element.39.refs_5_), channel_id=1, source_target_pairs={{0,4},{1,29},{2,6},{3,31},{4,0},{5,9},{6,2},{7,11},{8,12},{9,5},{1... | collective-permute-start | bytes 1179656 | tf_op jit(solution)/shard_map/ppermute | solution.py:50
  6.8 13.2 %copy-start.10 = (s32[129]{0:T(256)S(1)}, s32[129]{0:T(256)}, u32[]{:S(2)}) copy-start(s32[129]{0:T(256)} %param.21) | copy-start | bytes 1552
  6.8 19.2 %copy-start.5 = (bf16[1280,64]{0,1:T(8,128)(2,1)S(1)}, bf16[1280,64]{0,1:T(8,128)(2,1)}, u32[]{:S(2)}) copy-start(bf16[1280,64]{0,1:T(8,128)(2,1)} %param.17) | copy-start | bytes 491524
  10.6 57.1 %collective-permute-start.7 = (bf16[640,1280]{1,0:T(8,128)(2,1)}, bf16[640,1280]{1,0:T(8,128)(2,1)S(1)}, u32[]{:S(2)}, u32[]{:S(2)}) collective-permute-start(bf16[640,1280]{1,0:T(8,128)(2,1)} %get-tuple-element.72), channel_id=1, source_target_pairs={{0,2},{1,3},{2,0},{3,1},{4,6},{5,7},{6,4},{7,5},{8,10},{9,11},{10,... | collective-permute-start | bytes 4915208 | tf_op jit(solution)/shard_map/ppermute | solution.py:62
  12.2 55.5 %collective-permute-start.8 = (bf16[640,1280]{1,0:T(8,128)(2,1)}, bf16[640,1280]{1,0:T(8,128)(2,1)S(1)}, u32[]{:S(2)}, u32[]{:S(2)}) collective-permute-start(bf16[640,1280]{1,0:T(8,128)(2,1)} %get-tuple-element.71), channel_id=1, source_target_pairs={{0,34},{1,35},{2,32},{3,33},{4,38},{5,39},{6,36},{7,37},{8,42},{9,... | collective-permute-start | bytes 4915208 | tf_op jit(solution)/shard_map/ppermute | solution.py:58
  14.4 19.8 %collective-permute-start = (bf16[384,640]{1,0:T(8,128)(2,1)}, bf16[384,640]{1,0:T(8,128)(2,1)}, u32[]{:S(2)}, u32[]{:S(2)}) collective-permute-start(bf16[384,640]{1,0:T(8,128)(2,1)} %get-tuple-element.36), channel_id=1, source_target_pairs={{0,28},{1,5},{2,30},{3,7},{4,8},{5,1},{6,10},{7,3},{8,4},{9,13},{1... | collective-permute-start | bytes 1474568 | tf_op jit(solution)/shard_map/ppermute | solution.py:40
  19.3 23.1 %collective-permute-start.1 = (bf16[384,640]{1,0:T(8,128)(2,1)}, bf16[384,640]{1,0:T(8,128)(2,1)}, u32[]{:S(2)}, u32[]{:S(2)}) collective-permute-start(bf16[384,640]{1,0:T(8,128)(2,1)} %get-tuple-element.37), channel_id=1, source_target_pairs={{0,8},{1,25},{2,10},{3,27},{4,28},{5,13},{6,30},{7,15},{8,16},{9,1... | collective-permute-start | bytes 1474568 | tf_op jit(solution)/shard_map/ppermute | solution.py:40
  21.3 31.3 %collective-permute-start.2 = (bf16[384,640]{1,0:T(8,128)(2,1)}, bf16[384,640]{1,0:T(8,128)(2,1)}, u32[]{:S(2)}, u32[]{:S(2)}) collective-permute-start(bf16[384,640]{1,0:T(8,128)(2,1)} %get-tuple-element.38), channel_id=1, source_target_pairs={{0,20},{1,13},{2,22},{3,15},{4,16},{5,25},{6,18},{7,27},{8,28},{9,... | collective-permute-start | bytes 1474568 | tf_op jit(solution)/shard_map/ppermute | solution.py:40
  26.0 1.5 %copy-start = (bf16[3,256,1280]{2,1,0:T(8,128)(2,1)S(1)}, bf16[3,256,1280]{2,1,0:T(8,128)(2,1)}, u32[]{:S(2)}) copy-start(bf16[3,256,1280]{2,1,0:T(8,128)(2,1)} %time_ref.1) | copy-start | bytes 5898244
  28.1 0.7 copy-start.3
  31.6 28.6 %copy-start.2 = (bf16[384,256]{1,0:T(8,128)(2,1)S(1)}, bf16[384,256]{1,0:T(8,128)(2,1)}, u32[]{:S(2)}) copy-start(bf16[384,256]{1,0:T(8,128)(2,1)} %get-tuple-element.46.refs_3_.refs_4_) | copy-start | bytes 589828
  31.6 28.6 %copy-start.8 = (bf16[384,512]{1,0:T(8,128)(2,1)S(1)}, bf16[384,512]{1,0:T(8,128)(2,1)}, u32[]{:S(2)}) copy-start(bf16[384,512]{1,0:T(8,128)(2,1)} %get-tuple-element.39.refs_5_) | copy-start | bytes 1179652
  53.7 14.0 %collective-permute-start.4 = (bf16[384,512]{1,0:T(8,128)(2,1)S(1)}, bf16[384,512]{1,0:T(8,128)(2,1)S(1)}, u32[]{:S(2)}, u32[]{:S(2)}) collective-permute-start(bf16[384,512]{1,0:T(8,128)(2,1)S(1)} %slice.9), channel_id=1, source_target_pairs={{0,4},{1,29},{2,6},{3,31},{4,0},{5,9},{6,2},{7,11},{8,12},{9,5},{1... | collective-permute-start | bytes 1179656 | tf_op jit(solution)/shard_map/ppermute | solution.py:50
  56.8 11.0 %collective-permute-start.5 = (bf16[384,512]{1,0:T(8,128)(2,1)S(1)}, bf16[384,512]{1,0:T(8,128)(2,1)S(1)}, u32[]{:S(2)}, u32[]{:S(2)}) collective-permute-start(bf16[384,512]{1,0:T(8,128)(2,1)S(1)} %slice.10), channel_id=1, source_target_pairs={{0,4},{1,29},{2,6},{3,31},{4,0},{5,9},{6,2},{7,11},{8,12},{9,5},{1... | collective-permute-start | bytes 1179656 | tf_op jit(solution)/shard_map/ppermute | solution.py:50
  57.9 12.0 %collective-permute-start.6 = (bf16[384,512]{1,0:T(8,128)(2,1)S(1)}, bf16[384,512]{1,0:T(8,128)(2,1)S(1)}, u32[]{:S(2)}, u32[]{:S(2)}) collective-permute-start(bf16[384,512]{1,0:T(8,128)(2,1)S(1)} %slice.11), channel_id=1, source_target_pairs={{0,4},{1,29},{2,6},{3,31},{4,0},{5,9},{6,2},{7,11},{8,12},{9,5},{1... | collective-permute-start | bytes 1179656 | tf_op jit(solution)/shard_map/ppermute | solution.py:50
  67.7 21.6 %copy-start.7 = (s32[7]{0:T(128)S(1)}, s32[7]{0:T(128)}, u32[]{:S(2)}) copy-start(s32[7]{0:T(128)} %stack.31.head_ref.refs_0_) | copy-start | bytes 88
  76.3 13.0 %collective-permute-start.15 = (bf16[384,256]{1,0:T(8,128)(2,1)S(1)}, bf16[384,256]{1,0:T(8,128)(2,1)S(1)}, u32[]{:S(2)}, u32[]{:S(2)}) collective-permute-start(bf16[384,256]{1,0:T(8,128)(2,1)S(1)} %get-tuple-element.58.refs_1_), channel_id=1, source_target_pairs={{0,2},{1,3},{2,0},{3,1},{4,6},{5,7},{6,4},{7,5},{8,10},{9,11},{10,... | collective-permute-start | bytes 589832 | tf_op jit(solution)/shard_map/ppermute | solution.py:62
  77.1 5.8 %collective-permute-start.9 = (bf16[384,128]{1,0:T(8,128)(2,1)S(1)}, bf16[384,128]{1,0:T(8,128)(2,1)S(1)}, u32[]{:S(2)}, u32[]{:S(2)}) collective-permute-start(bf16[384,128]{1,0:T(8,128)(2,1)S(1)} %get-tuple-element.54), channel_id=1, source_target_pairs={{28,0},{5,1},{30,2},{7,3},{8,4},{1,5},{10,6},{3,7},{4,8},{13,9},{6... | collective-permute-start | bytes 294920 | tf_op jit(solution)/shard_map/ppermute | solution.py:40
  78.8 5.6 %collective-permute-start.11 = (bf16[384,128]{1,0:T(8,128)(2,1)S(1)}, bf16[384,128]{1,0:T(8,128)(2,1)S(1)}, u32[]{:S(2)}, u32[]{:S(2)}) collective-permute-start(bf16[384,128]{1,0:T(8,128)(2,1)S(1)} %get-tuple-element.55), channel_id=1, source_target_pairs={{8,0},{25,1},{10,2},{27,3},{28,4},{13,5},{30,6},{15,7},{16,8},{1,9... | collective-permute-start | bytes 294920 | tf_op jit(solution)/shard_map/ppermute | solution.py:40
  80.3 7.6 %collective-permute-start.13 = (bf16[384,128]{1,0:T(8,128)(2,1)S(1)}, bf16[384,128]{1,0:T(8,128)(2,1)S(1)}, u32[]{:S(2)}, u32[]{:S(2)}) collective-permute-start(bf16[384,128]{1,0:T(8,128)(2,1)S(1)} %get-tuple-element.56), channel_id=1, source_target_pairs={{20,0},{13,1},{22,2},{15,3},{16,4},{25,5},{18,6},{27,7},{28,8},{21... | collective-permute-start | bytes 294920 | tf_op jit(solution)/shard_map/ppermute | solution.py:40
  82.9 8.1 %collective-permute-start.10 = (bf16[384,128]{1,0:T(8,128)(2,1)S(1)}, bf16[384,128]{1,0:T(8,128)(2,1)S(1)}, u32[]{:S(2)}, u32[]{:S(2)}) collective-permute-start(bf16[384,128]{1,0:T(8,128)(2,1)S(1)} %collective-permute-done.9.refs_3_), channel_id=1, source_target_pairs={{0,2},{1,3},{2,0},{3,1},{4,6},{5,7},{6,4},{7,5},{8,10},{9,11},{10,... | collective-permute-start | bytes 294920 | tf_op jit(solution)/shard_map/ppermute | solution.py:62
  84.5 6.6 %collective-permute-start.12 = (bf16[384,128]{1,0:T(8,128)(2,1)S(1)}, bf16[384,128]{1,0:T(8,128)(2,1)S(1)}, u32[]{:S(2)}, u32[]{:S(2)}) collective-permute-start(bf16[384,128]{1,0:T(8,128)(2,1)S(1)} %collective-permute-done.11.refs_4_), channel_id=1, source_target_pairs={{0,2},{1,3},{2,0},{3,1},{4,6},{5,7},{6,4},{7,5},{8,10},{9,11},{10,... | collective-permute-start | bytes 294920 | tf_op jit(solution)/shard_map/ppermute | solution.py:62
  87.9 4.6 %collective-permute-start.14 = (bf16[384,128]{1,0:T(8,128)(2,1)S(1)}, bf16[384,128]{1,0:T(8,128)(2,1)S(1)}, u32[]{:S(2)}, u32[]{:S(2)}) collective-permute-start(bf16[384,128]{1,0:T(8,128)(2,1)S(1)} %collective-permute-done.13.refs_5_), channel_id=1, source_target_pairs={{0,2},{1,3},{2,0},{3,1},{4,6},{5,7},{6,4},{7,5},{8,10},{9,11},{10,... | collective-permute-start | bytes 294920 | tf_op jit(solution)/shard_map/ppermute | solution.py:62
  93.8 3.1 %collective-permute-start.16 = (bf16[384,1280]{1,0:T(8,128)(2,1)S(1)}, bf16[384,1280]{1,0:T(8,128)(2,1)S(1)}, u32[]{:S(2)}, u32[]{:S(2)}) collective-permute-start(bf16[384,1280]{1,0:T(8,128)(2,1)S(1)} %shard_map.137), channel_id=1, source_target_pairs={{0,1},{1,0},{2,3},{3,2},{4,5},{5,4},{6,7},{7,6},{8,9},{9,8},{10,11... | collective-permute-start | bytes 2949128 | tf_op jit(solution)/shard_map/ppermute | solution.py:62
  95.6 1.3 %copy-start.1 = (bf16[384,1280]{1,0:T(8,128)(2,1)S(1)}, bf16[384,1280]{1,0:T(8,128)(2,1)}, u32[]{:S(2)}) copy-start(bf16[384,1280]{1,0:T(8,128)(2,1)} %in_ref.1) | copy-start | bytes 2949124
  95.6 1.3 %copy-start.4 = (bf16[128,1280]{1,0:T(8,128)(2,1)S(1)}, bf16[128,1280]{1,0:T(8,128)(2,1)}, u32[]{:S(2)}) copy-start(bf16[128,1280]{1,0:T(8,128)(2,1)} %copy-done.3) | copy-start | bytes 983044
  96.8 8.5 %copy-start.6 = (f32[384,64]{0,1:T(8,128)S(1)}, f32[384,64]{0,1:T(8,128)}, u32[]{:S(2)}) copy-start(f32[384,64]{0,1:T(8,128)} %param.18) | copy-start | bytes 294916
  96.9 16.3 %copy-start.9 = (f32[384,64]{0,1:T(8,128)S(1)}, f32[384,64]{0,1:T(8,128)}, u32[]{:S(2)}) copy-start(f32[384,64]{0,1:T(8,128)} %param.19) | copy-start | bytes 294916
  98.8 1.9 %collective-permute-start.17 = (bf16[80,512]{1,0:T(8,128)(2,1)S(1)}, bf16[80,512]{1,0:T(8,128)(2,1)S(1)}, u32[]{:S(2)}, u32[]{:S(2)}) collective-permute-start(bf16[80,512]{1,0:T(8,128)(2,1)S(1)} %get-tuple-element.65.m0), channel_id=1, source_target_pairs={{0,1},{1,0},{2,3},{3,2},{4,5},{5,4},{6,7},{7,6},{8,9},{9,8},{10,11... | collective-permute-start | bytes 245768 | tf_op jit(solution)/shard_map/ppermute | solution.py:62
  99.3 4.6 %collective-permute-start.18 = (bf16[80,512]{1,0:T(8,128)(2,1)S(1)}, bf16[80,512]{1,0:T(8,128)(2,1)S(1)}, u32[]{:S(2)}, u32[]{:S(2)}) collective-permute-start(bf16[80,512]{1,0:T(8,128)(2,1)S(1)} %get-tuple-element.65.m0), channel_id=1, source_target_pairs={{0,2},{1,3},{2,0},{3,1},{4,6},{5,7},{6,4},{7,5},{8,10},{9,11},{10,... | collective-permute-start | bytes 245768 | tf_op jit(solution)/shard_map/ppermute | solution.py:62
  100.7 4.7 %collective-permute-start.19 = (bf16[80,512]{1,0:T(8,128)(2,1)S(1)}, bf16[80,512]{1,0:T(8,128)(2,1)S(1)}, u32[]{:S(2)}, u32[]{:S(2)}) collective-permute-start(bf16[80,512]{1,0:T(8,128)(2,1)S(1)} %get-tuple-element.65.m0), channel_id=1, source_target_pairs={{0,3},{1,2},{2,1},{3,0},{4,7},{5,6},{6,5},{7,4},{8,11},{9,10},{10,... | collective-permute-start | bytes 245768 | tf_op jit(solution)/shard_map/ppermute | solution.py:62
  106.2 7.0 %collective-permute-start.20 = (bf16[64,384]{1,0:T(8,128)(2,1)S(1)}, bf16[64,384]{1,0:T(8,128)(2,1)S(1)}, u32[]{:S(2)}, u32[]{:S(2)}) collective-permute-start(bf16[64,384]{1,0:T(8,128)(2,1)S(1)} %get-tuple-element.68), channel_id=1, source_target_pairs={{4,0},{8,4},{12,8},{16,12},{20,16},{24,20},{28,24},{32,28},{36,32}... | collective-permute-start | bytes 147464 | tf_op jit(solution)/shard_map/ppermute | solution.py:68

commit v3 on v2

--- a/solution.py
+++ b/solution.py
@@ -16,6 +16,7 @@
 BF16 = jnp.bfloat16
 COLUMN_BLOCK = 256
 SPREAD_HEADS = 4
+STAT_ROWS = 32
 SMALL = pl.CostEstimate(flops=1000, bytes_accessed=1000, transcendentals=0)
 ATTEND_COST = pl.CostEstimate(flops=9_000_000_000, bytes_accessed=1000, transcendentals=0)
 EXP_SCALE = HD ** (-0.5) / math.log(2.0)
@@ -116,53 +117,116 @@
         copy.wait()
         for at, ref in targets:
             ref[:, slot * HD : (slot + 1) * HD] = source[:, lanes(at)]
-            ref[:, (slot + 2) * HD : (slot + 3) * HD] = source[:, common]
+        kv_ref[:, (slot + 2) * HD : (slot + 3) * HD] = source[:, common]
     copies[2].wait()
     for at, ref in targets[:3]:
-        ref[:, 4 * HD :] = q_ref[:, lanes(at)]
+        ref[:, 2 * HD : 3 * HD] = q_ref[:, lanes(at)]
+        ref[:, 3 * HD :] = q_ref[:, common]
     q_out_ref[:, 0:HD] = q_ref[:, lanes(0)]
     q_out_ref[:, HD:] = q_ref[:, common]
 
 
-def attend_kernel(query_lanes, block_count, first, last, *refs):
+def softmax_block(query, keys, values, old=None):
+    scores = [dot_t(query, key) for key in keys]
+    peak = max_of([jnp.max(s, axis=1, keepdims=True) for s in scores])
+    if old is not None:
+        old_acc, old_peak, old_total = old
+        peak = jnp.maximum(peak, old_peak)
+    acc = None
+    total = None
+    for s, value in zip(scores, values):
+        weights = jnp.exp2((s - peak) * EXP_SCALE)
+        part = sum_lanes(weights)
+        total = part if total is None else total + part
+        mixed = dot(weights.astype(BF16), value)
+        acc = mixed if acc is None else acc + mixed
+    if old is not None:
+        shrink = jnp.exp2((old_peak - peak) * EXP_SCALE)
+        acc = acc + old_acc * shrink
+        total = total + old_total * shrink
+    return acc, peak, total
+
+
+def attend_kernel(operand_count, last, *refs):
     refs = list(refs)
-    q_refs = [refs.pop(0) for _ in query_lanes]
-    blocks = [refs.pop(0) for _ in range(block_count)]
-    if not first:
-        acc_in, peak_in, total_in = refs.pop(0), refs.pop(0), refs.pop(0)
-    row_count = q_refs[0].shape[0]
-    for at, (q_ref, (q_low, shared)) in enumerate(zip(q_refs, query_lanes)):
-        key_low = 2 * HD if shared else 0
-        query = q_ref[:, q_low : q_low + HD]
-        scores = [dot_t(query, ref[:, key_low : key_low + HD]) for ref in blocks]
-        peak = max_of([jnp.max(s, axis=1, keepdims=True) for s in scores])
+    far_q_ref, own_q_ref = refs.pop(0), refs.pop(0)
+    row_count = own_q_ref.shape[0]
+    far_count = far_q_ref.shape[0] // row_count
+    queries = [far_q_ref[at * row_count : (at + 1) * row_count, 0:HD] for at in range(far_count)]
+    queries.append(own_q_ref[:, 0:HD])
+    blocks = []
+    for _ in range(operand_count):
+        ref = refs.pop(0)
+        blocks += [(ref, low) for low in range(0, ref.shape[0], row_count)]
+    states = [refs.pop(0) for _ in range(3)] if last else None
+    keys = [ref[low : low + row_count, 0:HD] for ref, low in blocks]
+    values = [ref[low : low + row_count, HD : 2 * HD] for ref, low in blocks]
+    for at, query in enumerate(queries):
         rows = slice(at * row_count, (at + 1) * row_count)
-        if not first:
-            old_peak = peak_in[rows, 0:1]
-            peak = jnp.maximum(peak, old_peak)
-        acc = None
-        total = None
-        for s, ref in zip(scores, blocks):
-            weights = jnp.exp2((s - peak) * EXP_SCALE)
-            part = sum_lanes(weights)
-            total = part if total is None else total + part
-            mixed = dot(weights.astype(BF16), ref[:, key_low + HD : key_low + 2 * HD])
-            acc = mixed if acc is None else acc + mixed
-        if not first:
-            shrink = jnp.exp2((old_peak - peak) * EXP_SCALE)
-            acc = acc + acc_in[rows, :] * shrink
-            total = total + total_in[rows, :] * shrink
+        old = (states[0][rows, :], states[1][rows, 0:1], states[2][rows, :]) if last else None
+        acc, peak, total = softmax_block(query, keys, values, old)
         if last:
-            out = (acc / jnp.sum(total, axis=1, keepdims=True)).astype(BF16)
-            if at < PART // 2 - 1:
-                refs[at][...] = out
-            else:
-                low = (at - PART // 2 + 1) * HD
-                refs[-1][:, low : low + HD] = out
+            refs[at][...] = (acc / jnp.sum(total, axis=1, keepdims=True)).astype(BF16)
         else:
             refs[0][rows, :] = acc
             refs[1][rows, :] = jnp.broadcast_to(peak, acc.shape)
             refs[2][rows, :] = total
+
+
+def gather_kernel(x1_ref, x2_ref, x3_ref, kv_ref, q_ref):
+    row_count = x1_ref.shape[0]
+    for at, ref in enumerate((x1_ref, x2_ref, x3_ref)):
+        rows = slice(at * row_count, (at + 1) * row_count)
+        kv_ref[rows, :] = ref[:, 0 : 2 * HD]
+        q_ref[rows, :] = ref[:, 2 * HD :]
+
+
+def common_kernel(own_q_ref, far_q_ref, kv0, kv1, *refs):
+    row_count = own_q_ref.shape[0]
+    keys = [ref[:, 2 * HD : 3 * HD] for ref in (kv0, kv1)]
+    values = [ref[:, 3 * HD :] for ref in (kv0, kv1)]
+    queries = [far_q_ref[at * row_count : (at + 1) * row_count, HD:] for at in range(3)]
+    for at, query in enumerate((*queries, own_q_ref[:, HD:])):
+        acc, peak, total = softmax_block(query, keys, values)
+        total = jnp.sum(total, axis=1, keepdims=True)
+        if at == 3:
+            refs[3][...] = acc
+            refs[4][...] = jnp.broadcast_to(peak, acc.shape)
+            refs[5][...] = jnp.broadcast_to(total, acc.shape)
+            continue
+        refs[at][0:row_count, :] = (acc / total).astype(BF16)
+        rows = []
+        for value in (peak, total):
+            for low in range(0, row_count, HD):
+                block = jnp.broadcast_to(value[low : low + HD], (HD, HD))
+                rows += [x.astype(F32) for x in split3(jnp.transpose(block)[0:1])]
+        rows += [jnp.zeros((STAT_ROWS - len(rows), HD), F32)]
+        refs[at][row_count:, :] = jnp.concatenate(rows, axis=0).astype(BF16)
+
+
+def merge_kernel(m1, m2, m3, acc_ref, peak_ref, total_ref, own_ref, out_ref):
+    out_ref[:, 0:HD] = own_ref[...]
+    row_count = acc_ref.shape[0]
+    stats = [ref[row_count:, :].astype(F32) for ref in (m1, m2, m3)]
+
+    def column(stat, at):
+        row = stat[3 * at : 3 * at + 1] + stat[3 * at + 1 : 3 * at + 2] + stat[3 * at + 2 : 3 * at + 3]
+        return jnp.transpose(jnp.broadcast_to(row, (HD, HD)))
+
+    count = row_count // HD
+    for at in range(count):
+        rows = slice(at * HD, (at + 1) * HD)
+        peaks = [peak_ref[rows, :]] + [column(stat, at) for stat in stats]
+        totals = [total_ref[rows, :]] + [column(stat, count + at) for stat in stats]
+        top = max_of(peaks)
+        shares = [jnp.exp2((peak - top) * EXP_SCALE) for peak in peaks]
+        numerator = acc_ref[rows, :] * shares[0]
+        denominator = totals[0] * shares[0]
+        for ref, share, total in zip((m1, m2, m3), shares[1:], totals[1:]):
+            weight = share * total
+            numerator = numerator + ref[rows, :].astype(F32) * weight
+            denominator = denominator + weight
+        out_ref[rows, HD:] = (numerator / denominator).astype(BF16)
 
 
 def max_of(values):
@@ -179,19 +243,17 @@
     return result
 
 
-def attend(queries, query_lanes, blocks, state, cost):
-    row_count = queries[0].shape[0]
-    operands = list(queries) + list(blocks)
-    first = state is None
-    if first:
-        out_shape = [jax.ShapeDtypeStruct((row_count * len(queries), HD), F32)] * 3
+def attend(far_queries, own_queries, blocks, state, cost):
+    row_count = own_queries.shape[0]
+    query_rows = row_count + far_queries.shape[0]
+    operands = [far_queries, own_queries, *blocks] + ([] if state is None else list(state))
+    if state is not None:
+        out_shape = [jax.ShapeDtypeStruct((row_count, HD), BF16)] * (query_rows // row_count)
     else:
-        operands += list(state)
-        out_shape = [jax.ShapeDtypeStruct((row_count, HD), BF16)] * 3
-        out_shape += [jax.ShapeDtypeStruct((row_count, 2 * HD), BF16)]
+        out_shape = [jax.ShapeDtypeStruct((query_rows, HD), F32)] * 3
 
     def body(*refs):
-        attend_kernel(query_lanes, len(blocks), first, not first, *refs)
+        attend_kernel(len(blocks), state is not None, *refs)
 
     return pl.pallas_call(body, out_shape=out_shape, compiler_params=params(), cost_estimate=cost)(*operands)
 
@@ -396,7 +458,7 @@
         ]
     ).astype(jnp.int32)
     depth = out_weight.shape[0]
-    kv_width, packed_width = 4 * HD, 5 * HD
+    kv_width, packed_width = 2 * HD, 4 * HD
     in_smem = pl.BlockSpec(memory_space=pltpu.SMEM)
     in_hbm = pl.BlockSpec(memory_space=pltpu.HBM)
     x1, x2, x3, own_kv, own_q = pl.pallas_call(
@@ -405,7 +467,7 @@
         out_specs=[pl.BlockSpec(memory_space=pltpu.VMEM)] * 5,
         scratch_shapes=[pltpu.VMEM(queries.shape, BF16)] * 3 + [pltpu.SemaphoreType.DMA((3,))],
         out_shape=[jax.ShapeDtypeStruct((row_count, packed_width), BF16)] * 3
-        + [jax.ShapeDtypeStruct((row_count, kv_width), BF16), jax.ShapeDtypeStruct((row_count, 2 * HD), BF16)],
+        + [jax.ShapeDtypeStruct((row_count, packed_width), BF16), jax.ShapeDtypeStruct((row_count, 2 * HD), BF16)],
         compiler_params=params(COPY_LIMIT),
         cost_estimate=SMALL,
     )(heads, queries, keys, values)
@@ -414,6 +476,7 @@
     x2 = spread(x2, 2)
     x1 = spread(x1, 1)
     partner = [swap_pair(own_kv)]
+    partner[0], out_weight = barrier((partner[0], out_weight))
     far = [
         lax.dynamic_slice(out_weight, (0, ((1 - side) * 2 + core) * width), (depth, width))
         for core in (core_index, 1 - core_index)
@@ -422,14 +485,36 @@
     own_weight = lax.dynamic_slice(out_weight, (0, side * 2 * width), (depth, 2 * width))
     x1, x2, x3, partner, own_weight, tables = barrier((x1, x2, x3, partner, own_weight, tables))
     gate, lifted, extra, step = tables
-    partner += [swap_pair(x[:, :kv_width]) for x in (x1, x2, x3)]
-    queries_in = (x1, x2, x3, own_q, own_q)
-    query_lanes = ((kv_width, False),) * 3 + ((0, False), (HD, True))
-    state = attend(queries_in, query_lanes, (own_kv, x1, x2, x3, partner[0]), None, ATTEND_COST)
-    state, far = barrier((state, far))
-    *results, mine = attend(queries_in, query_lanes, partner[1:], state, SMALL)
-    back = [spread(x, i + 1, True) for i, x in enumerate(results)]
-    back_across = [peer(x, 2) for x in back]
+    far_kv, far_q = pl.pallas_call(
+        gather_kernel,
+        out_shape=[jax.ShapeDtypeStruct((3 * row_count, kv_width), BF16)] * 2,
+        compiler_params=params(),
+        cost_estimate=SMALL,
+    )(x1, x2, x3)
+    swapped = swap_pair(far_kv)
+    *parts, acc, peak, total = pl.pallas_call(
+        common_kernel,
+        out_shape=[jax.ShapeDtypeStruct((row_count + STAT_ROWS, HD), BF16)] * 3
+        + [jax.ShapeDtypeStruct((row_count, HD), F32)] * 3,
+        compiler_params=params(),
+        cost_estimate=SMALL,
+    )(own_q, far_q, own_kv, partner[0])
+    state = attend(far_q, own_q, (own_kv, partner[0], far_kv), None, ATTEND_COST)
+    parts[0], state = barrier((parts[0], state))
+    parts = [spread(x, i + 1, True) for i, x in enumerate(parts)]
+    *results, own_result = attend(far_q, own_q, (swapped,), state, SMALL)
+    results, own_result, far = barrier((results, own_result, far))
+    mine = pl.pallas_call(
+        merge_kernel,
+        out_shape=jax.ShapeDtypeStruct((row_count, 2 * HD), BF16),
+        compiler_params=params(),
+        cost_estimate=SMALL,
+    )(*parts, acc, peak, total, own_result)
+    back, back_across = [None] * 3, [None] * 3
+    for at in (2, 1, 0):
+        back[at] = spread(results[at], at + 1, True)
+    for at in (0, 1, 2):
+        back_across[at] = peer(back[at], 2)
     mine_across = peer(mine, 2)
     mine_rows, back_rows = (0, None), (1, 2, 3)
     sums = [

time: 114 us -> 105 us (0.921)
  waiting for transfers between devices: 33.9 us -> 24.1 us
  starting transfers between devices: 37.3 us -> 42.3 us
  local copies, waits for them, and re-layouts: 12 us -> 9.21 us
  Pallas kernels: 26.4 us -> 25 us
    ppermute x6 -> x9, starting transfers between devices: 15.2 us -> 23.9 us  [spread(): return lax.ppermute(x, ('frame', 'tensor'), pairs)]
    ppermute x6 -> x9, waiting for transfers between devices: 23.6 us -> 15.9 us  [spread(): return lax.ppermute(x, ('frame', 'tensor'), pairs)]
    pallas_call x2, Pallas kernels: 13.8 us -> 8.46 us  [attend(): pl.pallas_call(body, out_shape=out_shape, compiler_params=params(), cost_...]
    ppermute x4 -> x2, starting transfers between devices: 6.43 us -> 2.28 us  [swap_pair(): return lax.ppermute(x, ('frame', 'tensor'), pairs)]
    pallas_call x0 -> x3, Pallas kernels: none -> 4.15 us  [the longest x1 2.42 us: local(): pl.pallas_call(common_kernel, out_shape=[jax.ShapeDtypeStruct((row_count...]
    slice x3 -> x0, local copies, waits for them, and re-layouts: 3.06 us -> none  [local(): partner += [swap_pair(x[:, :kv_width]) for x in (x1, x2, x3)]]
    ppermute x4 -> x2, waiting for transfers between devices: 2.25 us -> 0.01 us  [swap_pair(): return lax.ppermute(x, ('frame', 'tensor'), pairs)]
    unnamed x22 -> x26, local copies, waits for them, and re-layouts: 2.32 us -> 2.31 us
  transfers between devices with their start and end apart: 21 -> 22, of which waited for: 11 -> 11; matrix products, arithmetic and copies ran while one was open for 9% -> 7% of each run, Pallas kernels for 11% -> 17%
where the time goes in v3:
time: 105 us
  starting transfers between devices  42.3 us (40%)
  Pallas kernels  25 us (24%)
  waiting for transfers between devices  24.1 us (23%)
  local copies, waits for them, and re-layouts  9.21 us (9%)
  between operations  2.99 us (3%)
  other arithmetic  1.37 us (1%)
    ppermute x9, starting transfers between devices, spread(): return lax.ppermute(x, ('frame', 'tensor'), pairs)  23.9 us
    ppermute x9, waiting for transfers between devices, spread(): return lax.ppermute(x, ('frame', 'tensor'), pairs)  15.9 us
    pallas_call x2, Pallas kernels, attend(): pl.pallas_call(body, out_shape=out_shape, compiler_params=params(), cost_...  8.46 us
    ppermute x9, starting transfers between devices, peer(): return lax.ppermute(x, 'tensor', [(i, i ^ mask) for i in range(N_TENSOR)])  7.85 us
    ppermute x9, waiting for transfers between devices, peer(): return lax.ppermute(x, 'tensor', [(i, i ^ mask) for i in range(N_TENSOR)])  6.17 us
    ppermute x1, starting transfers between devices, shifted(): return lax.ppermute(x, axis, pairs)  6.15 us
    pallas_call x4, Pallas kernels, mix(): pl.pallas_call(body, in_specs=[pl.BlockSpec(memory_space=pltpu.SMEM)] + [...  5.89 us
    dynamic_slice x1, local copies, waits for them, and re-layouts, local(): lax.dynamic_slice(out_weight, (0, ((1 - side) * 2 + core) * width), (dept...  4.01 us
  transfers between devices with their start and end apart: 22, of which 11 were waited for; matrix products, arithmetic and copies ran while one was open for 7% of the time, Pallas kernels for 17%

profile of v3, /device:TPU:6, one launch (start us, length us, event | category | flops | bytes accessed | tf_op | source)
XLA Modules:
  0.0 104.9 jit_solution(16471325892128014043)
XLA Ops:
  1.4 3.2 %shard_map.130 = (bf16[384,512]{1,0:T(8,128)(2,1)}, bf16[384,512]{1,0:T(8,128)(2,1)}, bf16[384,512]{1,0:T(8,128)(2,1)}, bf16[384,512]{1,0:T(8,128)(2,1)}, bf16[384,256]{1,0:T(8,128)(2,1)}) custom-call(s32[7]{0:T(128)} %stack.31.head_ref.refs_0_, bf16[384,640]{1,0:T(8,128)(2,1)} %q_hbm.1, bf16[384,640]{1,0:T(8,128)(2,1)} %k_hbm.1, bf16[384,640]{1,0:T(8,128)(2,1)} %v_hbm.1), custom_call_target="tpu_custom_call" | custom-call | flops 1000 | bytes 1000 | tf_op jit(solution)/shard_map/pallas_call | solution.py:464
  4.6 2.0 %collective-permute-start.3 = (bf16[384,512]{1,0:T(8,128)(2,1)}, bf16[384,512]{1,0:T(8,128)(2,1)S(1)}, u32[]{:S(2)}, u32[]{:S(2)}) collective-permute-start(bf16[384,512]{1,0:T(8,128)(2,1)} %get-tuple-element.54.kv0.refs_2_), channel_id=1, source_target_pairs={{0,4},{1,29},{2,6},{3,31},{4,0},{5,9},{6,2},{7,11},{8,12},{9,5},{1... | collective-permute-start | bytes 1179656 | tf_op jit(solution)/shard_map/ppermute | solution.py:51
  6.6 4.9 %collective-permute-start = (bf16[384,512]{1,0:T(8,128)(2,1)}, bf16[384,512]{1,0:T(8,128)(2,1)}, u32[]{:S(2)}, u32[]{:S(2)}) collective-permute-start(bf16[384,512]{1,0:T(8,128)(2,1)} %get-tuple-element.51), channel_id=1, source_target_pairs={{0,28},{1,5},{2,30},{3,7},{4,8},{5,1},{6,10},{7,3},{8,4},{9,13},{1... | collective-permute-start | bytes 1179656 | tf_op jit(solution)/shard_map/ppermute | solution.py:41
  11.6 4.6 %collective-permute-start.2 = (bf16[384,512]{1,0:T(8,128)(2,1)}, bf16[384,512]{1,0:T(8,128)(2,1)}, u32[]{:S(2)}, u32[]{:S(2)}) collective-permute-start(bf16[384,512]{1,0:T(8,128)(2,1)} %get-tuple-element.53), channel_id=1, source_target_pairs={{0,20},{1,13},{2,22},{3,15},{4,16},{5,25},{6,18},{7,27},{8,28},{9,... | collective-permute-start | bytes 1179656 | tf_op jit(solution)/shard_map/ppermute | solution.py:41
  16.9 4.0 %constant_dynamic-slice_fusion = (bf16[640,1280]{1,0:T(8,128)(2,1)}, bf16[640,1280]{1,0:T(8,128)(2,1)}) fusion(bf16[640,5120]{1,0:T(8,128)(2,1)} %param.15, s32[]{:T(128)S(6)} %select_n.80, s32[]{:T(128)S(6)} %select_n.79), kind=kLoop, calls=%fused_computation.7 | loop fusion | bytes 6553608 | tf_op jit(solution)/shard_map/dynamic_slice | solution.py:481
  20.9 1.6 %collective-permute-start.5 = (bf16[640,1280]{1,0:T(8,128)(2,1)}, bf16[640,1280]{1,0:T(8,128)(2,1)S(1)}, u32[]{:S(2)}, u32[]{:S(2)}) collective-permute-start(bf16[640,1280]{1,0:T(8,128)(2,1)} %get-tuple-element.102), channel_id=1, source_target_pairs={{0,2},{1,3},{2,0},{3,1},{4,6},{5,7},{6,4},{7,5},{8,10},{9,11},{10,... | collective-permute-start | bytes 4915208 | tf_op jit(solution)/shard_map/ppermute | solution.py:63
  22.4 2.2 %collective-permute-start.6 = (bf16[640,1280]{1,0:T(8,128)(2,1)}, bf16[640,1280]{1,0:T(8,128)(2,1)S(1)}, u32[]{:S(2)}, u32[]{:S(2)}) collective-permute-start(bf16[640,1280]{1,0:T(8,128)(2,1)} %get-tuple-element.101), channel_id=1, source_target_pairs={{0,34},{1,35},{2,32},{3,33},{4,38},{5,39},{6,36},{7,37},{8,42},{9,... | collective-permute-start | bytes 4915208 | tf_op jit(solution)/shard_map/ppermute | solution.py:59
  26.0 1.5 %copy-done = bf16[3,256,1280]{2,1,0:T(8,128)(2,1)S(1)} copy-done((bf16[3,256,1280]{2,1,0:T(8,128)(2,1)S(1)}, bf16[3,256,1280]{2,1,0:T(8,128)(2,1)}, u32[]{:S(2)}) %copy-start) | copy-done | bytes 1966104
  29.5 2.2 %constant_dynamic-slice_fusion.2.refs_2_.refs_6_ = bf16[640,2560]{1,0:T(8,128)(2,1)S(1)} fusion(bf16[640,5120]{1,0:T(8,128)(2,1)} %param.15, s32[]{:T(128)S(6)} %select_n.76), kind=kLoop, calls=%fused_computation.9 | loop fusion | bytes 6553604 | tf_op jit(solution)/shard_map/dynamic_slice | solution.py:485
  31.7 10.6 %collective-permute-done.1.x2_ref = bf16[384,512]{1,0:T(8,128)(2,1)} collective-permute-done((bf16[384,512]{1,0:T(8,128)(2,1)}, bf16[384,512]{1,0:T(8,128)(2,1)}, u32[]{:S(2)}, u32[]{:S(2)}) %collective-permute-start.1) | collective-permute-done | bytes 393248 | tf_op jit(solution)/shard_map/ppermute | solution.py:41
  42.3 1.3 %shard_map.132 = (bf16[1152,256]{1,0:T(8,128)(2,1)S(1)}, bf16[1152,256]{1,0:T(8,128)(2,1)S(1)}) custom-call(bf16[384,512]{1,0:T(8,128)(2,1)} %collective-permute-done.x1_ref, bf16[384,512]{1,0:T(8,128)(2,1)} %collective-permute-done.1.x2_ref, bf16[384,512]{1,0:T(8,128)(2,1)} %collective-permute-done.2.x3_ref), custom_call_target="tpu_custom_call" | custom-call | flops 1000 | bytes 1000 | tf_op jit(solution)/shard_map/pallas_call | solution.py:488
  44.0 2.4 %shard_map.133 = (bf16[416,128]{1,0:T(8,128)(2,1)S(1)}, bf16[416,128]{1,0:T(8,128)(2,1)S(1)}, bf16[416,128]{1,0:T(8,128)(2,1)S(1)}, f32[384,128]{1,0:T(8,128)S(1...) custom-call(bf16[384,256]{1,0:T(8,128)(2,1)S(1)} %copy-done.2, ...), custom_call_target="tpu_custom_call" | custom-call | flops 1000 | bytes 1000 | tf_op jit(solution)/shard_map/pallas_call | solution.py:495
  46.4 4.5 %shard_map.134 = (f32[1536,128]{1,0:T(8,128)S(1)}, f32[1536,128]{1,0:T(8,128)S(1)}, f32[1536,128]{1,0:T(8,128)S(1)}) custom-call(bf16[1152,256]{1,0:T(8,128)(2,1)S(1)} %get-tuple-element.63.far_q_ref.refs_0_, bf16[384,256]{1,0:T(8,128)(2,1)S(1)} %copy-done.2, bf16[384,512]{1,0:T(8,128)(2,1)S(1)} %copy-done.3, bf16[384,512]{1,0:T(8,128)(2,1)S(1)} %copy-done.5, ...), custom_call_target="tpu_custom_call" | custom-call | flops 8999999488 | bytes 1000 | tf_op jit(solution)/shard_map/pallas_call | solution.py:258
  50.9 3.6 %collective-permute-start.13 = (bf16[416,128]{1,0:T(8,128)(2,1)S(1)}, bf16[416,128]{1,0:T(8,128)(2,1)S(1)}, u32[]{:S(2)}, u32[]{:S(2)}) collective-permute-start(bf16[416,128]{1,0:T(8,128)(2,1)S(1)} %get-tuple-element.82), channel_id=1, source_target_pairs={{28,0},{5,1},{30,2},{7,3},{8,4},{1,5},{10,6},{3,7},{4,8},{13,9},{6... | collective-permute-start | bytes 319496 | tf_op jit(solution)/shard_map/ppermute | solution.py:41
  55.1 3.2 %collective-permute-start.15 = (bf16[416,128]{1,0:T(8,128)(2,1)S(1)}, bf16[416,128]{1,0:T(8,128)(2,1)S(1)}, u32[]{:S(2)}, u32[]{:S(2)}) collective-permute-start(bf16[416,128]{1,0:T(8,128)(2,1)S(1)} %get-tuple-element.84), channel_id=1, source_target_pairs={{20,0},{13,1},{22,2},{15,3},{16,4},{25,5},{18,6},{27,7},{28,8},{21... | collective-permute-start | bytes 319496 | tf_op jit(solution)/shard_map/ppermute | solution.py:41
  58.3 3.9 %shard_map.135 = (bf16[384,128]{1,0:T(8,128)(2,1)S(1)}, bf16[384,128]{1,0:T(8,128)(2,1)S(1)}, bf16[384,128]{1,0:T(8,128)(2,1)S(1)}, bf16[384,128]{1,0:T(8,128)(2,1)S(1)}) custom-call(bf16[1152,256]{1,0:T(8,128)(2,1)S(1)} %get-tuple-element.63.far_q_ref.refs_0_, bf16[384,256]{1,0:T(8,128)(2,1)S(1)} %copy-done.2, ...), custom_call_target="tpu_custom_call" | custom-call | flops 1000 | bytes 1000 | tf_op jit(solution)/shard_map/pallas_call | solution.py:258
  63.3 1.7 %collective-permute-start.16 = (bf16[384,256]{1,0:T(8,128)(2,1)S(1)}, bf16[384,256]{1,0:T(8,128)(2,1)S(1)}, u32[]{:S(2)}, u32[]{:S(2)}) collective-permute-start(bf16[384,256]{1,0:T(8,128)(2,1)S(1)} %shard_map.136.refs_1_), channel_id=1, source_target_pairs={{0,2},{1,3},{2,0},{3,1},{4,6},{5,7},{6,4},{7,5},{8,10},{9,11},{10,... | collective-permute-start | bytes 589832 | tf_op jit(solution)/shard_map/ppermute | solution.py:63
  65.0 3.5 %collective-permute-start.9 = (bf16[384,128]{1,0:T(8,128)(2,1)S(1)}, bf16[384,128]{1,0:T(8,128)(2,1)S(1)}, u32[]{:S(2)}, u32[]{:S(2)}) collective-permute-start(bf16[384,128]{1,0:T(8,128)(2,1)S(1)} %get-tuple-element.79), channel_id=1, source_target_pairs={{8,0},{25,1},{10,2},{27,3},{28,4},{13,5},{30,6},{15,7},{16,8},{1,9... | collective-permute-start | bytes 294920 | tf_op jit(solution)/shard_map/ppermute | solution.py:41
  68.5 1.1 %collective-permute-start.11 = (bf16[384,128]{1,0:T(8,128)(2,1)S(1)}, bf16[384,128]{1,0:T(8,128)(2,1)S(1)}, u32[]{:S(2)}, u32[]{:S(2)}) collective-permute-start(bf16[384,128]{1,0:T(8,128)(2,1)S(1)} %get-tuple-element.80), channel_id=1, source_target_pairs={{20,0},{13,1},{22,2},{15,3},{16,4},{25,5},{18,6},{27,7},{28,8},{21... | collective-permute-start | bytes 294920 | tf_op jit(solution)/shard_map/ppermute | solution.py:41
  69.6 2.3 %collective-permute-start.7 = (bf16[384,128]{1,0:T(8,128)(2,1)S(1)}, bf16[384,128]{1,0:T(8,128)(2,1)S(1)}, u32[]{:S(2)}, u32[]{:S(2)}) collective-permute-start(bf16[384,128]{1,0:T(8,128)(2,1)S(1)} %get-tuple-element.78), channel_id=1, source_target_pairs={{28,0},{5,1},{30,2},{7,3},{8,4},{1,5},{10,6},{3,7},{4,8},{13,9},{6... | collective-permute-start | bytes 294920 | tf_op jit(solution)/shard_map/ppermute | solution.py:41
  71.9 1.4 %collective-permute-done.9.refs_4_ = bf16[384,128]{1,0:T(8,128)(2,1)S(1)} collective-permute-done((bf16[384,128]{1,0:T(8,128)(2,1)S(1)}, bf16[384,128]{1,0:T(8,128)(2,1)S(1)}, u32[]{:S(2)}, u32[]{:S(2)}) %collective-permute-start.9) | collective-permute-done | bytes 98336 | tf_op jit(solution)/shard_map/ppermute | solution.py:41
  73.7 3.5 %collective-permute-done.11.refs_5_ = bf16[384,128]{1,0:T(8,128)(2,1)S(1)} collective-permute-done((bf16[384,128]{1,0:T(8,128)(2,1)S(1)}, bf16[384,128]{1,0:T(8,128)(2,1)S(1)}, u32[]{:S(2)}, u32[]{:S(2)}) %collective-permute-start.11) | collective-permute-done | bytes 98336 | tf_op jit(solution)/shard_map/ppermute | solution.py:41
  77.7 1.5 %collective-permute-start.8 = (bf16[384,128]{1,0:T(8,128)(2,1)S(1)}, bf16[384,128]{1,0:T(8,128)(2,1)S(1)}, u32[]{:S(2)}, u32[]{:S(2)}) collective-permute-start(bf16[384,128]{1,0:T(8,128)(2,1)S(1)} %collective-permute-done.7.refs_3_), channel_id=1, source_target_pairs={{0,2},{1,3},{2,0},{3,1},{4,6},{5,7},{6,4},{7,5},{8,10},{9,11},{10,... | collective-permute-start | bytes 294920 | tf_op jit(solution)/shard_map/ppermute | solution.py:63
  79.2 1.7 %shard_map.139.refs_5_ = f32[384,1280]{1,0:T(8,128)S(1)} custom-call(s32[7]{0:T(128)S(1)} %copy-done.10, bf16[384,256]{1,0:T(8,128)(2,1)S(1)} %shard_map.136.refs_1_, bf16[640,2560]{1,0:T(8,128)(2,1)S(1)} %constant_dynamic-slice_fusion.2.refs_2_.refs_6_, bf16[384,128]{1,0:T(8,128)(2,1)S(1)} %collective-permute-done.7.refs_3_, ...), custom_call_target="tpu_custom_call" | custom-call | flops 1000 | bytes 1000 | tf_op jit(solution)/shard_map/pallas_call | solution.py:332
  81.8 1.1 %collective-permute-done.8.refs_1_ = bf16[384,128]{1,0:T(8,128)(2,1)S(1)} collective-permute-done((bf16[384,128]{1,0:T(8,128)(2,1)S(1)}, bf16[384,128]{1,0:T(8,128)(2,1)S(1)}, u32[]{:S(2)}, u32[]{:S(2)}) %collective-permute-start.8) | collective-permute-done | bytes 98336 | tf_op jit(solution)/shard_map/ppermute | solution.py:63
  82.9 1.2 %shard_map.140 = bf16[384,1280]{1,0:T(8,128)(2,1)S(1)} custom-call(s32[7]{0:T(128)S(1)} %copy-done.10, bf16[384,128]{1,0:T(8,128)(2,1)S(1)} %collective-permute-done.8.refs_1_, bf16[384,128]{1,0:T(8,128)(2,1)S(1)} %collective-permute-done.10.refs_2_, bf16[384,128]{1,0:T(8,128)(2,1)S(1)} %collective-permute-done.12.refs_3_, ...), custom_call_target="tpu_custom_call" | custom-call | flops 1000 | bytes 1000 | tf_op jit(solution)/shard_map/pallas_call | solution.py:332
  84.4 1.7 %shard_map.137.refs_5_ = f32[384,1280]{1,0:T(8,128)S(1)} custom-call(s32[7]{0:T(128)S(1)} %copy-done.10, bf16[384,256]{1,0:T(8,128)(2,1)S(1)} %shard_map.136.refs_1_, bf16[640,2560]{1,0:T(8,128)(2,1)S(1)} %constant_dynamic-slice_fusion.2.refs_2_.refs_6_, bf16[384,128]{1,0:T(8,128)(2,1)S(1)} %collective-permute-done.7.refs_3_, ...), custom_call_target="tpu_custom_call" | custom-call | flops 1000 | bytes 1000 | tf_op jit(solution)/shard_map/pallas_call | solution.py:332
  86.2 1.2 %shard_map.138.acc_ref = f32[384,1280]{1,0:T(8,128)S(1)} custom-call(s32[7]{0:T(128)S(1)} %copy-done.10, bf16[384,128]{1,0:T(8,128)(2,1)S(1)} %collective-permute-done.8.refs_1_, bf16[384,128]{1,0:T(8,128)(2,1)S(1)} %collective-permute-done.10.refs_2_, bf16[384,128]{1,0:T(8,128)(2,1)S(1)} %collective-permute-done.12.refs_3_, ...), custom_call_target="tpu_custom_call" | custom-call | flops 1000 | bytes 1000 | tf_op jit(solution)/shard_map/pallas_call | solution.py:332
  87.5 1.9 %shard_map.141 = (bf16[384,1280]{1,0:T(8,128)(2,1)}, bf16[80,512]{1,0:T(8,128)(2,1)S(1)}) custom-call(f32[384,1280]{1,0:T(8,128)S(1)} %shard_map.138.acc_ref, bf16[384,1280]{1,0:T(8,128)(2,1)S(1)} %collective-permute-done.17.other_ref, bf16[384,1280]{1,0:T(8,128)(2,1)S(1)} %copy-done.1, f32[8,1280]{1,0:T(8,128)S(1)} %get-tuple-element.91.gate_ref, ...), custom_call_target="tpu_custom_call" | custom-call | flops 1000 | bytes 1000 | tf_op jit(solution)/shard_map/pallas_call | solution.py:537
  91.3 3.6 %collective-permute-done.19.m2 = bf16[80,512]{1,0:T(8,128)(2,1)S(1)} collective-permute-done((bf16[80,512]{1,0:T(8,128)(2,1)S(1)}, bf16[80,512]{1,0:T(8,128)(2,1)S(1)}, u32[]{:S(2)}, u32[]{:S(2)}) %collective-permute-start.19) | collective-permute-done | bytes 81952 | tf_op jit(solution)/shard_map/ppermute | solution.py:63
  96.4 6.1 %collective-permute-start.21 = (bf16[64,384]{1,0:T(8,128)(2,1)S(1)}, bf16[64,384]{1,0:T(8,128)(2,1)S(1)}, u32[]{:S(2)}, u32[]{:S(2)}) collective-permute-start(bf16[64,384]{1,0:T(8,128)(2,1)S(1)} %get-tuple-element.98), channel_id=1, source_target_pairs={{4,0},{8,4},{12,8},{16,12},{20,16},{24,20},{28,24},{32,28},{36,32}... | collective-permute-start | bytes 147464 | tf_op jit(solution)/shard_map/ppermute | solution.py:69
  102.6 1.7 %collective-permute-done.21 = bf16[64,384]{1,0:T(8,128)(2,1)S(1)} collective-permute-done((bf16[64,384]{1,0:T(8,128)(2,1)S(1)}, bf16[64,384]{1,0:T(8,128)(2,1)S(1)}, u32[]{:S(2)}, u32[]{:S(2)}) %collective-permute-start.21) | collective-permute-done | bytes 49184 | tf_op jit(solution)/shard_map/ppermute | solution.py:69
  (58 shorter events, 10.6 us)
Async XLA Ops:
  4.6 12.2 %collective-permute-start.3 = (bf16[384,512]{1,0:T(8,128)(2,1)}, bf16[384,512]{1,0:T(8,128)(2,1)S(1)}, u32[]{:S(2)}, u32[]{:S(2)}) collective-permute-start(bf16[384,512]{1,0:T(8,128)(2,1)} %get-tuple-element.54.kv0.refs_2_), channel_id=1, source_target_pairs={{0,4},{1,29},{2,6},{3,31},{4,0},{5,9},{6,2},{7,11},{8,12},{9,5},{1... | collective-permute-start | bytes 1179656 | tf_op jit(solution)/shard_map/ppermute | solution.py:51
  6.6 25.1 %collective-permute-start = (bf16[384,512]{1,0:T(8,128)(2,1)}, bf16[384,512]{1,0:T(8,128)(2,1)}, u32[]{:S(2)}, u32[]{:S(2)}) collective-permute-start(bf16[384,512]{1,0:T(8,128)(2,1)} %get-tuple-element.51), channel_id=1, source_target_pairs={{0,28},{1,5},{2,30},{3,7},{4,8},{5,1},{6,10},{7,3},{8,4},{9,13},{1... | collective-permute-start | bytes 1179656 | tf_op jit(solution)/shard_map/ppermute | solution.py:41
  11.6 30.8 %collective-permute-start.1 = (bf16[384,512]{1,0:T(8,128)(2,1)}, bf16[384,512]{1,0:T(8,128)(2,1)}, u32[]{:S(2)}, u32[]{:S(2)}) collective-permute-start(bf16[384,512]{1,0:T(8,128)(2,1)} %get-tuple-element.52), channel_id=1, source_target_pairs={{0,8},{1,25},{2,10},{3,27},{4,28},{5,13},{6,30},{7,15},{8,16},{9,1... | collective-permute-start | bytes 1179656 | tf_op jit(solution)/shard_map/ppermute | solution.py:41
  11.6 30.8 %collective-permute-start.2 = (bf16[384,512]{1,0:T(8,128)(2,1)}, bf16[384,512]{1,0:T(8,128)(2,1)}, u32[]{:S(2)}, u32[]{:S(2)}) collective-permute-start(bf16[384,512]{1,0:T(8,128)(2,1)} %get-tuple-element.53), channel_id=1, source_target_pairs={{0,20},{1,13},{2,22},{3,15},{4,16},{5,25},{6,18},{7,27},{8,28},{9,... | collective-permute-start | bytes 1179656 | tf_op jit(solution)/shard_map/ppermute | solution.py:41
  16.8 7.8 %copy-start.12 = (s32[129]{0:T(256)S(1)}, s32[129]{0:T(256)}, u32[]{:S(2)}) copy-start(s32[129]{0:T(256)} %param.21) | copy-start | bytes 1552
  16.8 9.2 %copy-start.8 = (bf16[1280,64]{0,1:T(8,128)(2,1)S(1)}, bf16[1280,64]{0,1:T(8,128)(2,1)}, u32[]{:S(2)}) copy-start(bf16[1280,64]{0,1:T(8,128)(2,1)} %param.17) | copy-start | bytes 491524
  16.9 4.0 %copy-start.4 = (bf16[384,512]{1,0:T(8,128)(2,1)}, bf16[384,512]{1,0:T(8,128)(2,1)S(1)}, u32[]{:S(2)}) copy-start(bf16[384,512]{1,0:T(8,128)(2,1)S(1)} %collective-permute-done.3.kv1.refs_3_) | copy-start | bytes 1179652
  20.9 41.4 %collective-permute-start.5 = (bf16[640,1280]{1,0:T(8,128)(2,1)}, bf16[640,1280]{1,0:T(8,128)(2,1)S(1)}, u32[]{:S(2)}, u32[]{:S(2)}) collective-permute-start(bf16[640,1280]{1,0:T(8,128)(2,1)} %get-tuple-element.102), channel_id=1, source_target_pairs={{0,2},{1,3},{2,0},{3,1},{4,6},{5,7},{6,4},{7,5},{8,10},{9,11},{10,... | collective-permute-start | bytes 4915208 | tf_op jit(solution)/shard_map/ppermute | solution.py:63
  22.4 40.1 %collective-permute-start.6 = (bf16[640,1280]{1,0:T(8,128)(2,1)}, bf16[640,1280]{1,0:T(8,128)(2,1)S(1)}, u32[]{:S(2)}, u32[]{:S(2)}) collective-permute-start(bf16[640,1280]{1,0:T(8,128)(2,1)} %get-tuple-element.101), channel_id=1, source_target_pairs={{0,34},{1,35},{2,32},{3,33},{4,38},{5,39},{6,36},{7,37},{8,42},{9,... | collective-permute-start | bytes 4915208 | tf_op jit(solution)/shard_map/ppermute | solution.py:59
  26.0 1.5 %copy-start = (bf16[3,256,1280]{2,1,0:T(8,128)(2,1)S(1)}, bf16[3,256,1280]{2,1,0:T(8,128)(2,1)}, u32[]{:S(2)}) copy-start(bf16[3,256,1280]{2,1,0:T(8,128)(2,1)} %time_ref.1) | copy-start | bytes 5898244
  29.4 14.5 %copy-start.2 = (bf16[384,256]{1,0:T(8,128)(2,1)S(1)}, bf16[384,256]{1,0:T(8,128)(2,1)}, u32[]{:S(2)}) copy-start(bf16[384,256]{1,0:T(8,128)(2,1)} %get-tuple-element.64.own_q_ref.refs_1_) | copy-start | bytes 589828
  29.4 14.5 %copy-start.3 = (bf16[384,512]{1,0:T(8,128)(2,1)S(1)}, bf16[384,512]{1,0:T(8,128)(2,1)}, u32[]{:S(2)}) copy-start(bf16[384,512]{1,0:T(8,128)(2,1)} %get-tuple-element.54.kv0.refs_2_) | copy-start | bytes 1179652
  29.4 14.5 %copy-start.5 = (bf16[384,512]{1,0:T(8,128)(2,1)S(1)}, bf16[384,512]{1,0:T(8,128)(2,1)}, u32[]{:S(2)}) copy-start(bf16[384,512]{1,0:T(8,128)(2,1)} %copy-done.4) | copy-start | bytes 1179652
  43.7 11.4 %collective-permute-start.4 = (bf16[1152,256]{1,0:T(8,128)(2,1)S(1)}, bf16[1152,256]{1,0:T(8,128)(2,1)S(1)}, u32[]{:S(2)}, u32[]{:S(2)}) collective-permute-start(bf16[1152,256]{1,0:T(8,128)(2,1)S(1)} %get-tuple-element.65.refs_4_), channel_id=1, source_target_pairs={{0,4},{1,29},{2,6},{3,31},{4,0},{5,9},{6,2},{7,11},{8,12},{9,5},{1... | collective-permute-start | bytes 1769480 | tf_op jit(solution)/shard_map/ppermute | solution.py:51
  50.9 11.6 %collective-permute-start.13 = (bf16[416,128]{1,0:T(8,128)(2,1)S(1)}, bf16[416,128]{1,0:T(8,128)(2,1)S(1)}, u32[]{:S(2)}, u32[]{:S(2)}) collective-permute-start(bf16[416,128]{1,0:T(8,128)(2,1)S(1)} %get-tuple-element.82), channel_id=1, source_target_pairs={{28,0},{5,1},{30,2},{7,3},{8,4},{1,5},{10,6},{3,7},{4,8},{13,9},{6... | collective-permute-start | bytes 319496 | tf_op jit(solution)/shard_map/ppermute | solution.py:41
  54.5 8.0 %collective-permute-start.14 = (bf16[416,128]{1,0:T(8,128)(2,1)S(1)}, bf16[416,128]{1,0:T(8,128)(2,1)S(1)}, u32[]{:S(2)}, u32[]{:S(2)}) collective-permute-start(bf16[416,128]{1,0:T(8,128)(2,1)S(1)} %get-tuple-element.83), channel_id=1, source_target_pairs={{8,0},{25,1},{10,2},{27,3},{28,4},{13,5},{30,6},{15,7},{16,8},{1,9... | collective-permute-start | bytes 319496 | tf_op jit(solution)/shard_map/ppermute | solution.py:41
  55.1 24.2 %copy-start.10 = (s32[7]{0:T(128)S(1)}, s32[7]{0:T(128)}, u32[]{:S(2)}) copy-start(s32[7]{0:T(128)} %stack.31.head_ref.refs_0_) | copy-start | bytes 88
  55.1 7.8 %collective-permute-start.15 = (bf16[416,128]{1,0:T(8,128)(2,1)S(1)}, bf16[416,128]{1,0:T(8,128)(2,1)S(1)}, u32[]{:S(2)}, u32[]{:S(2)}) collective-permute-start(bf16[416,128]{1,0:T(8,128)(2,1)S(1)} %get-tuple-element.84), channel_id=1, source_target_pairs={{20,0},{13,1},{22,2},{15,3},{16,4},{25,5},{18,6},{27,7},{28,8},{21... | collective-permute-start | bytes 319496 | tf_op jit(solution)/shard_map/ppermute | solution.py:41
  63.3 15.9 %collective-permute-start.16 = (bf16[384,256]{1,0:T(8,128)(2,1)S(1)}, bf16[384,256]{1,0:T(8,128)(2,1)S(1)}, u32[]{:S(2)}, u32[]{:S(2)}) collective-permute-start(bf16[384,256]{1,0:T(8,128)(2,1)S(1)} %shard_map.136.refs_1_), channel_id=1, source_target_pairs={{0,2},{1,3},{2,0},{3,1},{4,6},{5,7},{6,4},{7,5},{8,10},{9,11},{10,... | collective-permute-start | bytes 589832 | tf_op jit(solution)/shard_map/ppermute | solution.py:63
  65.0 8.3 %collective-permute-start.9 = (bf16[384,128]{1,0:T(8,128)(2,1)S(1)}, bf16[384,128]{1,0:T(8,128)(2,1)S(1)}, u32[]{:S(2)}, u32[]{:S(2)}) collective-permute-start(bf16[384,128]{1,0:T(8,128)(2,1)S(1)} %get-tuple-element.79), channel_id=1, source_target_pairs={{8,0},{25,1},{10,2},{27,3},{28,4},{13,5},{30,6},{15,7},{16,8},{1,9... | collective-permute-start | bytes 294920 | tf_op jit(solution)/shard_map/ppermute | solution.py:41
  68.5 8.7 %collective-permute-start.11 = (bf16[384,128]{1,0:T(8,128)(2,1)S(1)}, bf16[384,128]{1,0:T(8,128)(2,1)S(1)}, u32[]{:S(2)}, u32[]{:S(2)}) collective-permute-start(bf16[384,128]{1,0:T(8,128)(2,1)S(1)} %get-tuple-element.80), channel_id=1, source_target_pairs={{20,0},{13,1},{22,2},{15,3},{16,4},{25,5},{18,6},{27,7},{28,8},{21... | collective-permute-start | bytes 294920 | tf_op jit(solution)/shard_map/ppermute | solution.py:41
  69.6 8.1 %collective-permute-start.7 = (bf16[384,128]{1,0:T(8,128)(2,1)S(1)}, bf16[384,128]{1,0:T(8,128)(2,1)S(1)}, u32[]{:S(2)}, u32[]{:S(2)}) collective-permute-start(bf16[384,128]{1,0:T(8,128)(2,1)S(1)} %get-tuple-element.78), channel_id=1, source_target_pairs={{28,0},{5,1},{30,2},{7,3},{8,4},{1,5},{10,6},{3,7},{4,8},{13,9},{6... | collective-permute-start | bytes 294920 | tf_op jit(solution)/shard_map/ppermute | solution.py:41
  73.3 7.7 %collective-permute-start.10 = (bf16[384,128]{1,0:T(8,128)(2,1)S(1)}, bf16[384,128]{1,0:T(8,128)(2,1)S(1)}, u32[]{:S(2)}, u32[]{:S(2)}) collective-permute-start(bf16[384,128]{1,0:T(8,128)(2,1)S(1)} %collective-permute-done.9.refs_4_), channel_id=1, source_target_pairs={{0,2},{1,3},{2,0},{3,1},{4,6},{5,7},{6,4},{7,5},{8,10},{9,11},{10,... | collective-permute-start | bytes 294920 | tf_op jit(solution)/shard_map/ppermute | solution.py:63
  77.2 4.6 %collective-permute-start.12 = (bf16[384,128]{1,0:T(8,128)(2,1)S(1)}, bf16[384,128]{1,0:T(8,128)(2,1)S(1)}, u32[]{:S(2)}, u32[]{:S(2)}) collective-permute-start(bf16[384,128]{1,0:T(8,128)(2,1)S(1)} %collective-permute-done.11.refs_5_), channel_id=1, source_target_pairs={{0,2},{1,3},{2,0},{3,1},{4,6},{5,7},{6,4},{7,5},{8,10},{9,11},{10,... | collective-permute-start | bytes 294920 | tf_op jit(solution)/shard_map/ppermute | solution.py:63
  77.7 5.1 %collective-permute-start.8 = (bf16[384,128]{1,0:T(8,128)(2,1)S(1)}, bf16[384,128]{1,0:T(8,128)(2,1)S(1)}, u32[]{:S(2)}, u32[]{:S(2)}) collective-permute-start(bf16[384,128]{1,0:T(8,128)(2,1)S(1)} %collective-permute-done.7.refs_3_), channel_id=1, source_target_pairs={{0,2},{1,3},{2,0},{3,1},{4,6},{5,7},{6,4},{7,5},{8,10},{9,11},{10,... | collective-permute-start | bytes 294920 | tf_op jit(solution)/shard_map/ppermute | solution.py:63
  84.1 3.4 %collective-permute-start.17 = (bf16[384,1280]{1,0:T(8,128)(2,1)S(1)}, bf16[384,1280]{1,0:T(8,128)(2,1)S(1)}, u32[]{:S(2)}, u32[]{:S(2)}) collective-permute-start(bf16[384,1280]{1,0:T(8,128)(2,1)S(1)} %shard_map.140), channel_id=1, source_target_pairs={{0,1},{1,0},{2,3},{3,2},{4,5},{5,4},{6,7},{7,6},{8,9},{9,8},{10,11... | collective-permute-start | bytes 2949128 | tf_op jit(solution)/shard_map/ppermute | solution.py:63
  87.4 8.1 %copy-start.9 = (f32[384,64]{0,1:T(8,128)S(1)}, f32[384,64]{0,1:T(8,128)}, u32[]{:S(2)}) copy-start(f32[384,64]{0,1:T(8,128)} %param.18) | copy-start | bytes 294916
  87.4 16.8 %copy-start.11 = (f32[384,64]{0,1:T(8,128)S(1)}, f32[384,64]{0,1:T(8,128)}, u32[]{:S(2)}) copy-start(f32[384,64]{0,1:T(8,128)} %param.19) | copy-start | bytes 294916
  89.4 1.9 %collective-permute-start.18 = (bf16[80,512]{1,0:T(8,128)(2,1)S(1)}, bf16[80,512]{1,0:T(8,128)(2,1)S(1)}, u32[]{:S(2)}, u32[]{:S(2)}) collective-permute-start(bf16[80,512]{1,0:T(8,128)(2,1)S(1)} %get-tuple-element.95.m0), channel_id=1, source_target_pairs={{0,1},{1,0},{2,3},{3,2},{4,5},{5,4},{6,7},{7,6},{8,9},{9,8},{10,11... | collective-permute-start | bytes 245768 | tf_op jit(solution)/shard_map/ppermute | solution.py:63
  89.9 5.0 %collective-permute-start.19 = (bf16[80,512]{1,0:T(8,128)(2,1)S(1)}, bf16[80,512]{1,0:T(8,128)(2,1)S(1)}, u32[]{:S(2)}, u32[]{:S(2)}) collective-permute-start(bf16[80,512]{1,0:T(8,128)(2,1)S(1)} %get-tuple-element.95.m0), channel_id=1, source_target_pairs={{0,2},{1,3},{2,0},{3,1},{4,6},{5,7},{6,4},{7,5},{8,10},{9,11},{10,... | collective-permute-start | bytes 245768 | tf_op jit(solution)/shard_map/ppermute | solution.py:63
  90.9 4.7 %collective-permute-start.20 = (bf16[80,512]{1,0:T(8,128)(2,1)S(1)}, bf16[80,512]{1,0:T(8,128)(2,1)S(1)}, u32[]{:S(2)}, u32[]{:S(2)}) collective-permute-start(bf16[80,512]{1,0:T(8,128)(2,1)S(1)} %get-tuple-element.95.m0), channel_id=1, source_target_pairs={{0,3},{1,2},{2,1},{3,0},{4,7},{5,6},{6,5},{7,4},{8,11},{9,10},{10,... | collective-permute-start | bytes 245768 | tf_op jit(solution)/shard_map/ppermute | solution.py:63
  96.4 7.9 %collective-permute-start.21 = (bf16[64,384]{1,0:T(8,128)(2,1)S(1)}, bf16[64,384]{1,0:T(8,128)(2,1)S(1)}, u32[]{:S(2)}, u32[]{:S(2)}) collective-permute-start(bf16[64,384]{1,0:T(8,128)(2,1)S(1)} %get-tuple-element.98), channel_id=1, source_target_pairs={{4,0},{8,4},{12,8},{16,12},{20,16},{24,20},{28,24},{32,28},{36,32}... | collective-permute-start | bytes 147464 | tf_op jit(solution)/shard_map/ppermute | solution.py:69
  (3 other events, 3.3 us)

commit v4 on v3

--- a/solution.py
+++ b/solution.py
@@ -98,9 +98,17 @@
     return hi, mid, (rest - mid.astype(F32)).astype(BF16)
 
 
-def pack_kernel(
-    head_ref, q_hbm, k_hbm, v_hbm, x1_ref, x2_ref, x3_ref, kv_ref, q_out_ref, q_ref, k_ref, v_ref, sem
-):
+def ring_heads():
+    at = lax.rem(lax.axis_index("frame") - lax.rem(lax.axis_index("tensor"), 2) + PART, PART)
+    pair, member = lax.div(at, 2), lax.rem(at, 2)
+    ahead = lax.rem(pair + 1, SPREAD_HEADS)
+    behind = lax.rem(pair + SPREAD_HEADS - 1, SPREAD_HEADS)
+    first = member * ahead + (1 - member) * behind
+    second = member * behind + (1 - member) * ahead
+    return [pair, first, second, lax.rem(pair + 2, SPREAD_HEADS)]
+
+
+def pack_kernel(q_hbm, k_hbm, v_hbm, x1_ref, x2_ref, x3_ref, kv_ref, q_out_ref, q_ref, k_ref, v_ref, sem, out_sem):
     common = pl.ds(SPREAD_HEADS * HD, HD)
     copies = [
         pltpu.make_async_copy(source, target, sem.at[at])
@@ -108,22 +116,31 @@
     ]
     for copy in copies:
         copy.start()
-
-    def lanes(at):
-        return pl.ds(pl.multiple_of(head_ref[at] * HD, HD), HD)
-
-    targets = ((3, x3_ref), (2, x2_ref), (1, x1_ref), (0, kv_ref))
+    own = [pl.ds(pl.multiple_of(head * HD, HD), HD) for head in ring_heads()]
+    moves = []
+
+    def move(source, lanes, target, slot):
+        moves.append(
+            pltpu.make_async_copy(
+                source.at[:, lanes], target.at[:, pl.ds(slot * HD, HD)], out_sem.at[len(moves)]
+            )
+        )
+        moves[-1].start()
+
+    targets = (kv_ref, x1_ref, x2_ref, x3_ref)
     for slot, (copy, source) in enumerate(zip(copies[:2], (k_ref, v_ref))):
         copy.wait()
-        for at, ref in targets:
-            ref[:, slot * HD : (slot + 1) * HD] = source[:, lanes(at)]
-        kv_ref[:, (slot + 2) * HD : (slot + 3) * HD] = source[:, common]
+        for at, ref in enumerate(targets):
+            move(source, own[at], ref, slot)
+        move(source, common, kv_ref, slot + 2)
     copies[2].wait()
-    for at, ref in targets[:3]:
-        ref[:, 2 * HD : 3 * HD] = q_ref[:, lanes(at)]
-        ref[:, 3 * HD :] = q_ref[:, common]
-    q_out_ref[:, 0:HD] = q_ref[:, lanes(0)]
-    q_out_ref[:, HD:] = q_ref[:, common]
+    for at, ref in enumerate(targets[1:], 1):
+        move(q_ref, own[at], ref, 2)
+        move(q_ref, common, ref, 3)
+    move(q_ref, own[0], q_out_ref, 0)
+    move(q_ref, common, q_out_ref, 1)
+    for copy in moves:
+        copy.wait()
 
 
 def softmax_block(query, keys, values, old=None):
@@ -273,7 +290,7 @@
     lifted_ref[channels:] = low
     lift_head = jnp.sum(high.astype(F32) + low.astype(F32), axis=1, keepdims=True)
     shift_head = jnp.sum(head * shift, axis=1, keepdims=True)
-    extra_ref[...] = place(split3(lift_head) + split3(shift_head), extra_ref.shape).astype(BF16)
+    extra_ref[...] = place((lift_head, shift_head), extra_ref.shape)
 
 
 def place(pieces, shape):
@@ -343,7 +360,7 @@
     acc_ref, other_ref, in_ref, gate_ref, lifted_ref, extra_ref, stream_ref, message_ref
 ):
     row_count, width = stream_ref.shape
-    channels = extra_ref.shape[0]
+    channels = lifted_ref.shape[0] // 2
     total = None
     squares = None
     share = None
@@ -370,37 +387,58 @@
     spread = jnp.sum(squares, axis=1, keepdims=True) - mean * mean * width
     stats = jnp.transpose(place((mean, spread), (row_count, HD)))
     mean_row, spread_row = stats[0:1], stats[1:2]
-    extra = extra_ref[...].astype(F32)
-    lift_head = extra[:, 0:1] + extra[:, 1:2] + extra[:, 2:3]
-    share = share[0:channels] + share[channels:] + rest - lift_head * mean_row
-    rows = [x.astype(F32) for x in split3(mean_row) + split3(spread_row)]
+    extra = extra_ref[...]
+    share = share[0:channels] + share[channels:] + rest - extra[:, 0:1] * mean_row
+    message_ref[0:channels, 0:row_count] = share
+    message_ref[0:channels, row_count:] = extra
+    message_ref[channels:, 0:row_count] = jnp.concatenate(
+        [mean_row, spread_row, jnp.zeros((6, row_count), F32)], axis=0
+    )
+    message_ref[channels:, row_count:] = jnp.zeros((8, HD), F32)
+
+
+def pair_kernel(a_ref, b_ref, out_ref):
+    channels = a_ref.shape[0] - 8
+    row_count = a_ref.shape[1] - HD
+    width = D // N_TENSOR
+    refs = (a_ref, b_ref)
+    means = [ref[channels : channels + 1, 0:row_count] for ref in refs]
+    spreads = [ref[channels + 1 : channels + 2, 0:row_count] for ref in refs]
+    mean = (means[0] + means[1]) * 0.5
+    offsets = [x - mean for x in means]
+    spread = (spreads[0] + spreads[1]) + (offsets[0] * offsets[0] + offsets[1] * offsets[1]) * width
+    extras = [ref[0:channels, row_count:] for ref in refs]
+    shares = [ref[0:channels, 0:row_count] + o * e[:, 0:1] for ref, o, e in zip(refs, offsets, extras)]
+    out_ref[0:channels, 0:row_count] = (shares[0] + shares[1]).astype(BF16)
+    extra = extras[0] + extras[1]
+    pieces = split3(extra[:, 0:1]) + split3(extra[:, 1:2])
+    out_ref[0:channels, row_count:] = place(pieces, (channels, HD)).astype(BF16)
+    rows = [x.astype(F32) for x in split3(mean) + split3(spread)]
     rows = jnp.concatenate(rows + [jnp.zeros((10, row_count), F32)], axis=0)
-    message_ref[0:channels, 0:row_count] = share.astype(BF16)
-    message_ref[channels:, 0:row_count] = rows.astype(BF16)
-    message_ref[0:channels, row_count:] = extra_ref[...]
-    message_ref[channels:, row_count:] = jnp.zeros((16, HD), BF16)
-
-
-def finish_kernel(m0, m1, m2, m3, latent_ref, step_ref, velocity_ref, updated_ref):
-    channels, row_count = velocity_ref.shape
-    refs = (m0, m1, m2, m3)
-
-    def tree(values):
-        return (values[0] + values[1]) + (values[2] + values[3])
-
-    shares = [ref[0:channels, 0:row_count].astype(F32) for ref in refs]
+    out_ref[channels:, 0:row_count] = rows.astype(BF16)
+    out_ref[channels:, row_count:] = jnp.zeros((16, HD), BF16)
+
+
+def velocity_of(a_ref, b_ref):
+    channels = a_ref.shape[0] - 16
+    row_count = a_ref.shape[1] - HD
+    refs = (a_ref, b_ref)
     stats = [ref[channels:, 0:row_count].astype(F32) for ref in refs]
     extras = [ref[0:channels, row_count:].astype(F32) for ref in refs]
     means = [x[0:1] + x[1:2] + x[2:3] for x in stats]
     spreads = [x[3:4] + x[4:5] + x[5:6] for x in stats]
     lifts = [x[:, 0:1] + x[:, 1:2] + x[:, 2:3] for x in extras]
     shifts = [x[:, 3:4] + x[:, 4:5] + x[:, 5:6] for x in extras]
-    mean = tree(means) * (1.0 / N_TENSOR)
+    mean = (means[0] + means[1]) * 0.5
     offsets = [x - mean for x in means]
-    variance = tree(spreads) * (1.0 / D) + tree([x * x for x in offsets]) * (1.0 / N_TENSOR)
-    inv_std = lax.rsqrt(variance + 1e-06)
-    total = tree([s + o * b for s, o, b in zip(shares, offsets, lifts)])
-    velocity = total * inv_std + tree(shifts)
+    variance = (spreads[0] + spreads[1]) * (1.0 / D)
+    variance = variance + (offsets[0] * offsets[0] + offsets[1] * offsets[1]) * 0.5
+    shares = [ref[0:channels, 0:row_count].astype(F32) + o * b for ref, o, b in zip(refs, offsets, lifts)]
+    return (shares[0] + shares[1]) * lax.rsqrt(variance + 1e-06) + (shifts[0] + shifts[1])
+
+
+def finish_kernel(p0, p1, latent_ref, step_ref, velocity_ref, updated_ref):
+    velocity = velocity_of(p0, p1)
     velocity_ref[...] = velocity
     updated_ref[...] = (latent_ref[...] + step_ref[0, 0] * velocity).astype(BF16)
 
@@ -435,7 +473,7 @@
         out_shape=[
             jax.ShapeDtypeStruct((8, width), F32),
             jax.ShapeDtypeStruct((2 * channels, width), BF16),
-            jax.ShapeDtypeStruct((channels, HD), BF16),
+            jax.ShapeDtypeStruct((channels, HD), F32),
         ],
         compiler_params=params(),
         cost_estimate=SMALL,
@@ -443,15 +481,9 @@
     tables = (gate, lifted, extra, step)
 
     core_index, side = tensor_index % 2, tensor_index // 2
-    at = (frame_index - core_index) % PART
-    pair, member = at // 2, at % 2
-    ahead, behind = (pair + 1) % SPREAD_HEADS, (pair + SPREAD_HEADS - 1) % SPREAD_HEADS
     heads = jnp.stack(
         [
-            pair,
-            jnp.where(member == 1, ahead, behind),
-            jnp.where(member == 1, behind, ahead),
-            (pair + 2) % SPREAD_HEADS,
+            *ring_heads(),
             side,
             core_index,
             1 - core_index,
@@ -463,14 +495,15 @@
     in_hbm = pl.BlockSpec(memory_space=pltpu.HBM)
     x1, x2, x3, own_kv, own_q = pl.pallas_call(
         pack_kernel,
-        in_specs=[in_smem] + [in_hbm] * 3,
-        out_specs=[pl.BlockSpec(memory_space=pltpu.VMEM)] * 5,
-        scratch_shapes=[pltpu.VMEM(queries.shape, BF16)] * 3 + [pltpu.SemaphoreType.DMA((3,))],
+        in_specs=[in_hbm] * 3,
+        out_specs=[in_hbm] * 5,
+        scratch_shapes=[pltpu.VMEM(queries.shape, BF16)] * 3
+        + [pltpu.SemaphoreType.DMA((3,)), pltpu.SemaphoreType.DMA((18,))],
         out_shape=[jax.ShapeDtypeStruct((row_count, packed_width), BF16)] * 3
         + [jax.ShapeDtypeStruct((row_count, packed_width), BF16), jax.ShapeDtypeStruct((row_count, 2 * HD), BF16)],
         compiler_params=params(COPY_LIMIT),
         cost_estimate=SMALL,
-    )(heads, queries, keys, values)
+    )(queries, keys, values)
 
     x3 = spread(x3, 3)
     x2 = spread(x2, 2)
@@ -483,7 +516,9 @@
     ]
     far = [peer(far[0], 2), across_both(far[1])]
     own_weight = lax.dynamic_slice(out_weight, (0, side * 2 * width), (depth, 2 * width))
-    x1, x2, x3, partner, own_weight, tables = barrier((x1, x2, x3, partner, own_weight, tables))
+    x1, x2, x3, partner, own_weight, tables, heads = barrier(
+        (x1, x2, x3, partner, own_weight, tables, heads)
+    )
     gate, lifted, extra, step = tables
     far_kv, far_q = pl.pallas_call(
         gather_kernel,
@@ -500,7 +535,7 @@
         cost_estimate=SMALL,
     )(own_q, far_q, own_kv, partner[0])
     state = attend(far_q, own_q, (own_kv, partner[0], far_kv), None, ATTEND_COST)
-    parts[0], state = barrier((parts[0], state))
+    parts[2], state = barrier((parts[2], state))
     parts = [spread(x, i + 1, True) for i, x in enumerate(parts)]
     *results, own_result = attend(far_q, own_q, (swapped,), state, SMALL)
     results, own_result, far = barrier((results, own_result, far))
@@ -538,22 +573,27 @@
         hidden_kernel,
         out_shape=[
             jax.ShapeDtypeStruct((row_count, width), BF16),
-            jax.ShapeDtypeStruct((channels + 16, row_count + HD), BF16),
+            jax.ShapeDtypeStruct((channels + 8, row_count + HD), F32),
         ],
         compiler_params=params(),
         cost_estimate=SMALL,
     )(kept, received, stream_in, gate, lifted, extra)
-    messages = [message] + [peer(message, mask) for mask in (1, 2, 3)]
+    paired = pl.pallas_call(
+        pair_kernel,
+        out_shape=jax.ShapeDtypeStruct((channels + 16, row_count + HD), BF16),
+        compiler_params=params(),
+        cost_estimate=SMALL,
+    )(message, peer(message, 1))
     velocity, updated = pl.pallas_call(
         finish_kernel,
-        in_specs=[pl.BlockSpec(memory_space=pltpu.VMEM)] * 5 + [pl.BlockSpec(memory_space=pltpu.SMEM)],
+        in_specs=[pl.BlockSpec(memory_space=pltpu.VMEM)] * 3 + [in_smem],
         out_shape=[
             jax.ShapeDtypeStruct((channels, row_count), F32),
             jax.ShapeDtypeStruct((channels, row_count), BF16),
         ],
         compiler_params=params(),
         cost_estimate=SMALL,
-    )(*messages, latent.T, step)
+    )(paired, peer(paired, 2), latent.T, step)
     arrived = shifted(updated, "frame", -1).astype(F32)
     queue_next = jnp.where(frame_index == frame_count - 1, new_noise.T, arrived)
     return (stream, velocity.T, queue_next.T)

time: 105 us -> 102 us (0.971)
  starting transfers between devices: 42.3 us -> 39.6 us
  Pallas kernels: 25 us -> 23.5 us
  waiting for transfers between devices: 24.1 us -> 25.4 us
    ppermute x9, starting transfers between devices: 23.9 us -> 22.6 us  [spread(): return lax.ppermute(x, ('frame', 'tensor'), pairs)]
    ppermute x1, starting transfers between devices: 6.15 us -> 4.96 us  [shifted(): return lax.ppermute(x, axis, pairs)]
    pallas_call x1 -> x2, Pallas kernels: 3.21 us -> 2.53 us  [the longest x1 2.41 us: local(): pl.pallas_call(pack_kernel, in_specs=[in_hbm] * 3, out_specs=[in_hbm] * 5...]
    ppermute x9 -> x8, waiting for transfers between devices: 6.17 us -> 6.63 us  [peer(): return lax.ppermute(x, 'tensor', [(i, i ^ mask) for i in range(N_TENSOR)])]
    ppermute x9 -> x8, starting transfers between devices: 7.85 us -> 7.63 us  [peer(): return lax.ppermute(x, 'tensor', [(i, i ^ mask) for i in range(N_TENSOR)])]
    unnamed x26 -> x24, local copies, waits for them, and re-layouts: 2.31 us -> 2.33 us
  transfers between devices with their start and end apart: 22 -> 21, of which waited for: 11 -> 9; matrix products, arithmetic and copies ran while one was open for 7% -> 7% of each run, Pallas kernels for 17% -> 17%
where the time goes in v4:
time: 102 us
  starting transfers between devices  39.6 us (39%)
  waiting for transfers between devices  25.4 us (25%)
  Pallas kernels  23.5 us (23%)
  local copies, waits for them, and re-layouts  8.66 us (8%)
  between operations  2.95 us (3%)
  other arithmetic  1.41 us (1%)
    ppermute x9, starting transfers between devices, spread(): return lax.ppermute(x, ('frame', 'tensor'), pairs)  22.6 us
    ppermute x9, waiting for transfers between devices, spread(): return lax.ppermute(x, ('frame', 'tensor'), pairs)  16.5 us
    pallas_call x2, Pallas kernels, attend(): pl.pallas_call(body, out_shape=out_shape, compiler_params=params(), cost_...  8.1 us
    ppermute x8, starting transfers between devices, peer(): return lax.ppermute(x, 'tensor', [(i, i ^ mask) for i in range(N_TENSOR)])  7.63 us
    ppermute x8, waiting for transfers between devices, peer(): return lax.ppermute(x, 'tensor', [(i, i ^ mask) for i in range(N_TENSOR)])  6.63 us
    pallas_call x4, Pallas kernels, mix(): pl.pallas_call(body, in_specs=[pl.BlockSpec(memory_space=pltpu.SMEM)] + [...  5.91 us
    ppermute x1, starting transfers between devices, shifted(): return lax.ppermute(x, axis, pairs)  4.96 us
    dynamic_slice x1, local copies, waits for them, and re-layouts, local(): lax.dynamic_slice(out_weight, (0, ((1 - side) * 2 + core) * width), (dept...  4.02 us
  transfers between devices with their start and end apart: 21, of which 9 were waited for; matrix products, arithmetic and copies ran while one was open for 7% of the time, Pallas kernels for 17%

profile of v4, /device:TPU:6, one launch (start us, length us, event | category | flops | bytes accessed | tf_op | source)
XLA Modules:
  0.0 101.6 jit_solution(15924275900943576121)
XLA Ops:
  0.6 2.4 %shard_map.130 = (bf16[384,512]{1,0:T(8,128)(2,1)}, bf16[384,512]{1,0:T(8,128)(2,1)}, bf16[384,512]{1,0:T(8,128)(2,1)}, bf16[384,512]{1,0:T(8,128)(2,1)}, bf16[384,256]{1,0:T(8,128)(2,1)}) custom-call(bf16[384,640]{1,0:T(8,128)(2,1)} %q_hbm.1, bf16[384,640]{1,0:T(8,128)(2,1)} %k_hbm.1, bf16[384,640]{1,0:T(8,128)(2,1)} %v_hbm.1), custom_call_target="tpu_custom_call" | custom-call | flops 1000 | bytes 1000 | tf_op jit(solution)/shard_map/pallas_call | solution.py:496
  3.1 2.0 %collective-permute-start.3 = (bf16[384,512]{1,0:T(8,128)(2,1)}, bf16[384,512]{1,0:T(8,128)(2,1)S(1)}, u32[]{:S(2)}, u32[]{:S(2)}) collective-permute-start(bf16[384,512]{1,0:T(8,128)(2,1)} %get-tuple-element.55.kv0.refs_2_), channel_id=1, source_target_pairs={{0,4},{1,29},{2,6},{3,31},{4,0},{5,9},{6,2},{7,11},{8,12},{9,5},{1... | collective-permute-start | bytes 1179656 | tf_op jit(solution)/shard_map/ppermute | solution.py:51
  5.1 4.9 %collective-permute-start = (bf16[384,512]{1,0:T(8,128)(2,1)}, bf16[384,512]{1,0:T(8,128)(2,1)}, u32[]{:S(2)}, u32[]{:S(2)}) collective-permute-start(bf16[384,512]{1,0:T(8,128)(2,1)} %get-tuple-element.52), channel_id=1, source_target_pairs={{0,28},{1,5},{2,30},{3,7},{4,8},{5,1},{6,10},{7,3},{8,4},{9,13},{1... | collective-permute-start | bytes 1179656 | tf_op jit(solution)/shard_map/ppermute | solution.py:41
  10.0 4.6 %collective-permute-start.2 = (bf16[384,512]{1,0:T(8,128)(2,1)}, bf16[384,512]{1,0:T(8,128)(2,1)}, u32[]{:S(2)}, u32[]{:S(2)}) collective-permute-start(bf16[384,512]{1,0:T(8,128)(2,1)} %get-tuple-element.54), channel_id=1, source_target_pairs={{0,20},{1,13},{2,22},{3,15},{4,16},{5,25},{6,18},{7,27},{8,28},{9,... | collective-permute-start | bytes 1179656 | tf_op jit(solution)/shard_map/ppermute | solution.py:41
  15.3 4.0 %constant_dynamic-slice_fusion = (bf16[640,1280]{1,0:T(8,128)(2,1)}, bf16[640,1280]{1,0:T(8,128)(2,1)}) fusion(bf16[640,5120]{1,0:T(8,128)(2,1)} %param.15, s32[]{:T(128)S(6)} %select_n.43, s32[]{:T(128)S(6)} %select_n.42), kind=kLoop, calls=%fused_computation.7 | loop fusion | bytes 6553608 | tf_op jit(solution)/shard_map/dynamic_slice | solution.py:514
  19.3 1.6 %collective-permute-start.5 = (bf16[640,1280]{1,0:T(8,128)(2,1)}, bf16[640,1280]{1,0:T(8,128)(2,1)S(1)}, u32[]{:S(2)}, u32[]{:S(2)}) collective-permute-start(bf16[640,1280]{1,0:T(8,128)(2,1)} %get-tuple-element.104), channel_id=1, source_target_pairs={{0,2},{1,3},{2,0},{3,1},{4,6},{5,7},{6,4},{7,5},{8,10},{9,11},{10,... | collective-permute-start | bytes 4915208 | tf_op jit(solution)/shard_map/ppermute | solution.py:63
  20.9 2.2 %collective-permute-start.6 = (bf16[640,1280]{1,0:T(8,128)(2,1)}, bf16[640,1280]{1,0:T(8,128)(2,1)S(1)}, u32[]{:S(2)}, u32[]{:S(2)}) collective-permute-start(bf16[640,1280]{1,0:T(8,128)(2,1)} %get-tuple-element.103), channel_id=1, source_target_pairs={{0,34},{1,35},{2,32},{3,33},{4,38},{5,39},{6,36},{7,37},{8,42},{9,... | collective-permute-start | bytes 4915208 | tf_op jit(solution)/shard_map/ppermute | solution.py:59
  24.5 1.5 %copy-done = bf16[3,256,1280]{2,1,0:T(8,128)(2,1)S(1)} copy-done((bf16[3,256,1280]{2,1,0:T(8,128)(2,1)S(1)}, bf16[3,256,1280]{2,1,0:T(8,128)(2,1)}, u32[]{:S(2)}) %copy-start) | copy-done | bytes 1966104
  28.1 2.2 %constant_dynamic-slice_fusion.2.refs_2_.refs_6_ = bf16[640,2560]{1,0:T(8,128)(2,1)S(1)} fusion(bf16[640,5120]{1,0:T(8,128)(2,1)} %param.15, s32[]{:T(128)S(6)} %select_n.38), kind=kLoop, calls=%fused_computation.9 | loop fusion | bytes 6553604 | tf_op jit(solution)/shard_map/dynamic_slice | solution.py:518
  30.4 10.4 %collective-permute-done.1.x2_ref = bf16[384,512]{1,0:T(8,128)(2,1)} collective-permute-done((bf16[384,512]{1,0:T(8,128)(2,1)}, bf16[384,512]{1,0:T(8,128)(2,1)}, u32[]{:S(2)}, u32[]{:S(2)}) %collective-permute-start.1) | collective-permute-done | bytes 393248 | tf_op jit(solution)/shard_map/ppermute | solution.py:41
  40.8 1.3 %shard_map.132 = (bf16[1152,256]{1,0:T(8,128)(2,1)S(1)}, bf16[1152,256]{1,0:T(8,128)(2,1)S(1)}) custom-call(bf16[384,512]{1,0:T(8,128)(2,1)} %collective-permute-done.x1_ref, bf16[384,512]{1,0:T(8,128)(2,1)} %collective-permute-done.1.x2_ref, bf16[384,512]{1,0:T(8,128)(2,1)} %collective-permute-done.2.x3_ref), custom_call_target="tpu_custom_call" | custom-call | flops 1000 | bytes 1000 | tf_op jit(solution)/shard_map/pallas_call | solution.py:523
  42.4 2.4 %shard_map.133 = (bf16[416,128]{1,0:T(8,128)(2,1)S(1)}, bf16[416,128]{1,0:T(8,128)(2,1)S(1)}, bf16[416,128]{1,0:T(8,128)(2,1)S(1)}, f32[384,128]{1,0:T(8,128)S(1...) custom-call(bf16[384,256]{1,0:T(8,128)(2,1)S(1)} %copy-done.2, ...), custom_call_target="tpu_custom_call" | custom-call | flops 1000 | bytes 1000 | tf_op jit(solution)/shard_map/pallas_call | solution.py:530
  44.8 4.3 %shard_map.134 = (f32[1536,128]{1,0:T(8,128)S(1)}, f32[1536,128]{1,0:T(8,128)S(1)}, f32[1536,128]{1,0:T(8,128)S(1)}) custom-call(bf16[1152,256]{1,0:T(8,128)(2,1)S(1)} %get-tuple-element.65.far_q_ref.refs_0_, bf16[384,256]{1,0:T(8,128)(2,1)S(1)} %copy-done.2, bf16[384,512]{1,0:T(8,128)(2,1)S(1)} %copy-done.3, bf16[384,512]{1,0:T(8,128)(2,1)S(1)} %copy-done.5, ...), custom_call_target="tpu_custom_call" | custom-call | flops 8999999488 | bytes 1000 | tf_op jit(solution)/shard_map/pallas_call | solution.py:275
  49.2 3.6 %collective-permute-start.15 = (bf16[416,128]{1,0:T(8,128)(2,1)S(1)}, bf16[416,128]{1,0:T(8,128)(2,1)S(1)}, u32[]{:S(2)}, u32[]{:S(2)}) collective-permute-start(bf16[416,128]{1,0:T(8,128)(2,1)S(1)} %get-tuple-element.86), channel_id=1, source_target_pairs={{20,0},{13,1},{22,2},{15,3},{16,4},{25,5},{18,6},{27,7},{28,8},{21... | collective-permute-start | bytes 319496 | tf_op jit(solution)/shard_map/ppermute | solution.py:41
  52.7 1.6 %collective-permute-start.13 = (bf16[416,128]{1,0:T(8,128)(2,1)S(1)}, bf16[416,128]{1,0:T(8,128)(2,1)S(1)}, u32[]{:S(2)}, u32[]{:S(2)}) collective-permute-start(bf16[416,128]{1,0:T(8,128)(2,1)S(1)} %get-tuple-element.84), channel_id=1, source_target_pairs={{28,0},{5,1},{30,2},{7,3},{8,4},{1,5},{10,6},{3,7},{4,8},{13,9},{6... | collective-permute-start | bytes 319496 | tf_op jit(solution)/shard_map/ppermute | solution.py:41
  54.4 2.3 %collective-permute-start.14 = (bf16[416,128]{1,0:T(8,128)(2,1)S(1)}, bf16[416,128]{1,0:T(8,128)(2,1)S(1)}, u32[]{:S(2)}, u32[]{:S(2)}) collective-permute-start(bf16[416,128]{1,0:T(8,128)(2,1)S(1)} %get-tuple-element.85), channel_id=1, source_target_pairs={{8,0},{25,1},{10,2},{27,3},{28,4},{13,5},{30,6},{15,7},{16,8},{1,9... | collective-permute-start | bytes 319496 | tf_op jit(solution)/shard_map/ppermute | solution.py:41
  56.6 3.8 %shard_map.135 = (bf16[384,128]{1,0:T(8,128)(2,1)S(1)}, bf16[384,128]{1,0:T(8,128)(2,1)S(1)}, bf16[384,128]{1,0:T(8,128)(2,1)S(1)}, bf16[384,128]{1,0:T(8,128)(2,1)S(1)}) custom-call(bf16[1152,256]{1,0:T(8,128)(2,1)S(1)} %get-tuple-element.65.far_q_ref.refs_0_, bf16[384,256]{1,0:T(8,128)(2,1)S(1)} %copy-done.2, ...), custom_call_target="tpu_custom_call" | custom-call | flops 1000 | bytes 1000 | tf_op jit(solution)/shard_map/pallas_call | solution.py:275
  61.0 1.4 %collective-permute-done.14.m2 = bf16[416,128]{1,0:T(8,128)(2,1)S(1)} collective-permute-done((bf16[416,128]{1,0:T(8,128)(2,1)S(1)}, bf16[416,128]{1,0:T(8,128)(2,1)S(1)}, u32[]{:S(2)}, u32[]{:S(2)}) %collective-permute-start.14) | collective-permute-done | bytes 106528 | tf_op jit(solution)/shard_map/ppermute | solution.py:41
  62.8 1.7 %collective-permute-start.16 = (bf16[384,256]{1,0:T(8,128)(2,1)S(1)}, bf16[384,256]{1,0:T(8,128)(2,1)S(1)}, u32[]{:S(2)}, u32[]{:S(2)}) collective-permute-start(bf16[384,256]{1,0:T(8,128)(2,1)S(1)} %shard_map.136.refs_1_), channel_id=1, source_target_pairs={{0,2},{1,3},{2,0},{3,1},{4,6},{5,7},{6,4},{7,5},{8,10},{9,11},{10,... | collective-permute-start | bytes 589832 | tf_op jit(solution)/shard_map/ppermute | solution.py:63
  64.5 2.2 %collective-permute-start.9 = (bf16[384,128]{1,0:T(8,128)(2,1)S(1)}, bf16[384,128]{1,0:T(8,128)(2,1)S(1)}, u32[]{:S(2)}, u32[]{:S(2)}) collective-permute-start(bf16[384,128]{1,0:T(8,128)(2,1)S(1)} %get-tuple-element.81), channel_id=1, source_target_pairs={{8,0},{25,1},{10,2},{27,3},{28,4},{13,5},{30,6},{15,7},{16,8},{1,9... | collective-permute-start | bytes 294920 | tf_op jit(solution)/shard_map/ppermute | solution.py:41
  66.7 1.3 %collective-permute-start.11 = (bf16[384,128]{1,0:T(8,128)(2,1)S(1)}, bf16[384,128]{1,0:T(8,128)(2,1)S(1)}, u32[]{:S(2)}, u32[]{:S(2)}) collective-permute-start(bf16[384,128]{1,0:T(8,128)(2,1)S(1)} %get-tuple-element.82), channel_id=1, source_target_pairs={{20,0},{13,1},{22,2},{15,3},{16,4},{25,5},{18,6},{27,7},{28,8},{21... | collective-permute-start | bytes 294920 | tf_op jit(solution)/shard_map/ppermute | solution.py:41
  67.9 2.1 %collective-permute-start.7 = (bf16[384,128]{1,0:T(8,128)(2,1)S(1)}, bf16[384,128]{1,0:T(8,128)(2,1)S(1)}, u32[]{:S(2)}, u32[]{:S(2)}) collective-permute-start(bf16[384,128]{1,0:T(8,128)(2,1)S(1)} %get-tuple-element.80), channel_id=1, source_target_pairs={{28,0},{5,1},{30,2},{7,3},{8,4},{1,5},{10,6},{3,7},{4,8},{13,9},{6... | collective-permute-start | bytes 294920 | tf_op jit(solution)/shard_map/ppermute | solution.py:41
  70.5 4.7 %collective-permute-done.11.refs_5_ = bf16[384,128]{1,0:T(8,128)(2,1)S(1)} collective-permute-done((bf16[384,128]{1,0:T(8,128)(2,1)S(1)}, bf16[384,128]{1,0:T(8,128)(2,1)S(1)}, u32[]{:S(2)}, u32[]{:S(2)}) %collective-permute-start.11) | collective-permute-done | bytes 98336 | tf_op jit(solution)/shard_map/ppermute | solution.py:41
  75.9 1.4 %collective-permute-start.8 = (bf16[384,128]{1,0:T(8,128)(2,1)S(1)}, bf16[384,128]{1,0:T(8,128)(2,1)S(1)}, u32[]{:S(2)}, u32[]{:S(2)}) collective-permute-start(bf16[384,128]{1,0:T(8,128)(2,1)S(1)} %collective-permute-done.7.refs_3_), channel_id=1, source_target_pairs={{0,2},{1,3},{2,0},{3,1},{4,6},{5,7},{6,4},{7,5},{8,10},{9,11},{10,... | collective-permute-start | bytes 294920 | tf_op jit(solution)/shard_map/ppermute | solution.py:63
  77.3 1.7 %shard_map.139.refs_5_ = f32[384,1280]{1,0:T(8,128)S(1)} custom-call(s32[7]{0:T(128)S(1)} %stack.31.refs_0_, bf16[384,256]{1,0:T(8,128)(2,1)S(1)} %shard_map.136.refs_1_, bf16[640,2560]{1,0:T(8,128)(2,1)S(1)} %constant_dynamic-slice_fusion.2.refs_2_.refs_6_, bf16[384,128]{1,0:T(8,128)(2,1)S(1)} %collective-permute-done.7.refs_3_, ...), custom_call_target="tpu_custom_call" | custom-call | flops 1000 | bytes 1000 | tf_op jit(solution)/shard_map/pallas_call | solution.py:349
  80.9 1.2 %shard_map.140 = bf16[384,1280]{1,0:T(8,128)(2,1)S(1)} custom-call(s32[7]{0:T(128)S(1)} %stack.31.refs_0_, bf16[384,128]{1,0:T(8,128)(2,1)S(1)} %collective-permute-done.8.refs_1_, bf16[384,128]{1,0:T(8,128)(2,1)S(1)} %collective-permute-done.10.refs_2_, bf16[384,128]{1,0:T(8,128)(2,1)S(1)} %collective-permute-done.12.refs_3_, ...), custom_call_target="tpu_custom_call" | custom-call | flops 1000 | bytes 1000 | tf_op jit(solution)/shard_map/pallas_call | solution.py:349
  82.5 1.7 %shard_map.137.refs_5_ = f32[384,1280]{1,0:T(8,128)S(1)} custom-call(s32[7]{0:T(128)S(1)} %stack.31.refs_0_, bf16[384,256]{1,0:T(8,128)(2,1)S(1)} %shard_map.136.refs_1_, bf16[640,2560]{1,0:T(8,128)(2,1)S(1)} %constant_dynamic-slice_fusion.2.refs_2_.refs_6_, bf16[384,128]{1,0:T(8,128)(2,1)S(1)} %collective-permute-done.7.refs_3_, ...), custom_call_target="tpu_custom_call" | custom-call | flops 1000 | bytes 1000 | tf_op jit(solution)/shard_map/pallas_call | solution.py:349
  84.2 1.2 %shard_map.138.acc_ref = f32[384,1280]{1,0:T(8,128)S(1)} custom-call(s32[7]{0:T(128)S(1)} %stack.31.refs_0_, bf16[384,128]{1,0:T(8,128)(2,1)S(1)} %collective-permute-done.8.refs_1_, bf16[384,128]{1,0:T(8,128)(2,1)S(1)} %collective-permute-done.10.refs_2_, bf16[384,128]{1,0:T(8,128)(2,1)S(1)} %collective-permute-done.12.refs_3_, ...), custom_call_target="tpu_custom_call" | custom-call | flops 1000 | bytes 1000 | tf_op jit(solution)/shard_map/pallas_call | solution.py:349
  85.5 1.5 %shard_map.141 = (bf16[384,1280]{1,0:T(8,128)(2,1)}, f32[72,512]{1,0:T(8,128)S(1)}) custom-call(f32[384,1280]{1,0:T(8,128)S(1)} %shard_map.138.acc_ref, bf16[384,1280]{1,0:T(8,128)(2,1)S(1)} %collective-permute-done.17.other_ref, bf16[384,1280]{1,0:T(8,128)(2,1)S(1)} %copy-done.1, f32[8,1280]{1,0:T(8,128)S(1)} %get-tuple-element.93.gate_ref, ...), custom_call_target="tpu_custom_call" | custom-call | flops 1000 | bytes 1000 | tf_op jit(solution)/shard_map/pallas_call | solution.py:572
  89.7 3.7 %collective-permute-done.19.p1 = bf16[80,512]{1,0:T(8,128)(2,1)S(1)} collective-permute-done((bf16[80,512]{1,0:T(8,128)(2,1)S(1)}, bf16[80,512]{1,0:T(8,128)(2,1)S(1)}, u32[]{:S(2)}, u32[]{:S(2)}) %collective-permute-start.19) | collective-permute-done | bytes 81952 | tf_op jit(solution)/shard_map/ppermute | solution.py:63
  94.3 5.0 %collective-permute-start.20 = (bf16[64,384]{1,0:T(8,128)(2,1)S(1)}, bf16[64,384]{1,0:T(8,128)(2,1)S(1)}, u32[]{:S(2)}, u32[]{:S(2)}) collective-permute-start(bf16[64,384]{1,0:T(8,128)(2,1)S(1)} %get-tuple-element.100), channel_id=1, source_target_pairs={{4,0},{8,4},{12,8},{16,12},{20,16},{24,20},{28,24},{32,28},{36,32}... | collective-permute-start | bytes 147464 | tf_op jit(solution)/shard_map/ppermute | solution.py:69
  99.2 1.7 %collective-permute-done.20 = bf16[64,384]{1,0:T(8,128)(2,1)S(1)} collective-permute-done((bf16[64,384]{1,0:T(8,128)(2,1)S(1)}, bf16[64,384]{1,0:T(8,128)(2,1)S(1)}, u32[]{:S(2)}, u32[]{:S(2)}) %collective-permute-start.20) | collective-permute-done | bytes 49184 | tf_op jit(solution)/shard_map/ppermute | solution.py:69
  (55 shorter events, 10.9 us)
Async XLA Ops:
  3.1 12.2 %collective-permute-start.3 = (bf16[384,512]{1,0:T(8,128)(2,1)}, bf16[384,512]{1,0:T(8,128)(2,1)S(1)}, u32[]{:S(2)}, u32[]{:S(2)}) collective-permute-start(bf16[384,512]{1,0:T(8,128)(2,1)} %get-tuple-element.55.kv0.refs_2_), channel_id=1, source_target_pairs={{0,4},{1,29},{2,6},{3,31},{4,0},{5,9},{6,2},{7,11},{8,12},{9,5},{1... | collective-permute-start | bytes 1179656 | tf_op jit(solution)/shard_map/ppermute | solution.py:51
  5.1 25.3 %collective-permute-start = (bf16[384,512]{1,0:T(8,128)(2,1)}, bf16[384,512]{1,0:T(8,128)(2,1)}, u32[]{:S(2)}, u32[]{:S(2)}) collective-permute-start(bf16[384,512]{1,0:T(8,128)(2,1)} %get-tuple-element.52), channel_id=1, source_target_pairs={{0,28},{1,5},{2,30},{3,7},{4,8},{5,1},{6,10},{7,3},{8,4},{9,13},{1... | collective-permute-start | bytes 1179656 | tf_op jit(solution)/shard_map/ppermute | solution.py:41
  10.0 30.8 %collective-permute-start.1 = (bf16[384,512]{1,0:T(8,128)(2,1)}, bf16[384,512]{1,0:T(8,128)(2,1)}, u32[]{:S(2)}, u32[]{:S(2)}) collective-permute-start(bf16[384,512]{1,0:T(8,128)(2,1)} %get-tuple-element.53), channel_id=1, source_target_pairs={{0,8},{1,25},{2,10},{3,27},{4,28},{5,13},{6,30},{7,15},{8,16},{9,1... | collective-permute-start | bytes 1179656 | tf_op jit(solution)/shard_map/ppermute | solution.py:41
  10.0 30.8 %collective-permute-start.2 = (bf16[384,512]{1,0:T(8,128)(2,1)}, bf16[384,512]{1,0:T(8,128)(2,1)}, u32[]{:S(2)}, u32[]{:S(2)}) collective-permute-start(bf16[384,512]{1,0:T(8,128)(2,1)} %get-tuple-element.54), channel_id=1, source_target_pairs={{0,20},{1,13},{2,22},{3,15},{4,16},{5,25},{6,18},{7,27},{8,28},{9,... | collective-permute-start | bytes 1179656 | tf_op jit(solution)/shard_map/ppermute | solution.py:41
  15.2 7.8 %copy-start.11 = (s32[129]{0:T(256)S(1)}, s32[129]{0:T(256)}, u32[]{:S(2)}) copy-start(s32[129]{0:T(256)} %param.21) | copy-start | bytes 1552
  15.3 9.3 %copy-start.8 = (bf16[1280,64]{0,1:T(8,128)(2,1)S(1)}, bf16[1280,64]{0,1:T(8,128)(2,1)}, u32[]{:S(2)}) copy-start(bf16[1280,64]{0,1:T(8,128)(2,1)} %param.17) | copy-start | bytes 491524
  15.3 4.0 %copy-start.4 = (bf16[384,512]{1,0:T(8,128)(2,1)}, bf16[384,512]{1,0:T(8,128)(2,1)S(1)}, u32[]{:S(2)}) copy-start(bf16[384,512]{1,0:T(8,128)(2,1)S(1)} %collective-permute-done.3.kv1.refs_3_) | copy-start | bytes 1179652
  19.3 41.1 %collective-permute-start.5 = (bf16[640,1280]{1,0:T(8,128)(2,1)}, bf16[640,1280]{1,0:T(8,128)(2,1)S(1)}, u32[]{:S(2)}, u32[]{:S(2)}) collective-permute-start(bf16[640,1280]{1,0:T(8,128)(2,1)} %get-tuple-element.104), channel_id=1, source_target_pairs={{0,2},{1,3},{2,0},{3,1},{4,6},{5,7},{6,4},{7,5},{8,10},{9,11},{10,... | collective-permute-start | bytes 4915208 | tf_op jit(solution)/shard_map/ppermute | solution.py:63
  20.9 40.1 %collective-permute-start.6 = (bf16[640,1280]{1,0:T(8,128)(2,1)}, bf16[640,1280]{1,0:T(8,128)(2,1)S(1)}, u32[]{:S(2)}, u32[]{:S(2)}) collective-permute-start(bf16[640,1280]{1,0:T(8,128)(2,1)} %get-tuple-element.103), channel_id=1, source_target_pairs={{0,34},{1,35},{2,32},{3,33},{4,38},{5,39},{6,36},{7,37},{8,42},{9,... | collective-permute-start | bytes 4915208 | tf_op jit(solution)/shard_map/ppermute | solution.py:59
  24.5 1.5 %copy-start = (bf16[3,256,1280]{2,1,0:T(8,128)(2,1)S(1)}, bf16[3,256,1280]{2,1,0:T(8,128)(2,1)}, u32[]{:S(2)}) copy-start(bf16[3,256,1280]{2,1,0:T(8,128)(2,1)} %time_ref.1) | copy-start | bytes 5898244
  28.1 14.3 %copy-start.2 = (bf16[384,256]{1,0:T(8,128)(2,1)S(1)}, bf16[384,256]{1,0:T(8,128)(2,1)}, u32[]{:S(2)}) copy-start(bf16[384,256]{1,0:T(8,128)(2,1)} %get-tuple-element.66.own_q_ref.refs_1_) | copy-start | bytes 589828
  28.1 14.3 %copy-start.3 = (bf16[384,512]{1,0:T(8,128)(2,1)S(1)}, bf16[384,512]{1,0:T(8,128)(2,1)}, u32[]{:S(2)}) copy-start(bf16[384,512]{1,0:T(8,128)(2,1)} %get-tuple-element.55.kv0.refs_2_) | copy-start | bytes 1179652
  28.1 14.3 %copy-start.5 = (bf16[384,512]{1,0:T(8,128)(2,1)S(1)}, bf16[384,512]{1,0:T(8,128)(2,1)}, u32[]{:S(2)}) copy-start(bf16[384,512]{1,0:T(8,128)(2,1)} %copy-done.4) | copy-start | bytes 1179652
  42.1 12.3 %collective-permute-start.4 = (bf16[1152,256]{1,0:T(8,128)(2,1)S(1)}, bf16[1152,256]{1,0:T(8,128)(2,1)S(1)}, u32[]{:S(2)}, u32[]{:S(2)}) collective-permute-start(bf16[1152,256]{1,0:T(8,128)(2,1)S(1)} %get-tuple-element.67.refs_4_), channel_id=1, source_target_pairs={{0,4},{1,29},{2,6},{3,31},{4,0},{5,9},{6,2},{7,11},{8,12},{9,5},{1... | collective-permute-start | bytes 1769480 | tf_op jit(solution)/shard_map/ppermute | solution.py:51
  49.2 11.8 %collective-permute-start.15 = (bf16[416,128]{1,0:T(8,128)(2,1)S(1)}, bf16[416,128]{1,0:T(8,128)(2,1)S(1)}, u32[]{:S(2)}, u32[]{:S(2)}) collective-permute-start(bf16[416,128]{1,0:T(8,128)(2,1)S(1)} %get-tuple-element.86), channel_id=1, source_target_pairs={{20,0},{13,1},{22,2},{15,3},{16,4},{25,5},{18,6},{27,7},{28,8},{21... | collective-permute-start | bytes 319496 | tf_op jit(solution)/shard_map/ppermute | solution.py:41
  52.7 8.2 %collective-permute-start.13 = (bf16[416,128]{1,0:T(8,128)(2,1)S(1)}, bf16[416,128]{1,0:T(8,128)(2,1)S(1)}, u32[]{:S(2)}, u32[]{:S(2)}) collective-permute-start(bf16[416,128]{1,0:T(8,128)(2,1)S(1)} %get-tuple-element.84), channel_id=1, source_target_pairs={{28,0},{5,1},{30,2},{7,3},{8,4},{1,5},{10,6},{3,7},{4,8},{13,9},{6... | collective-permute-start | bytes 319496 | tf_op jit(solution)/shard_map/ppermute | solution.py:41
  54.4 8.0 %collective-permute-start.14 = (bf16[416,128]{1,0:T(8,128)(2,1)S(1)}, bf16[416,128]{1,0:T(8,128)(2,1)S(1)}, u32[]{:S(2)}, u32[]{:S(2)}) collective-permute-start(bf16[416,128]{1,0:T(8,128)(2,1)S(1)} %get-tuple-element.85), channel_id=1, source_target_pairs={{8,0},{25,1},{10,2},{27,3},{28,4},{13,5},{30,6},{15,7},{16,8},{1,9... | collective-permute-start | bytes 319496 | tf_op jit(solution)/shard_map/ppermute | solution.py:41
  62.8 14.4 %collective-permute-start.16 = (bf16[384,256]{1,0:T(8,128)(2,1)S(1)}, bf16[384,256]{1,0:T(8,128)(2,1)S(1)}, u32[]{:S(2)}, u32[]{:S(2)}) collective-permute-start(bf16[384,256]{1,0:T(8,128)(2,1)S(1)} %shard_map.136.refs_1_), channel_id=1, source_target_pairs={{0,2},{1,3},{2,0},{3,1},{4,6},{5,7},{6,4},{7,5},{8,10},{9,11},{10,... | collective-permute-start | bytes 589832 | tf_op jit(solution)/shard_map/ppermute | solution.py:63
  64.5 5.6 %collective-permute-start.9 = (bf16[384,128]{1,0:T(8,128)(2,1)S(1)}, bf16[384,128]{1,0:T(8,128)(2,1)S(1)}, u32[]{:S(2)}, u32[]{:S(2)}) collective-permute-start(bf16[384,128]{1,0:T(8,128)(2,1)S(1)} %get-tuple-element.81), channel_id=1, source_target_pairs={{8,0},{25,1},{10,2},{27,3},{28,4},{13,5},{30,6},{15,7},{16,8},{1,9... | collective-permute-start | bytes 294920 | tf_op jit(solution)/shard_map/ppermute | solution.py:41
  66.7 8.6 %collective-permute-start.11 = (bf16[384,128]{1,0:T(8,128)(2,1)S(1)}, bf16[384,128]{1,0:T(8,128)(2,1)S(1)}, u32[]{:S(2)}, u32[]{:S(2)}) collective-permute-start(bf16[384,128]{1,0:T(8,128)(2,1)S(1)} %get-tuple-element.82), channel_id=1, source_target_pairs={{20,0},{13,1},{22,2},{15,3},{16,4},{25,5},{18,6},{27,7},{28,8},{21... | collective-permute-start | bytes 294920 | tf_op jit(solution)/shard_map/ppermute | solution.py:41
  67.9 8.0 %collective-permute-start.7 = (bf16[384,128]{1,0:T(8,128)(2,1)S(1)}, bf16[384,128]{1,0:T(8,128)(2,1)S(1)}, u32[]{:S(2)}, u32[]{:S(2)}) collective-permute-start(bf16[384,128]{1,0:T(8,128)(2,1)S(1)} %get-tuple-element.80), channel_id=1, source_target_pairs={{28,0},{5,1},{30,2},{7,3},{8,4},{1,5},{10,6},{3,7},{4,8},{13,9},{6... | collective-permute-start | bytes 294920 | tf_op jit(solution)/shard_map/ppermute | solution.py:41
  70.1 8.9 %collective-permute-start.10 = (bf16[384,128]{1,0:T(8,128)(2,1)S(1)}, bf16[384,128]{1,0:T(8,128)(2,1)S(1)}, u32[]{:S(2)}, u32[]{:S(2)}) collective-permute-start(bf16[384,128]{1,0:T(8,128)(2,1)S(1)} %collective-permute-done.9.refs_4_), channel_id=1, source_target_pairs={{0,2},{1,3},{2,0},{3,1},{4,6},{5,7},{6,4},{7,5},{8,10},{9,11},{10,... | collective-permute-start | bytes 294920 | tf_op jit(solution)/shard_map/ppermute | solution.py:63
  75.2 4.6 %collective-permute-start.12 = (bf16[384,128]{1,0:T(8,128)(2,1)S(1)}, bf16[384,128]{1,0:T(8,128)(2,1)S(1)}, u32[]{:S(2)}, u32[]{:S(2)}) collective-permute-start(bf16[384,128]{1,0:T(8,128)(2,1)S(1)} %collective-permute-done.11.refs_5_), channel_id=1, source_target_pairs={{0,2},{1,3},{2,0},{3,1},{4,6},{5,7},{6,4},{7,5},{8,10},{9,11},{10,... | collective-permute-start | bytes 294920 | tf_op jit(solution)/shard_map/ppermute | solution.py:63
  75.9 5.0 %collective-permute-start.8 = (bf16[384,128]{1,0:T(8,128)(2,1)S(1)}, bf16[384,128]{1,0:T(8,128)(2,1)S(1)}, u32[]{:S(2)}, u32[]{:S(2)}) collective-permute-start(bf16[384,128]{1,0:T(8,128)(2,1)S(1)} %collective-permute-done.7.refs_3_), channel_id=1, source_target_pairs={{0,2},{1,3},{2,0},{3,1},{4,6},{5,7},{6,4},{7,5},{8,10},{9,11},{10,... | collective-permute-start | bytes 294920 | tf_op jit(solution)/shard_map/ppermute | solution.py:63
  82.1 3.4 %collective-permute-start.17 = (bf16[384,1280]{1,0:T(8,128)(2,1)S(1)}, bf16[384,1280]{1,0:T(8,128)(2,1)S(1)}, u32[]{:S(2)}, u32[]{:S(2)}) collective-permute-start(bf16[384,1280]{1,0:T(8,128)(2,1)S(1)} %shard_map.140), channel_id=1, source_target_pairs={{0,1},{1,0},{2,3},{3,2},{4,5},{5,4},{6,7},{7,6},{8,9},{9,8},{10,11... | collective-permute-start | bytes 2949128 | tf_op jit(solution)/shard_map/ppermute | solution.py:63
  84.2 1.3 %copy-start.1 = (bf16[384,1280]{1,0:T(8,128)(2,1)S(1)}, bf16[384,1280]{1,0:T(8,128)(2,1)}, u32[]{:S(2)}) copy-start(bf16[384,1280]{1,0:T(8,128)(2,1)} %in_ref.1) | copy-start | bytes 2949124
  84.2 1.3 %copy-start.7 = (bf16[128,1280]{1,0:T(8,128)(2,1)S(1)}, bf16[128,1280]{1,0:T(8,128)(2,1)}, u32[]{:S(2)}) copy-start(bf16[128,1280]{1,0:T(8,128)(2,1)} %copy-done.6) | copy-start | bytes 983044
  85.5 8.0 %copy-start.9 = (f32[384,64]{0,1:T(8,128)S(1)}, f32[384,64]{0,1:T(8,128)}, u32[]{:S(2)}) copy-start(f32[384,64]{0,1:T(8,128)} %param.18) | copy-start | bytes 294916
  85.5 15.5 %copy-start.10 = (f32[384,64]{0,1:T(8,128)S(1)}, f32[384,64]{0,1:T(8,128)}, u32[]{:S(2)}) copy-start(f32[384,64]{0,1:T(8,128)} %param.19) | copy-start | bytes 294916
  87.0 1.5 %collective-permute-start.18 = (f32[72,512]{1,0:T(8,128)S(1)}, f32[72,512]{1,0:T(8,128)S(1)}, u32[]{:S(2)}, u32[]{:S(2)}) collective-permute-start(f32[72,512]{1,0:T(8,128)S(1)} %get-tuple-element.97.a_ref), channel_id=1, source_target_pairs={{0,1},{1,0},{2,3},{3,2},{4,5},{5,4},{6,7},{7,6},{8,9},{9,8},{10,11... | collective-permute-start | bytes 442376 | tf_op jit(solution)/shard_map/ppermute | solution.py:63
  88.6 4.8 %collective-permute-start.19 = (bf16[80,512]{1,0:T(8,128)(2,1)S(1)}, bf16[80,512]{1,0:T(8,128)(2,1)S(1)}, u32[]{:S(2)}, u32[]{:S(2)}) collective-permute-start(bf16[80,512]{1,0:T(8,128)(2,1)S(1)} %shard_map.142.p0), channel_id=1, source_target_pairs={{0,2},{1,3},{2,0},{3,1},{4,6},{5,7},{6,4},{7,5},{8,10},{9,11},{10,... | collective-permute-start | bytes 245768 | tf_op jit(solution)/shard_map/ppermute | solution.py:63
  94.3 6.7 %collective-permute-start.20 = (bf16[64,384]{1,0:T(8,128)(2,1)S(1)}, bf16[64,384]{1,0:T(8,128)(2,1)S(1)}, u32[]{:S(2)}, u32[]{:S(2)}) collective-permute-start(bf16[64,384]{1,0:T(8,128)(2,1)S(1)} %get-tuple-element.100), channel_id=1, source_target_pairs={{4,0},{8,4},{12,8},{16,12},{20,16},{24,20},{28,24},{32,28},{36,32}... | collective-permute-start | bytes 147464 | tf_op jit(solution)/shard_map/ppermute | solution.py:69
  (1 other events, 0.7 us)

commit v5 on v4

--- a/solution.py
+++ b/solution.py
@@ -551,7 +551,8 @@
     for at in (0, 1, 2):
         back_across[at] = peer(back[at], 2)
     mine_across = peer(mine, 2)
-    mine_rows, back_rows = (0, None), (1, 2, 3)
+    back, back_across = [[x[at] for at in (0, 2, 1)] for x in (back, back_across)]
+    mine_rows, back_rows = (0, None), (1, 3, 2)
     sums = [
         mix(
             heads,
@@ -559,14 +560,22 @@
             [
                 ([mine], [own_weight], mine_rows, column),
                 (back, [own_weight], back_rows, column),
-                ([mine_across], [weight], mine_rows, None),
             ],
             F32,
         )
-        for column, weight in ((6, far[1]), (5, far[0]))
+        for column in (6, 5)
     ]
-    sent = mix(heads, width, [(back_across, [far[1]], back_rows, None)], BF16, sums[0])
-    kept = mix(heads, width, [(back_across, [far[0]], back_rows, None)], F32, sums[1])
+    sums = barrier(sums)
+    sent, kept = [
+        mix(
+            heads,
+            width,
+            [(back_across, [weight], back_rows, None), ([mine_across], [weight], mine_rows, None)],
+            out_dtype,
+            base,
+        )
+        for weight, out_dtype, base in ((far[1], BF16, sums[0]), (far[0], F32, sums[1]))
+    ]
     received = peer(sent, 1)
 
     stream, message = pl.pallas_call(

time: 102 us -> 98.9 us (0.970)
  waiting for transfers between devices: 25.4 us -> 23.2 us
    ppermute x9, waiting for transfers between devices: 16.5 us -> 13.8 us  [spread(): return lax.ppermute(x, ('frame', 'tensor'), pairs)]
  transfers between devices with their start and end apart: 21 -> 21, of which waited for: 9 -> 9; matrix products, arithmetic and copies ran while one was open for 7% -> 7% of each run, Pallas kernels for 17% -> 18%
where the time goes in v5:
time: 98.9 us; the launch traced here: 98.7 us
  starting transfers between devices  38.7 us (39%)
  Pallas kernels  23.8 us (24%)
  waiting for transfers between devices  23.2 us (23%)
  local copies, waits for them, and re-layouts  8.66 us (9%)
  between operations  2.97 us (3%)
  other arithmetic  1.42 us (1%)
    ppermute x9, starting transfers between devices, spread(): return lax.ppermute(x, ('frame', 'tensor'), pairs)  23.4 us
    ppermute x9, waiting for transfers between devices, spread(): return lax.ppermute(x, ('frame', 'tensor'), pairs)  13.8 us
    pallas_call x2, Pallas kernels, attend(): pl.pallas_call(body, out_shape=out_shape, compiler_params=params(), cost_...  8.52 us
    ppermute x8, waiting for transfers between devices, peer(): return lax.ppermute(x, 'tensor', [(i, i ^ mask) for i in range(N_TENSOR)])  6.96 us
    ppermute x8, starting transfers between devices, peer(): return lax.ppermute(x, 'tensor', [(i, i ^ mask) for i in range(N_TENSOR)])  6.67 us
    pallas_call x4, Pallas kernels, mix(): pl.pallas_call(body, in_specs=[pl.BlockSpec(memory_space=pltpu.SMEM)] + [...  5.86 us
    ppermute x1, starting transfers between devices, shifted(): return lax.ppermute(x, axis, pairs)  4.09 us
    dynamic_slice x1, local copies, waits for them, and re-layouts, local(): lax.dynamic_slice(out_weight, (0, ((1 - side) * 2 + core) * width), (dept...  4.02 us
  transfers between devices with their start and end apart: 21, of which 9 were waited for; matrix products, arithmetic and copies ran while one was open for 7% of the time, Pallas kernels for 18%

profile of v5, /device:TPU:6, one launch (start us, length us, event | category | flops | bytes accessed | tf_op | source)
XLA Modules:
  0.0 98.7 jit_solution(9370204402518794859)
XLA Ops:
  0.6 2.4 %shard_map.130 = (bf16[384,512]{1,0:T(8,128)(2,1)}, bf16[384,512]{1,0:T(8,128)(2,1)}, bf16[384,512]{1,0:T(8,128)(2,1)}, bf16[384,512]{1,0:T(8,128)(2,1)}, bf16[384,256]{1,0:T(8,128)(2,1)}) custom-call(bf16[384,640]{1,0:T(8,128)(2,1)} %q_hbm.1, bf16[384,640]{1,0:T(8,128)(2,1)} %k_hbm.1, bf16[384,640]{1,0:T(8,128)(2,1)} %v_hbm.1), custom_call_target="tpu_custom_call" | custom-call | flops 1000 | bytes 1000 | tf_op jit(solution)/shard_map/pallas_call | solution.py:496
  3.1 2.0 %collective-permute-start.3 = (bf16[384,512]{1,0:T(8,128)(2,1)}, bf16[384,512]{1,0:T(8,128)(2,1)S(1)}, u32[]{:S(2)}, u32[]{:S(2)}) collective-permute-start(bf16[384,512]{1,0:T(8,128)(2,1)} %get-tuple-element.57.kv0.refs_2_), channel_id=1, source_target_pairs={{0,4},{1,29},{2,6},{3,31},{4,0},{5,9},{6,2},{7,11},{8,12},{9,5},{1... | collective-permute-start | bytes 1179656 | tf_op jit(solution)/shard_map/ppermute | solution.py:51
  5.1 4.9 %collective-permute-start = (bf16[384,512]{1,0:T(8,128)(2,1)}, bf16[384,512]{1,0:T(8,128)(2,1)}, u32[]{:S(2)}, u32[]{:S(2)}) collective-permute-start(bf16[384,512]{1,0:T(8,128)(2,1)} %get-tuple-element.54), channel_id=1, source_target_pairs={{0,28},{1,5},{2,30},{3,7},{4,8},{5,1},{6,10},{7,3},{8,4},{9,13},{1... | collective-permute-start | bytes 1179656 | tf_op jit(solution)/shard_map/ppermute | solution.py:41
  10.0 4.6 %collective-permute-start.2 = (bf16[384,512]{1,0:T(8,128)(2,1)}, bf16[384,512]{1,0:T(8,128)(2,1)}, u32[]{:S(2)}, u32[]{:S(2)}) collective-permute-start(bf16[384,512]{1,0:T(8,128)(2,1)} %get-tuple-element.56), channel_id=1, source_target_pairs={{0,20},{1,13},{2,22},{3,15},{4,16},{5,25},{6,18},{7,27},{8,28},{9,... | collective-permute-start | bytes 1179656 | tf_op jit(solution)/shard_map/ppermute | solution.py:41
  15.3 4.0 %constant_dynamic-slice_fusion = (bf16[640,1280]{1,0:T(8,128)(2,1)}, bf16[640,1280]{1,0:T(8,128)(2,1)}) fusion(bf16[640,5120]{1,0:T(8,128)(2,1)} %param.15, s32[]{:T(128)S(6)} %select_n.43, s32[]{:T(128)S(6)} %select_n.42), kind=kLoop, calls=%fused_computation.7 | loop fusion | bytes 6553608 | tf_op jit(solution)/shard_map/dynamic_slice | solution.py:514
  19.3 1.6 %collective-permute-start.5 = (bf16[640,1280]{1,0:T(8,128)(2,1)}, bf16[640,1280]{1,0:T(8,128)(2,1)S(1)}, u32[]{:S(2)}, u32[]{:S(2)}) collective-permute-start(bf16[640,1280]{1,0:T(8,128)(2,1)} %get-tuple-element.108), channel_id=1, source_target_pairs={{0,2},{1,3},{2,0},{3,1},{4,6},{5,7},{6,4},{7,5},{8,10},{9,11},{10,... | collective-permute-start | bytes 4915208 | tf_op jit(solution)/shard_map/ppermute | solution.py:63
  20.9 2.2 %collective-permute-start.6 = (bf16[640,1280]{1,0:T(8,128)(2,1)}, bf16[640,1280]{1,0:T(8,128)(2,1)S(1)}, u32[]{:S(2)}, u32[]{:S(2)}) collective-permute-start(bf16[640,1280]{1,0:T(8,128)(2,1)} %get-tuple-element.107), channel_id=1, source_target_pairs={{0,34},{1,35},{2,32},{3,33},{4,38},{5,39},{6,36},{7,37},{8,42},{9,... | collective-permute-start | bytes 4915208 | tf_op jit(solution)/shard_map/ppermute | solution.py:59
  24.5 1.5 %copy-done = bf16[3,256,1280]{2,1,0:T(8,128)(2,1)S(1)} copy-done((bf16[3,256,1280]{2,1,0:T(8,128)(2,1)S(1)}, bf16[3,256,1280]{2,1,0:T(8,128)(2,1)}, u32[]{:S(2)}) %copy-start) | copy-done | bytes 1966104
  28.1 2.2 %constant_dynamic-slice_fusion.2.refs_2_.refs_6_ = bf16[640,2560]{1,0:T(8,128)(2,1)S(1)} fusion(bf16[640,5120]{1,0:T(8,128)(2,1)} %param.15, s32[]{:T(128)S(6)} %select_n.38), kind=kLoop, calls=%fused_computation.9 | loop fusion | bytes 6553604 | tf_op jit(solution)/shard_map/dynamic_slice | solution.py:518
  30.4 10.4 %collective-permute-done.1.x2_ref = bf16[384,512]{1,0:T(8,128)(2,1)} collective-permute-done((bf16[384,512]{1,0:T(8,128)(2,1)}, bf16[384,512]{1,0:T(8,128)(2,1)}, u32[]{:S(2)}, u32[]{:S(2)}) %collective-permute-start.1) | collective-permute-done | bytes 393248 | tf_op jit(solution)/shard_map/ppermute | solution.py:41
  40.8 1.3 %shard_map.132 = (bf16[1152,256]{1,0:T(8,128)(2,1)S(1)}, bf16[1152,256]{1,0:T(8,128)(2,1)S(1)}) custom-call(bf16[384,512]{1,0:T(8,128)(2,1)} %collective-permute-done.x1_ref, bf16[384,512]{1,0:T(8,128)(2,1)} %collective-permute-done.1.x2_ref, bf16[384,512]{1,0:T(8,128)(2,1)} %collective-permute-done.2.x3_ref), custom_call_target="tpu_custom_call" | custom-call | flops 1000 | bytes 1000 | tf_op jit(solution)/shard_map/pallas_call | solution.py:523
  42.4 2.4 %shard_map.133 = (bf16[416,128]{1,0:T(8,128)(2,1)S(1)}, bf16[416,128]{1,0:T(8,128)(2,1)S(1)}, bf16[416,128]{1,0:T(8,128)(2,1)S(1)}, f32[384,128]{1,0:T(8,128)S(1...) custom-call(bf16[384,256]{1,0:T(8,128)(2,1)S(1)} %copy-done.2, ...), custom_call_target="tpu_custom_call" | custom-call | flops 1000 | bytes 1000 | tf_op jit(solution)/shard_map/pallas_call | solution.py:530
  44.8 4.6 %shard_map.134 = (f32[1536,128]{1,0:T(8,128)S(1)}, f32[1536,128]{1,0:T(8,128)S(1)}, f32[1536,128]{1,0:T(8,128)S(1)}) custom-call(bf16[1152,256]{1,0:T(8,128)(2,1)S(1)} %get-tuple-element.67.far_q_ref.refs_0_, bf16[384,256]{1,0:T(8,128)(2,1)S(1)} %copy-done.2, bf16[384,512]{1,0:T(8,128)(2,1)S(1)} %copy-done.3, bf16[384,512]{1,0:T(8,128)(2,1)S(1)} %copy-done.5, ...), custom_call_target="tpu_custom_call" | custom-call | flops 8999999488 | bytes 1000 | tf_op jit(solution)/shard_map/pallas_call | solution.py:275
  49.4 3.6 %collective-permute-start.15 = (bf16[416,128]{1,0:T(8,128)(2,1)S(1)}, bf16[416,128]{1,0:T(8,128)(2,1)S(1)}, u32[]{:S(2)}, u32[]{:S(2)}) collective-permute-start(bf16[416,128]{1,0:T(8,128)(2,1)S(1)} %get-tuple-element.88), channel_id=1, source_target_pairs={{20,0},{13,1},{22,2},{15,3},{16,4},{25,5},{18,6},{27,7},{28,8},{21... | collective-permute-start | bytes 319496 | tf_op jit(solution)/shard_map/ppermute | solution.py:41
  52.9 1.6 %collective-permute-start.13 = (bf16[416,128]{1,0:T(8,128)(2,1)S(1)}, bf16[416,128]{1,0:T(8,128)(2,1)S(1)}, u32[]{:S(2)}, u32[]{:S(2)}) collective-permute-start(bf16[416,128]{1,0:T(8,128)(2,1)S(1)} %get-tuple-element.86), channel_id=1, source_target_pairs={{28,0},{5,1},{30,2},{7,3},{8,4},{1,5},{10,6},{3,7},{4,8},{13,9},{6... | collective-permute-start | bytes 319496 | tf_op jit(solution)/shard_map/ppermute | solution.py:41
  54.6 1.8 %collective-permute-start.14 = (bf16[416,128]{1,0:T(8,128)(2,1)S(1)}, bf16[416,128]{1,0:T(8,128)(2,1)S(1)}, u32[]{:S(2)}, u32[]{:S(2)}) collective-permute-start(bf16[416,128]{1,0:T(8,128)(2,1)S(1)} %get-tuple-element.87), channel_id=1, source_target_pairs={{8,0},{25,1},{10,2},{27,3},{28,4},{13,5},{30,6},{15,7},{16,8},{1,9... | collective-permute-start | bytes 319496 | tf_op jit(solution)/shard_map/ppermute | solution.py:41
  56.4 4.0 %shard_map.135 = (bf16[384,128]{1,0:T(8,128)(2,1)S(1)}, bf16[384,128]{1,0:T(8,128)(2,1)S(1)}, bf16[384,128]{1,0:T(8,128)(2,1)S(1)}, bf16[384,128]{1,0:T(8,128)(2,1)S(1)}) custom-call(bf16[1152,256]{1,0:T(8,128)(2,1)S(1)} %get-tuple-element.67.far_q_ref.refs_0_, bf16[384,256]{1,0:T(8,128)(2,1)S(1)} %copy-done.2, ...), custom_call_target="tpu_custom_call" | custom-call | flops 1000 | bytes 1000 | tf_op jit(solution)/shard_map/pallas_call | solution.py:275
  61.0 1.9 %collective-permute-start.11 = (bf16[384,128]{1,0:T(8,128)(2,1)S(1)}, bf16[384,128]{1,0:T(8,128)(2,1)S(1)}, u32[]{:S(2)}, u32[]{:S(2)}) collective-permute-start(bf16[384,128]{1,0:T(8,128)(2,1)S(1)} %get-tuple-element.84), channel_id=1, source_target_pairs={{8,0},{25,1},{10,2},{27,3},{28,4},{13,5},{30,6},{15,7},{16,8},{1,9... | collective-permute-start | bytes 294920 | tf_op jit(solution)/shard_map/ppermute | solution.py:41
  62.9 4.4 %collective-permute-start.9 = (bf16[384,128]{1,0:T(8,128)(2,1)S(1)}, bf16[384,128]{1,0:T(8,128)(2,1)S(1)}, u32[]{:S(2)}, u32[]{:S(2)}) collective-permute-start(bf16[384,128]{1,0:T(8,128)(2,1)S(1)} %get-tuple-element.83), channel_id=1, source_target_pairs={{20,0},{13,1},{22,2},{15,3},{16,4},{25,5},{18,6},{27,7},{28,8},{21... | collective-permute-start | bytes 294920 | tf_op jit(solution)/shard_map/ppermute | solution.py:41
  68.4 2.8 %collective-permute-done.9.refs_4_ = bf16[384,128]{1,0:T(8,128)(2,1)S(1)} collective-permute-done((bf16[384,128]{1,0:T(8,128)(2,1)S(1)}, bf16[384,128]{1,0:T(8,128)(2,1)S(1)}, u32[]{:S(2)}, u32[]{:S(2)}) %collective-permute-start.9) | collective-permute-done | bytes 98336 | tf_op jit(solution)/shard_map/ppermute | solution.py:41
  71.7 1.5 %collective-permute-start.12 = (bf16[384,128]{1,0:T(8,128)(2,1)S(1)}, bf16[384,128]{1,0:T(8,128)(2,1)S(1)}, u32[]{:S(2)}, u32[]{:S(2)}) collective-permute-start(bf16[384,128]{1,0:T(8,128)(2,1)S(1)} %collective-permute-done.11.refs_5_), channel_id=1, source_target_pairs={{0,2},{1,3},{2,0},{3,1},{4,6},{5,7},{6,4},{7,5},{8,10},{9,11},{10,... | collective-permute-start | bytes 294920 | tf_op jit(solution)/shard_map/ppermute | solution.py:63
  73.8 1.9 %collective-permute-start.8 = (bf16[384,128]{1,0:T(8,128)(2,1)S(1)}, bf16[384,128]{1,0:T(8,128)(2,1)S(1)}, u32[]{:S(2)}, u32[]{:S(2)}) collective-permute-start(bf16[384,128]{1,0:T(8,128)(2,1)S(1)} %collective-permute-done.7.refs_3_), channel_id=1, source_target_pairs={{0,2},{1,3},{2,0},{3,1},{4,6},{5,7},{6,4},{7,5},{8,10},{9,11},{10,... | collective-permute-start | bytes 294920 | tf_op jit(solution)/shard_map/ppermute | solution.py:63
  75.7 1.5 %shard_map.138.refs_7_ = f32[384,1280]{1,0:T(8,128)S(1)} custom-call(s32[7]{0:T(128)S(1)} %stack.31.refs_0_, bf16[384,256]{1,0:T(8,128)(2,1)S(1)} %shard_map.136.refs_1_, bf16[640,2560]{1,0:T(8,128)(2,1)S(1)} %constant_dynamic-slice_fusion.2.refs_2_.refs_6_, bf16[384,128]{1,0:T(8,128)(2,1)S(1)} %collective-permute-done.7.refs_3_, ...), custom_call_target="tpu_custom_call" | custom-call | flops 1000 | bytes 1000 | tf_op jit(solution)/shard_map/pallas_call | solution.py:349
  77.2 1.5 %shard_map.137.refs_7_ = f32[384,1280]{1,0:T(8,128)S(1)} custom-call(s32[7]{0:T(128)S(1)} %stack.31.refs_0_, bf16[384,256]{1,0:T(8,128)(2,1)S(1)} %shard_map.136.refs_1_, bf16[640,2560]{1,0:T(8,128)(2,1)S(1)} %constant_dynamic-slice_fusion.2.refs_2_.refs_6_, bf16[384,128]{1,0:T(8,128)(2,1)S(1)} %collective-permute-done.7.refs_3_, ...), custom_call_target="tpu_custom_call" | custom-call | flops 1000 | bytes 1000 | tf_op jit(solution)/shard_map/pallas_call | solution.py:349
  79.6 1.5 %shard_map.140 = bf16[384,1280]{1,0:T(8,128)(2,1)S(1)} custom-call(s32[7]{0:T(128)S(1)} %stack.31.refs_0_, bf16[384,128]{1,0:T(8,128)(2,1)S(1)} %collective-permute-done.8.refs_1_, bf16[384,128]{1,0:T(8,128)(2,1)S(1)} %collective-permute-done.10.refs_2_, bf16[384,128]{1,0:T(8,128)(2,1)S(1)} %collective-permute-done.12.refs_3_, ...), custom_call_target="tpu_custom_call" | custom-call | flops 1000 | bytes 1000 | tf_op jit(solution)/shard_map/pallas_call | solution.py:349
  81.2 1.5 %shard_map.139.acc_ref = f32[384,1280]{1,0:T(8,128)S(1)} custom-call(s32[7]{0:T(128)S(1)} %stack.31.refs_0_, bf16[384,128]{1,0:T(8,128)(2,1)S(1)} %collective-permute-done.8.refs_1_, bf16[384,128]{1,0:T(8,128)(2,1)S(1)} %collective-permute-done.10.refs_2_, bf16[384,128]{1,0:T(8,128)(2,1)S(1)} %collective-permute-done.12.refs_3_, ...), custom_call_target="tpu_custom_call" | custom-call | flops 1000 | bytes 1000 | tf_op jit(solution)/shard_map/pallas_call | solution.py:349
  82.7 1.0 %collective-permute-done.17.other_ref = bf16[384,1280]{1,0:T(8,128)(2,1)S(1)} collective-permute-done((bf16[384,1280]{1,0:T(8,128)(2,1)S(1)}, bf16[384,1280]{1,0:T(8,128)(2,1)S(1)}, u32[]{:S(2)}, u32[]{:S(2)}) %collective-permute-start.17) | collective-permute-done | bytes 983072 | tf_op jit(solution)/shard_map/ppermute | solution.py:63
  83.7 1.5 %shard_map.141 = (bf16[384,1280]{1,0:T(8,128)(2,1)}, f32[72,512]{1,0:T(8,128)S(1)}) custom-call(f32[384,1280]{1,0:T(8,128)S(1)} %shard_map.139.acc_ref, bf16[384,1280]{1,0:T(8,128)(2,1)S(1)} %collective-permute-done.17.other_ref, bf16[384,1280]{1,0:T(8,128)(2,1)S(1)} %copy-done.1, f32[8,1280]{1,0:T(8,128)S(1)} %get-tuple-element.97.gate_ref, ...), custom_call_target="tpu_custom_call" | custom-call | flops 1000 | bytes 1000 | tf_op jit(solution)/shard_map/pallas_call | solution.py:581
  85.3 1.2 %collective-permute-done.18.b_ref = f32[72,512]{1,0:T(8,128)S(1)} collective-permute-done((f32[72,512]{1,0:T(8,128)S(1)}, f32[72,512]{1,0:T(8,128)S(1)}, u32[]{:S(2)}, u32[]{:S(2)}) %collective-permute-start.18) | collective-permute-done | bytes 147488 | tf_op jit(solution)/shard_map/ppermute | solution.py:63
  87.5 3.8 %collective-permute-done.19.p1 = bf16[80,512]{1,0:T(8,128)(2,1)S(1)} collective-permute-done((bf16[80,512]{1,0:T(8,128)(2,1)S(1)}, bf16[80,512]{1,0:T(8,128)(2,1)S(1)}, u32[]{:S(2)}, u32[]{:S(2)}) %collective-permute-start.19) | collective-permute-done | bytes 81952 | tf_op jit(solution)/shard_map/ppermute | solution.py:63
  92.1 4.1 %collective-permute-start.20 = (bf16[64,384]{1,0:T(8,128)(2,1)S(1)}, bf16[64,384]{1,0:T(8,128)(2,1)S(1)}, u32[]{:S(2)}, u32[]{:S(2)}) collective-permute-start(bf16[64,384]{1,0:T(8,128)(2,1)S(1)} %get-tuple-element.104), channel_id=1, source_target_pairs={{4,0},{8,4},{12,8},{16,12},{20,16},{24,20},{28,24},{32,28},{36,32}... | collective-permute-start | bytes 147464 | tf_op jit(solution)/shard_map/ppermute | solution.py:69
  96.2 1.9 %collective-permute-done.20 = bf16[64,384]{1,0:T(8,128)(2,1)S(1)} collective-permute-done((bf16[64,384]{1,0:T(8,128)(2,1)S(1)}, bf16[64,384]{1,0:T(8,128)(2,1)S(1)}, u32[]{:S(2)}, u32[]{:S(2)}) %collective-permute-start.20) | collective-permute-done | bytes 49184 | tf_op jit(solution)/shard_map/ppermute | solution.py:69
  (55 shorter events, 8.7 us)
Async XLA Ops:
  3.1 12.2 %collective-permute-start.3 = (bf16[384,512]{1,0:T(8,128)(2,1)}, bf16[384,512]{1,0:T(8,128)(2,1)S(1)}, u32[]{:S(2)}, u32[]{:S(2)}) collective-permute-start(bf16[384,512]{1,0:T(8,128)(2,1)} %get-tuple-element.57.kv0.refs_2_), channel_id=1, source_target_pairs={{0,4},{1,29},{2,6},{3,31},{4,0},{5,9},{6,2},{7,11},{8,12},{9,5},{1... | collective-permute-start | bytes 1179656 | tf_op jit(solution)/shard_map/ppermute | solution.py:51
  5.1 25.3 %collective-permute-start = (bf16[384,512]{1,0:T(8,128)(2,1)}, bf16[384,512]{1,0:T(8,128)(2,1)}, u32[]{:S(2)}, u32[]{:S(2)}) collective-permute-start(bf16[384,512]{1,0:T(8,128)(2,1)} %get-tuple-element.54), channel_id=1, source_target_pairs={{0,28},{1,5},{2,30},{3,7},{4,8},{5,1},{6,10},{7,3},{8,4},{9,13},{1... | collective-permute-start | bytes 1179656 | tf_op jit(solution)/shard_map/ppermute | solution.py:41
  10.0 30.8 %collective-permute-start.1 = (bf16[384,512]{1,0:T(8,128)(2,1)}, bf16[384,512]{1,0:T(8,128)(2,1)}, u32[]{:S(2)}, u32[]{:S(2)}) collective-permute-start(bf16[384,512]{1,0:T(8,128)(2,1)} %get-tuple-element.55), channel_id=1, source_target_pairs={{0,8},{1,25},{2,10},{3,27},{4,28},{5,13},{6,30},{7,15},{8,16},{9,1... | collective-permute-start | bytes 1179656 | tf_op jit(solution)/shard_map/ppermute | solution.py:41
  10.0 30.8 %collective-permute-start.2 = (bf16[384,512]{1,0:T(8,128)(2,1)}, bf16[384,512]{1,0:T(8,128)(2,1)}, u32[]{:S(2)}, u32[]{:S(2)}) collective-permute-start(bf16[384,512]{1,0:T(8,128)(2,1)} %get-tuple-element.56), channel_id=1, source_target_pairs={{0,20},{1,13},{2,22},{3,15},{4,16},{5,25},{6,18},{7,27},{8,28},{9,... | collective-permute-start | bytes 1179656 | tf_op jit(solution)/shard_map/ppermute | solution.py:41
  15.2 7.8 %copy-start.11 = (s32[129]{0:T(256)S(1)}, s32[129]{0:T(256)}, u32[]{:S(2)}) copy-start(s32[129]{0:T(256)} %param.21) | copy-start | bytes 1552
  15.3 9.3 %copy-start.8 = (bf16[1280,64]{0,1:T(8,128)(2,1)S(1)}, bf16[1280,64]{0,1:T(8,128)(2,1)}, u32[]{:S(2)}) copy-start(bf16[1280,64]{0,1:T(8,128)(2,1)} %param.17) | copy-start | bytes 491524
  15.3 4.0 %copy-start.4 = (bf16[384,512]{1,0:T(8,128)(2,1)}, bf16[384,512]{1,0:T(8,128)(2,1)S(1)}, u32[]{:S(2)}) copy-start(bf16[384,512]{1,0:T(8,128)(2,1)S(1)} %collective-permute-done.3.kv1.refs_3_) | copy-start | bytes 1179652
  19.3 41.1 %collective-permute-start.5 = (bf16[640,1280]{1,0:T(8,128)(2,1)}, bf16[640,1280]{1,0:T(8,128)(2,1)S(1)}, u32[]{:S(2)}, u32[]{:S(2)}) collective-permute-start(bf16[640,1280]{1,0:T(8,128)(2,1)} %get-tuple-element.108), channel_id=1, source_target_pairs={{0,2},{1,3},{2,0},{3,1},{4,6},{5,7},{6,4},{7,5},{8,10},{9,11},{10,... | collective-permute-start | bytes 4915208 | tf_op jit(solution)/shard_map/ppermute | solution.py:63
  20.9 40.1 %collective-permute-start.6 = (bf16[640,1280]{1,0:T(8,128)(2,1)}, bf16[640,1280]{1,0:T(8,128)(2,1)S(1)}, u32[]{:S(2)}, u32[]{:S(2)}) collective-permute-start(bf16[640,1280]{1,0:T(8,128)(2,1)} %get-tuple-element.107), channel_id=1, source_target_pairs={{0,34},{1,35},{2,32},{3,33},{4,38},{5,39},{6,36},{7,37},{8,42},{9,... | collective-permute-start | bytes 4915208 | tf_op jit(solution)/shard_map/ppermute | solution.py:59
  24.5 1.5 %copy-start = (bf16[3,256,1280]{2,1,0:T(8,128)(2,1)S(1)}, bf16[3,256,1280]{2,1,0:T(8,128)(2,1)}, u32[]{:S(2)}) copy-start(bf16[3,256,1280]{2,1,0:T(8,128)(2,1)} %time_ref.1) | copy-start | bytes 5898244
  28.1 14.3 %copy-start.2 = (bf16[384,256]{1,0:T(8,128)(2,1)S(1)}, bf16[384,256]{1,0:T(8,128)(2,1)}, u32[]{:S(2)}) copy-start(bf16[384,256]{1,0:T(8,128)(2,1)} %get-tuple-element.68.own_q_ref.refs_1_) | copy-start | bytes 589828
  28.1 14.3 %copy-start.3 = (bf16[384,512]{1,0:T(8,128)(2,1)S(1)}, bf16[384,512]{1,0:T(8,128)(2,1)}, u32[]{:S(2)}) copy-start(bf16[384,512]{1,0:T(8,128)(2,1)} %get-tuple-element.57.kv0.refs_2_) | copy-start | bytes 1179652
  28.1 14.3 %copy-start.5 = (bf16[384,512]{1,0:T(8,128)(2,1)S(1)}, bf16[384,512]{1,0:T(8,128)(2,1)}, u32[]{:S(2)}) copy-start(bf16[384,512]{1,0:T(8,128)(2,1)} %copy-done.4) | copy-start | bytes 1179652
  42.1 12.5 %collective-permute-start.4 = (bf16[1152,256]{1,0:T(8,128)(2,1)S(1)}, bf16[1152,256]{1,0:T(8,128)(2,1)S(1)}, u32[]{:S(2)}, u32[]{:S(2)}) collective-permute-start(bf16[1152,256]{1,0:T(8,128)(2,1)S(1)} %get-tuple-element.69.refs_4_), channel_id=1, source_target_pairs={{0,4},{1,29},{2,6},{3,31},{4,0},{5,9},{6,2},{7,11},{8,12},{9,5},{1... | collective-permute-start | bytes 1769480 | tf_op jit(solution)/shard_map/ppermute | solution.py:51
  49.4 17.9 %collective-permute-start.15 = (bf16[416,128]{1,0:T(8,128)(2,1)S(1)}, bf16[416,128]{1,0:T(8,128)(2,1)S(1)}, u32[]{:S(2)}, u32[]{:S(2)}) collective-permute-start(bf16[416,128]{1,0:T(8,128)(2,1)S(1)} %get-tuple-element.88), channel_id=1, source_target_pairs={{20,0},{13,1},{22,2},{15,3},{16,4},{25,5},{18,6},{27,7},{28,8},{21... | collective-permute-start | bytes 319496 | tf_op jit(solution)/shard_map/ppermute | solution.py:41
  52.9 14.4 %collective-permute-start.13 = (bf16[416,128]{1,0:T(8,128)(2,1)S(1)}, bf16[416,128]{1,0:T(8,128)(2,1)S(1)}, u32[]{:S(2)}, u32[]{:S(2)}) collective-permute-start(bf16[416,128]{1,0:T(8,128)(2,1)S(1)} %get-tuple-element.86), channel_id=1, source_target_pairs={{28,0},{5,1},{30,2},{7,3},{8,4},{1,5},{10,6},{3,7},{4,8},{13,9},{6... | collective-permute-start | bytes 319496 | tf_op jit(solution)/shard_map/ppermute | solution.py:41
  54.6 12.7 %collective-permute-start.14 = (bf16[416,128]{1,0:T(8,128)(2,1)S(1)}, bf16[416,128]{1,0:T(8,128)(2,1)S(1)}, u32[]{:S(2)}, u32[]{:S(2)}) collective-permute-start(bf16[416,128]{1,0:T(8,128)(2,1)S(1)} %get-tuple-element.87), channel_id=1, source_target_pairs={{8,0},{25,1},{10,2},{27,3},{28,4},{13,5},{30,6},{15,7},{16,8},{1,9... | collective-permute-start | bytes 319496 | tf_op jit(solution)/shard_map/ppermute | solution.py:41
  61.0 10.7 %collective-permute-start.11 = (bf16[384,128]{1,0:T(8,128)(2,1)S(1)}, bf16[384,128]{1,0:T(8,128)(2,1)S(1)}, u32[]{:S(2)}, u32[]{:S(2)}) collective-permute-start(bf16[384,128]{1,0:T(8,128)(2,1)S(1)} %get-tuple-element.84), channel_id=1, source_target_pairs={{8,0},{25,1},{10,2},{27,3},{28,4},{13,5},{30,6},{15,7},{16,8},{1,9... | collective-permute-start | bytes 294920 | tf_op jit(solution)/shard_map/ppermute | solution.py:41
  62.9 8.3 %collective-permute-start.9 = (bf16[384,128]{1,0:T(8,128)(2,1)S(1)}, bf16[384,128]{1,0:T(8,128)(2,1)S(1)}, u32[]{:S(2)}, u32[]{:S(2)}) collective-permute-start(bf16[384,128]{1,0:T(8,128)(2,1)S(1)} %get-tuple-element.83), channel_id=1, source_target_pairs={{20,0},{13,1},{22,2},{15,3},{16,4},{25,5},{18,6},{27,7},{28,8},{21... | collective-permute-start | bytes 294920 | tf_op jit(solution)/shard_map/ppermute | solution.py:41
  67.7 10.9 %collective-permute-start.16 = (bf16[384,256]{1,0:T(8,128)(2,1)S(1)}, bf16[384,256]{1,0:T(8,128)(2,1)S(1)}, u32[]{:S(2)}, u32[]{:S(2)}) collective-permute-start(bf16[384,256]{1,0:T(8,128)(2,1)S(1)} %shard_map.136.refs_1_), channel_id=1, source_target_pairs={{0,2},{1,3},{2,0},{3,1},{4,6},{5,7},{6,4},{7,5},{8,10},{9,11},{10,... | collective-permute-start | bytes 589832 | tf_op jit(solution)/shard_map/ppermute | solution.py:63
  67.8 5.9 %collective-permute-start.7 = (bf16[384,128]{1,0:T(8,128)(2,1)S(1)}, bf16[384,128]{1,0:T(8,128)(2,1)S(1)}, u32[]{:S(2)}, u32[]{:S(2)}) collective-permute-start(bf16[384,128]{1,0:T(8,128)(2,1)S(1)} %get-tuple-element.82), channel_id=1, source_target_pairs={{28,0},{5,1},{30,2},{7,3},{8,4},{1,5},{10,6},{3,7},{4,8},{13,9},{6... | collective-permute-start | bytes 294920 | tf_op jit(solution)/shard_map/ppermute | solution.py:41
  71.2 7.5 %collective-permute-start.10 = (bf16[384,128]{1,0:T(8,128)(2,1)S(1)}, bf16[384,128]{1,0:T(8,128)(2,1)S(1)}, u32[]{:S(2)}, u32[]{:S(2)}) collective-permute-start(bf16[384,128]{1,0:T(8,128)(2,1)S(1)} %collective-permute-done.9.refs_4_), channel_id=1, source_target_pairs={{0,2},{1,3},{2,0},{3,1},{4,6},{5,7},{6,4},{7,5},{8,10},{9,11},{10,... | collective-permute-start | bytes 294920 | tf_op jit(solution)/shard_map/ppermute | solution.py:63
  71.7 7.0 %collective-permute-start.12 = (bf16[384,128]{1,0:T(8,128)(2,1)S(1)}, bf16[384,128]{1,0:T(8,128)(2,1)S(1)}, u32[]{:S(2)}, u32[]{:S(2)}) collective-permute-start(bf16[384,128]{1,0:T(8,128)(2,1)S(1)} %collective-permute-done.11.refs_5_), channel_id=1, source_target_pairs={{0,2},{1,3},{2,0},{3,1},{4,6},{5,7},{6,4},{7,5},{8,10},{9,11},{10,... | collective-permute-start | bytes 294920 | tf_op jit(solution)/shard_map/ppermute | solution.py:63
  73.8 5.8 %collective-permute-start.8 = (bf16[384,128]{1,0:T(8,128)(2,1)S(1)}, bf16[384,128]{1,0:T(8,128)(2,1)S(1)}, u32[]{:S(2)}, u32[]{:S(2)}) collective-permute-start(bf16[384,128]{1,0:T(8,128)(2,1)S(1)} %collective-permute-done.7.refs_3_), channel_id=1, source_target_pairs={{0,2},{1,3},{2,0},{3,1},{4,6},{5,7},{6,4},{7,5},{8,10},{9,11},{10,... | collective-permute-start | bytes 294920 | tf_op jit(solution)/shard_map/ppermute | solution.py:63
  81.0 2.7 %copy-start.1 = (bf16[384,1280]{1,0:T(8,128)(2,1)S(1)}, bf16[384,1280]{1,0:T(8,128)(2,1)}, u32[]{:S(2)}) copy-start(bf16[384,1280]{1,0:T(8,128)(2,1)} %in_ref.1) | copy-start | bytes 2949124
  81.1 2.7 %copy-start.7 = (bf16[128,1280]{1,0:T(8,128)(2,1)S(1)}, bf16[128,1280]{1,0:T(8,128)(2,1)}, u32[]{:S(2)}) copy-start(bf16[128,1280]{1,0:T(8,128)(2,1)} %copy-done.6) | copy-start | bytes 983044
  81.1 2.7 %collective-permute-start.17 = (bf16[384,1280]{1,0:T(8,128)(2,1)S(1)}, bf16[384,1280]{1,0:T(8,128)(2,1)S(1)}, u32[]{:S(2)}, u32[]{:S(2)}) collective-permute-start(bf16[384,1280]{1,0:T(8,128)(2,1)S(1)} %shard_map.140), channel_id=1, source_target_pairs={{0,1},{1,0},{2,3},{3,2},{4,5},{5,4},{6,7},{7,6},{8,9},{9,8},{10,11... | collective-permute-start | bytes 2949128 | tf_op jit(solution)/shard_map/ppermute | solution.py:63
  82.7 8.6 %copy-start.9 = (f32[384,64]{0,1:T(8,128)S(1)}, f32[384,64]{0,1:T(8,128)}, u32[]{:S(2)}) copy-start(f32[384,64]{0,1:T(8,128)} %param.18) | copy-start | bytes 294916
  82.7 15.4 %copy-start.10 = (f32[384,64]{0,1:T(8,128)S(1)}, f32[384,64]{0,1:T(8,128)}, u32[]{:S(2)}) copy-start(f32[384,64]{0,1:T(8,128)} %param.19) | copy-start | bytes 294916
  85.2 1.4 %collective-permute-start.18 = (f32[72,512]{1,0:T(8,128)S(1)}, f32[72,512]{1,0:T(8,128)S(1)}, u32[]{:S(2)}, u32[]{:S(2)}) collective-permute-start(f32[72,512]{1,0:T(8,128)S(1)} %get-tuple-element.101.a_ref), channel_id=1, source_target_pairs={{0,1},{1,0},{2,3},{3,2},{4,5},{5,4},{6,7},{7,6},{8,9},{9,8},{10,11... | collective-permute-start | bytes 442376 | tf_op jit(solution)/shard_map/ppermute | solution.py:63
  86.7 4.6 %collective-permute-start.19 = (bf16[80,512]{1,0:T(8,128)(2,1)S(1)}, bf16[80,512]{1,0:T(8,128)(2,1)S(1)}, u32[]{:S(2)}, u32[]{:S(2)}) collective-permute-start(bf16[80,512]{1,0:T(8,128)(2,1)S(1)} %shard_map.142.p0), channel_id=1, source_target_pairs={{0,2},{1,3},{2,0},{3,1},{4,6},{5,7},{6,4},{7,5},{8,10},{9,11},{10,... | collective-permute-start | bytes 245768 | tf_op jit(solution)/shard_map/ppermute | solution.py:63
  92.1 6.0 %collective-permute-start.20 = (bf16[64,384]{1,0:T(8,128)(2,1)S(1)}, bf16[64,384]{1,0:T(8,128)(2,1)S(1)}, u32[]{:S(2)}, u32[]{:S(2)}) collective-permute-start(bf16[64,384]{1,0:T(8,128)(2,1)S(1)} %get-tuple-element.104), channel_id=1, source_target_pairs={{4,0},{8,4},{12,8},{16,12},{20,16},{24,20},{28,24},{32,28},{36,32}... | collective-permute-start | bytes 147464 | tf_op jit(solution)/shard_map/ppermute | solution.py:69
  (1 other events, 0.7 us)
